TPU v7x, 512 devices: a whole 4x8x8 slice. The times are simulated.
512 devices in a mesh: head: 4 (over x), pb: 8 (over z), kv: 16 (over y, core).
Axes of the slice: x: 4, y: 8, z: 8, core: 2. Of those that a mesh axis runs over, the one named last changes fastest.
Arguments:
- queries: bfloat16 [16384, 4096], P(('pb', 'kv'), 'head'), may hold values from -32 to 32
- keys: bfloat16 [16384, 1024], P(('pb', 'kv'), 'head'), may hold values from -32 to 32
- values: bfloat16 [16384, 1024], P(('pb', 'kv'), 'head'), may hold values from -6 to 6
- doc_lengths: int32 [17], replicated, may hold values from 1 to 1920, 16384 in all
- page_table: int32 [1024], replicated, may hold values from 0 to 1023, as said below
Outputs:
- attended: bfloat16 [16384, 4096], P(('pb', 'kv'), 'head')
- page_pool: bfloat16 [1024, 2, 16, 1024], P(('head', 'pb', 'kv'))
Inputs may be any that keep to these rules, and one draw needn't show every extreme that they name: `page_table`: each page number appears once. Slot s holds one of the pages b * 128 to (b + 1) * 128 - 1, where b = (s % 256) // 32.
All inputs are finite; a program needn't handle non-finite values.
Results may differ from a plain program's by a relative error of at most 0.0039.
Values may be sent and summed in bfloat16 or wider, within the bound.
No kernel may reach another device: no remote copies, remote signals or barrier semaphores. Data moves between devices by JAX's collectives and lax.ppermute only.
A program may use at most 64 MiB of HBM per device.

v0:
```python
import jax
import jax.numpy as jnp
from jax import lax
from jax.sharding import PartitionSpec as P

HD = 128
PAGE = 16


def passed_along(block, axis, distance):
    devices = range(lax.axis_size(axis))
    route = [(i - distance, i) for i in devices if i - distance in devices]
    return lax.ppermute(block, axis, route)


def document_ids(positions, bounds):
    return jnp.sum((positions[:, None] >= bounds[None, :]).astype(jnp.int32), axis=1)


def attend(state, qgrid, qpos, qdoc, key_rows, value_rows, kpos, kdoc):
    visible = (
        (kdoc[None, :] == qdoc[:, None]) & (kpos[None, :] <= qpos[:, None]) & (kpos[None, :] >= 0)
    )

    def update(carry):
        top, total, acc = carry
        groups = qgrid.shape[1]
        head_dim = qgrid.shape[3]
        kblk = key_rows.reshape(key_rows.shape[0], groups, head_dim)
        vblk = value_rows.reshape(value_rows.shape[0], groups, head_dim)
        mask = visible[:, None, None, :]
        scores = jnp.einsum(
            "rghd,ngd->rghn", qgrid, kblk, preferred_element_type=jnp.float32
        ) * head_dim ** (-0.5)
        scores = jnp.where(mask, scores, -1e30)
        new_top = jnp.maximum(top, jnp.max(scores, axis=-1))
        weights = jnp.where(mask, jnp.exp(scores - new_top[..., None]), 0.0)
        factor = jnp.exp(top - new_top)
        total = total * factor + jnp.sum(weights, axis=-1)
        acc = acc * factor[..., None] + jnp.einsum(
            "rghn,ngd->rghd", weights.astype(jnp.bfloat16), vblk, preferred_element_type=jnp.float32
        )
        return (new_top, total, acc)

    return lax.cond(jnp.any(visible), update, lambda carry: carry, state)


def copy_pages(pool, key_rows, value_rows, offsets):
    count = key_rows.shape[0]
    inside = (offsets >= 0) & (offsets < count)
    picks = jnp.clip(offsets, 0, count - PAGE)[:, None] + jnp.arange(PAGE, dtype=jnp.int32)[None, :]
    fresh = jnp.stack([key_rows[picks], value_rows[picks]], axis=1)
    return jnp.where(inside[:, None, None, None], fresh, pool)


def body(queries, keys, values, doc_lengths, page_table):
    rows = queries.shape[0]
    n_head = lax.axis_size("head")
    n_pb = lax.axis_size("pb")
    n_kv = lax.axis_size("kv")
    groups = keys.shape[1] // HD
    heads = queries.shape[1] // (groups * HD)
    slice_rows = rows * n_kv
    tokens_all = slice_rows * n_pb
    pb_index = lax.axis_index("pb")
    kv_index = lax.axis_index("kv")
    linear = pb_index * n_kv + kv_index
    bounds = jnp.cumsum(doc_lengths)
    offsets_row = jnp.arange(rows, dtype=jnp.int32)
    qpos = linear * rows + offsets_row
    qdoc = document_ids(qpos, bounds)
    qgrid = queries.reshape(rows, groups, heads, HD)
    init = (
        jnp.full((rows, groups, heads), -1e30, jnp.float32),
        jnp.zeros((rows, groups, heads), jnp.float32),
        jnp.zeros((rows, groups, heads, HD), jnp.float32),
    )
    slots_dev = rows // PAGE // n_head
    slot_ids = (
        jnp.arange(n_head, dtype=jnp.int32)[:, None] * (tokens_all // PAGE // n_head)
        + pb_index * (slice_rows // PAGE // n_head)
        + kv_index * slots_dev
        + jnp.arange(slots_dev, dtype=jnp.int32)[None, :]
    ).reshape(-1)
    offsets = (jnp.take(page_table, slot_ids) - pb_index * (slice_rows // PAGE)) * PAGE
    blank_pool = jnp.zeros((n_head * slots_dev, 2, PAGE, groups * HD), jnp.bfloat16)
    slice_start = pb_index * slice_rows
    prev_k, prev_v = passed_along((keys, values), "pb", 1)
    state = init
    own_keys = lax.all_gather(keys, "kv", axis=0, tiled=True)
    own_values = lax.all_gather(values, "kv", axis=0, tiled=True)
    old_keys = lax.all_gather(prev_k, "kv", axis=0, tiled=True)
    old_values = lax.all_gather(prev_v, "kv", axis=0, tiled=True)
    count = own_keys.shape[0]
    steps = jnp.arange(count, dtype=jnp.int32)
    own_pos = slice_start + steps
    old_pos = slice_start - slice_rows + steps
    state = attend(
        state, qgrid, qpos, qdoc, own_keys, own_values, own_pos, document_ids(own_pos, bounds)
    )
    state = attend(
        state, qgrid, qpos, qdoc, old_keys, old_values, old_pos, document_ids(old_pos, bounds)
    )
    pool_pre = copy_pages(
        blank_pool,
        lax.all_gather(keys, "kv", axis=0, tiled=True),
        lax.all_gather(values, "kv", axis=0, tiled=True),
        offsets,
    )
    top, total, acc = state
    attended = (acc / total[..., None]).astype(jnp.bfloat16).reshape(rows, groups * heads * HD)
    page_pool = lax.all_to_all(pool_pre, "head", split_axis=0, concat_axis=3, tiled=True)
    return (attended, page_pool)


def solution(mesh):
    in_specs = (P(("pb", "kv"), "head"), P(("pb", "kv"), "head"), P(("pb", "kv"), "head"), P(), P())
    out_specs = (P(("pb", "kv"), "head"), P(("head", "pb", "kv"), None, None, None))
    return jax.shard_map(body, mesh=mesh, in_specs=in_specs, out_specs=out_specs, check_vma=False)
```

profile of v0, /device:TPU:67, one launch (start us, length us, event | category | flops | bytes accessed | tf_op | source)
XLA Modules:
  0.0 204.5 jit_solution(3787392383258539924)
XLA Ops:
  7.2 0.7 all-gather.7.cloned.1.call-update
  8.0 0.7 all-gather.5.cloned.1.call-update
  8.7 4.0 %collective-permute-start = (bf16[128,256]{1,0:T(8,128)(2,1)}, bf16[128,256]{1,0:T(8,128)(2,1)S(1)}, u32[]{:S(2)}, u32[]{:S(2)}) collective-permute-start(bf16[128,256]{1,0:T(8,128)(2,1)} %param.10), channel_id=1, source_target_pairs={{0,16},{16,32},{32,48},{48,64},{64,80},{80,96},{96,112},{1,17},{17... | collective-permute-start | bytes 196616 | tf_op jit(solution)/shard_map/ppermute | solution.py:13
  12.7 1.6 collective-permute-done
  14.3 0.6 copy-done.5
  15.0 4.0 %collective-permute-start.1 = (bf16[128,256]{1,0:T(8,128)(2,1)}, bf16[128,256]{1,0:T(8,128)(2,1)S(1)}, u32[]{:S(2)}, u32[]{:S(2)}) collective-permute-start(bf16[128,256]{1,0:T(8,128)(2,1)} %param.11), channel_id=1, source_target_pairs={{0,16},{16,32},{32,48},{48,64},{64,80},{80,96},{96,112},{1,17},{17... | collective-permute-start | bytes 196616 | tf_op jit(solution)/shard_map/ppermute | solution.py:13
  19.2 1.5 collective-permute-done.1
  20.7 0.6 copy-done.6
  21.3 0.1 add.187
  21.4 0.1 add.185
  21.5 0.7 copy.48
  22.3 0.1 reduce
  22.4 0.1 convert_reduce_fusion.2
  22.5 0.1 convert_reduce_fusion
  22.6 2.7 %fusion.38 = (pred[]{:T(512)}, pred[128,2048]{0,1:T(8,128)(4,1)S(1)}, pred[]{:T(512)}, pred[128,2048]{0,1:T(8,128)(4,1)S(1)}) fusion(pred[2048]{0:T(1024)(128)(4,1)S(1)} %get-tuple-element.102, s32[128]{0:T(128)S(1)} %iota_add_fusion.3, s32[2048]{0:T(1024)S(1)} %get-tuple-element.100, s32[128]{0:T(128)S(1)} %convert_reduce_fusion.2, ...), kind=kLoop, calls=%fused_computation.62 | loop fusion | flops 2621438 | bytes 562178 | tf_op jit(solution)/shard_map/reduce_or | solution.py:45
  26.5 1.1 copy.49
  27.7 0.6 gather_fusion
  28.4 0.1 reshape.228
  28.5 26.9 %all-gather.7.cloned.1.call-done = bf16[2048,256]{1,0:T(8,128)(2,1)} async-done(((bf16[128,256]{1,0:T(8,128)(2,1)}), bf16[2048,256]{1,0:T(8,128)(2,1)}) %all-gather.7.cloned.1.call-update) | async-done | bytes 1048592 | tf_op jit(solution)/shard_map/all_gather | solution.py:91
  55.4 2.1 %gather_fusion.2 = bf16[128,256]{1,0:T(8,128)(2,1)S(1)} fusion(bf16[2048,256]{1,0:T(8,128)(2,1)} %all-gather.7.cloned.1.call-done, s32[1024]{0:T(1024)S(1)} %pad_clamp_fusion), kind=kCustom, calls=%fused_computation.2 | custom fusion | bytes 131584 | tf_op jit(solution)/shard_map/gather | solution.py:52
  57.6 39.8 %all-gather.5.cloned.1.call-done = bf16[2048,256]{1,0:T(8,128)(2,1)} async-done(((bf16[128,256]{1,0:T(8,128)(2,1)}), bf16[2048,256]{1,0:T(8,128)(2,1)}) %all-gather.5.cloned.1.call-update) | async-done | bytes 1048592 | tf_op jit(solution)/shard_map/all_gather | solution.py:90
  97.4 2.1 %gather_fusion.1 = bf16[128,256]{1,0:T(8,128)(2,1)S(1)} fusion(bf16[2048,256]{1,0:T(8,128)(2,1)} %all-gather.5.cloned.1.call-done, s32[1024]{0:T(1024)S(1)} %pad_clamp_fusion), kind=kCustom, calls=%fused_computation.1 | custom fusion | bytes 131584 | tf_op jit(solution)/shard_map/gather | solution.py:52
  99.5 0.7 maximum_select_fusion
  100.2 4.2 %all-to-all-start = ((bf16[8,2,16,256]{3,2,1,0:T(8,128)(2,1)}), bf16[8,2,16,256]{3,2,1,0:T(8,128)(2,1)S(1)}, u32[]{:S(2)}, u32[]{:S(2)}) async-start(bf16[8,2,16,256]{3,2,1,0:T(8,128)(2,1)} %maximum_select_fusion), calls=%async_computation | async-start | bytes 262144 | tf_op jit(solution)/shard_map/all_to_all | solution.py:112
  104.5 14.9 %conditional.2 = (f32[128,2,4]{0,2,1:T(4,128)}, f32[128,2,4]{0,2,1:T(4,128)S(1)}, f32[128,2,4,128]{3,0,2,1:T(8,128)S(1)}) conditional(s32[]{:T(128)} %convert_element_type.28, () %tuple.23, (pred[128,2048]{0,1:T(8,128)(4,1)S(1)}, bf16[2048,256]{1,0:T(8,128)(2,1)}, bf16[128,2,4,128]{0,3,2,1:T(8,128)(2,1)S(1)}, bf16[2048,256]{1,0:T(8,128)(2,1)}) %tuple.61), branch_computations={%region_6.7_spmd, %region_7.10_spmd} | conditional | flops 1101139968 | bytes 70824016 | solution.py:45
  104.5 1.3 reshape.206
  105.8 1.3 fusion
  107.2 0.6 exponential_multiply_fusion
  107.8 2.6 %copy-done.2 = f32[2,2048,128,4]{2,1,3,0:T(8,128)} copy-done((f32[2,2048,128,4]{2,1,3,0:T(8,128)}, f32[2,2048,128,4]{2,1,3,0:T(8,128)S(1)}, u32[]{:S(2)}) %copy-start.2) | copy-done | bytes 8388632 | tf_op jit(solution)/shard_map/cond
  110.4 2.7 %fusion.2 = f32[128,2,4]{0,2,1:T(4,128)S(1)} fusion(f32[2,2048,128,4]{2,1,3,0:T(8,128)S(1)} %get-tuple-element.95, f32[128,2,4]{0,2,1:T(4,128)} %get-tuple-element.109, pred[128,2048]{0,1:T(8,128)(4,1)S(1)} %get-tuple-element.26), kind=kLoop, calls=%fused_computation.7 | loop fusion | flops 10484736 | bytes 8658944 | tf_op jit(solution)/shard_map/cond/branch_1_fun/reduce_sum | solution.py:39
  113.1 0.7 fusion.18
  113.8 0.3 reshape.207
  114.1 5.3 %fusion.9 = f32[128,2,4,128]{3,0,2,1:T(8,128)S(1)} fusion(f32[2,2048,128,4]{2,1,3,0:T(8,128)} %copy-done.2, f32[128,2,4]{0,2,1:T(4,128)} %get-tuple-element.109, pred[128,2048]{0,1:T(8,128)(4,1)S(1)} %get-tuple-element.26, bf16[2048,2,128,1]{2,1,0,3:T(2,128)(2,1)S(1)} %bitcast.68, f32[128,2,4]{0,2,1:T(4,128)S(1)} %get-tuple-element.84), kind=kOutput, calls=%fused_computation.11 | convolution fusion | flops 547487744 | bytes 10231808 | tf_op jit(solution)/shard_map/cond/branch_1_fun/rghn,ngd->rghd/dot_general | solution.py:40
  119.3 20.6 %all-gather.9.cloned.1.call-done = bf16[2048,256]{1,0:T(8,128)(2,1)} async-done(((bf16[128,256]{1,0:T(8,128)(2,1)}), bf16[2048,256]{1,0:T(8,128)(2,1)}) %all-gather.9.cloned.1.call-update) | async-done | bytes 1048592 | tf_op jit(solution)/shard_map/all_gather | solution.py:92
  140.0 41.9 %all-gather.11.cloned.1.call-done = bf16[2048,256]{1,0:T(8,128)(2,1)} async-done(((bf16[128,256]{1,0:T(8,128)(2,1)}), bf16[2048,256]{1,0:T(8,128)(2,1)}) %all-gather.11.cloned.1.call-update) | async-done | bytes 1048592 | tf_op jit(solution)/shard_map/all_gather | solution.py:93
  181.9 14.1 %conditional.3 = ((f32[128,2,4]{0,2,1:T(4,128)S(1)}, f32[128,2,4,128]{3,0,2,1:T(8,128)S(1)})) conditional(s32[]{:T(128)} %convert_element_type.26, (f32[128,2,4]{0,2,1:T(4,128)S(1)}, f32[128,2,4,128]{3,0,2,1:T(8,128)S(1)}) %tuple.25, (pred[128,2048]{0,1:T(8,128)(4,1)S(1)}, bf16[2048,256]{1,0:T(8,128)(2,1)}, ...), branch_computations={%region_10.11_spmd, %region_11.14_spmd} | conditional | flops 1101268992 | bytes 71360592 | solution.py:45
  181.9 1.3 reshape.208
  183.2 1.3 fusion.19
  184.6 0.7 max.6
  185.2 2.5 %copy-done.1 = f32[2,2048,128,4]{2,1,3,0:T(8,128)} copy-done((f32[2,2048,128,4]{2,1,3,0:T(8,128)}, f32[2,2048,128,4]{2,1,3,0:T(8,128)S(1)}, u32[]{:S(2)}) %copy-start.1) | copy-done | bytes 8388632 | tf_op jit(solution)/shard_map/cond
  187.8 2.0 fusion.21
  189.8 0.7 multiply_add_fusion
  190.5 0.3 reshape.209
  190.8 5.2 %fusion.28 = f32[128,2,4,128]{3,0,2,1:T(8,128)S(1)} fusion(f32[2,2048,128,4]{2,1,3,0:T(8,128)} %copy-done.1, f32[128,2,4]{0,2,1:T(4,128)S(1)} %max.6, pred[128,2048]{0,1:T(8,128)(4,1)S(1)} %get-tuple-element.32, bf16[2048,2,128,1]{2,1,0,3:T(2,128)(2,1)S(1)} %bitcast.67, f32[128,2,4,128]{3,0,2,1:T(8,128)S(1)} %get-tuple-element.35, f32[128,2,4]{0,2,1:T(4,128)S(1)} %bitcast.81), kind=kOutput, calls=%fused_computation.29 | convolution fusion | flops 547618816 | bytes 10756096 | tf_op jit(solution)/shard_map/cond/branch_1_fun/rghn,ngd->rghd/dot_general | solution.py:40
  196.0 0.2 divide_convert_fusion
  196.2 0.2 copy.52
  196.4 0.9 reshape.217
  197.3 0.7 copy.72
  (29 shorter events, 0.5 us)
Async XLA Ops:
  7.2 20.5 %copy-start = (s32[1024]{0:T(1024)S(1)}, s32[1024]{0:T(1024)}, u32[]{:S(2)}) copy-start(s32[1024]{0:T(1024)} %param.13) | copy-start | bytes 12292
  7.2 48.3 %all-gather.7.cloned.1.call-start = ((), (), s32[]{:S(2)}) async-start(), calls=%async_computation.2 | async-start | bytes 1114112 | tf_op jit(solution)/shard_map/all_gather | solution.py:91
  7.9 89.5 %all-gather.5.cloned.1.call-start = ((), (), s32[]{:S(2)}) async-start(), calls=%async_computation.1 | async-start | bytes 1114112 | tf_op jit(solution)/shard_map/all_gather | solution.py:90
  8.7 131.3 %all-gather.9.cloned.1.call-start = ((), (), s32[]{:S(2)}) async-start(), calls=%async_computation.3 | async-start | bytes 1114112 | tf_op jit(solution)/shard_map/all_gather | solution.py:92
  8.7 5.6 %collective-permute-start = (bf16[128,256]{1,0:T(8,128)(2,1)}, bf16[128,256]{1,0:T(8,128)(2,1)S(1)}, u32[]{:S(2)}, u32[]{:S(2)}) collective-permute-start(bf16[128,256]{1,0:T(8,128)(2,1)} %param.10), channel_id=1, source_target_pairs={{0,16},{16,32},{32,48},{48,64},{64,80},{80,96},{96,112},{1,17},{17... | collective-permute-start | bytes 196616 | tf_op jit(solution)/shard_map/ppermute | solution.py:13
  14.3 0.6 copy-start.5
  15.0 166.9 %all-gather.11.cloned.1.call-start = ((), (), s32[]{:S(2)}) async-start(), calls=%async_computation.4 | async-start | bytes 1114112 | tf_op jit(solution)/shard_map/all_gather | solution.py:93
  15.0 5.6 %collective-permute-start.1 = (bf16[128,256]{1,0:T(8,128)(2,1)}, bf16[128,256]{1,0:T(8,128)(2,1)S(1)}, u32[]{:S(2)}, u32[]{:S(2)}) collective-permute-start(bf16[128,256]{1,0:T(8,128)(2,1)} %param.11), channel_id=1, source_target_pairs={{0,16},{16,32},{32,48},{48,64},{64,80},{80,96},{96,112},{1,17},{17... | collective-permute-start | bytes 196616 | tf_op jit(solution)/shard_map/ppermute | solution.py:13
  20.7 0.6 copy-start.6
  100.2 97.1 %all-to-all-start = ((bf16[8,2,16,256]{3,2,1,0:T(8,128)(2,1)}), bf16[8,2,16,256]{3,2,1,0:T(8,128)(2,1)S(1)}, u32[]{:S(2)}, u32[]{:S(2)}) async-start(bf16[8,2,16,256]{3,2,1,0:T(8,128)(2,1)} %maximum_select_fusion), calls=%async_computation | async-start | bytes 262144 | tf_op jit(solution)/shard_map/all_to_all | solution.py:112
  105.8 7.9 %copy-start.3 = (bf16[2048,256]{1,0:T(8,128)(2,1)S(1)}, bf16[2048,256]{1,0:T(8,128)(2,1)}, u32[]{:S(2)}) copy-start(bf16[2048,256]{1,0:T(8,128)(2,1)} %get-tuple-element.29) | copy-start | bytes 3145732 | tf_op jit(solution)/shard_map/cond
  107.2 3.2 %copy-start.2 = (f32[2,2048,128,4]{2,1,3,0:T(8,128)}, f32[2,2048,128,4]{2,1,3,0:T(8,128)S(1)}, u32[]{:S(2)}) copy-start(f32[2,2048,128,4]{2,1,3,0:T(8,128)S(1)} %get-tuple-element.95) | copy-start | bytes 25165828 | tf_op jit(solution)/shard_map/cond
  183.2 7.3 %copy-start.4 = (bf16[2048,256]{1,0:T(8,128)(2,1)S(1)}, bf16[2048,256]{1,0:T(8,128)(2,1)}, u32[]{:S(2)}) copy-start(bf16[2048,256]{1,0:T(8,128)(2,1)} %get-tuple-element.36) | copy-start | bytes 3145732 | tf_op jit(solution)/shard_map/cond
  184.6 3.2 %copy-start.1 = (f32[2,2048,128,4]{2,1,3,0:T(8,128)}, f32[2,2048,128,4]{2,1,3,0:T(8,128)S(1)}, u32[]{:S(2)}) copy-start(f32[2,2048,128,4]{2,1,3,0:T(8,128)S(1)} %get-tuple-element.97) | copy-start | bytes 25165828 | tf_op jit(solution)/shard_map/cond
Sparse Core Ops, SparseCore 0:
  10.1 45.2 all-gather.6
  57.6 39.7 all-gather.4
  100.1 39.8 all-gather.8
  142.0 39.8 all-gather.10
where the time goes:
time: 205 us
  waiting for transfers between devices  134 us (65%)
  local copies, waits for them, and re-layouts  18.3 us (9%)
  between operations  15.1 us (7%)
  matrix products  13.2 us (6%)
  starting transfers between devices  12.4 us (6%)
  other arithmetic  11.6 us (6%)
    all_gather x1, waiting for transfers between devices, body(): old_values = lax.all_gather(prev_v, 'kv', axis=0, tiled=True)  41.9 us
    all_gather x1, waiting for transfers between devices, body(): own_keys = lax.all_gather(keys, 'kv', axis=0, tiled=True)  39.8 us
    all_gather x1, waiting for transfers between devices, body(): own_values = lax.all_gather(values, 'kv', axis=0, tiled=True)  26.9 us
    all_gather x1, waiting for transfers between devices, body(): old_keys = lax.all_gather(prev_k, 'kv', axis=0, tiled=True)  20.6 us
    dot_general x2, matrix products, update(): jnp.einsum('rghn,ngd->rghd', weights.astype(jnp.bfloat16), vblk, preferre...  10.5 us
    ppermute x2, starting transfers between devices, passed_along(): return lax.ppermute(block, axis, route)  8 us
    cond x8, local copies, waits for them, and re-layouts  5.11 us
    reduce_sum x2, other arithmetic, update(): total = total * factor + jnp.sum(weights, axis=-1)  4.71 us
  transfers between devices with their start and end apart: 7, of which 6 were waited for; matrix products, arithmetic and copies ran while one was open for 18% of the time, Pallas kernels for 0%

commit v1 on v0

v1 whole, which is shorter than its diff:
```python
import functools
import math

import jax
import jax.numpy as jnp
from jax import lax
from jax.experimental import pallas as pl
from jax.experimental.pallas import tpu as pltpu
from jax.sharding import PartitionSpec as P

HD = 128
PAGE = 16
LOWEST = -1e30
STAT_ROWS = 16


def doc_start(lengths_ref, position):
    bound = jnp.int32(0)
    start = jnp.zeros_like(position)
    for i in range(lengths_ref.shape[0]):
        bound = bound + lengths_ref[i]
        start = jnp.where(bound <= position, bound, start)
    return start


def scan_keys(lengths_ref, q_ref, mine_ref, other_ref, q_base, k_base, core, acc, top, total):
    rows = q_ref.shape[0]
    half = mine_ref.shape[2]
    width = half // 2
    groups = width // HD
    heads = q_ref.shape[1] // width
    lanes = heads * rows
    factor = HD**-0.5 * math.log2(math.e)
    acc[...] = jnp.zeros_like(acc)
    top[...] = jnp.full_like(top, LOWEST)
    total[...] = jnp.zeros_like(total)
    first_start = doc_start(lengths_ref, q_base)
    last_start = doc_start(lengths_ref, q_base + rows - 1)
    q_pos = q_base + lax.broadcasted_iota(jnp.int32, (1, rows), 1)
    q_start = doc_start(lengths_ref, q_pos)

    def step(chip, masked):
        base = k_base + chip * 2 * rows
        if masked:
            row = lax.broadcasted_iota(jnp.int32, (2 * rows, rows), 0)
            k_pos = base + jnp.where(row < rows, row + core * rows, row - core * rows)
            seen = (k_pos <= q_pos) & (k_pos >= q_start)
            seen = jnp.concatenate([seen] * heads, axis=1)
        for g in range(groups):
            at = pl.ds(g * lanes, lanes)
            queries = jnp.concatenate(
                [q_ref[:, (g * heads + h) * HD : (g * heads + h + 1) * HD] for h in range(heads)], axis=0
            )
            k_cols = slice(g * HD, (g + 1) * HD)
            v_cols = slice(width + g * HD, width + (g + 1) * HD)
            keys = jnp.concatenate([mine_ref[chip, :, k_cols], other_ref[chip, :, k_cols]], axis=0)
            values = jnp.concatenate([mine_ref[chip, :, v_cols], other_ref[chip, :, v_cols]], axis=0)
            scores = lax.dot_general(keys, queries, (((1,), (1,)), ((), ())), preferred_element_type=jnp.float32)
            scores = scores * factor
            if masked:
                scores = jnp.where(seen, scores, LOWEST)
            old = top[:, at]
            new = jnp.maximum(old, jnp.max(scores, axis=0, keepdims=True))
            weights = jnp.exp2(scores - new)
            if masked:
                weights = jnp.where(seen, weights, 0.0)
            scale = jnp.exp2(old - new)
            top[:, at] = new
            total[:, at] = total[:, at] * scale + jnp.sum(weights, axis=0, keepdims=True)
            mixed = lax.dot_general(
                values, weights.astype(jnp.bfloat16), (((0,), (0,)), ((), ())), preferred_element_type=jnp.float32
            )
            acc[:, at] = acc[:, at] * scale + mixed

    def one(chip, carry):
        low = k_base + chip * 2 * rows
        high = low + 2 * rows - 1
        some = (low <= q_base + rows - 1) & (high >= first_start)
        whole = (high <= q_base) & (low >= last_start)

        @pl.when(whole)
        def _():
            step(chip, False)

        @pl.when(some & jnp.logical_not(whole))
        def _():
            step(chip, True)

        return carry

    lax.fori_loop(0, mine_ref.shape[0], one, 0)


def split_three(value):
    high = value.astype(jnp.bfloat16)
    rest = value - high.astype(jnp.float32)
    middle = rest.astype(jnp.bfloat16)
    low = (rest - middle.astype(jnp.float32)).astype(jnp.bfloat16)
    return [high, middle, low]


def later_kernel(at_ref, lengths_ref, table_ref, q_ref, mine_ref, other_ref, part_ref, pages_ref, acc, top, total):
    pb, kv, n_pb, n_kv, n_head = at_ref[0], at_ref[1], at_ref[2], at_ref[3], at_ref[4]
    core = lax.rem(kv, 2)
    rows = q_ref.shape[0]
    row_tokens = n_kv * rows
    n_slots = pages_ref.shape[0]
    width = pages_ref.shape[3]
    row_pages = row_tokens // PAGE
    slot_rows = row_pages // n_head
    per = n_slots // 4
    for i in range(n_slots):
        slot = (i // per) * (n_pb * slot_rows) + pb * slot_rows + kv * per + i % per
        page = table_ref[slot] - pb * row_pages
        block_pages = rows // PAGE
        block = lax.div(page, block_pages)
        chip = lax.div(block, 2)
        row = pl.multiple_of(lax.rem(page, block_pages) * PAGE, PAGE)
        own = lax.rem(block, 2) == core

        @pl.when(own)
        def _():
            pages_ref[i, 0] = mine_ref[chip, pl.ds(row, PAGE), 0:width]
            pages_ref[i, 1] = mine_ref[chip, pl.ds(row, PAGE), width : 2 * width]

        @pl.when(jnp.logical_not(own))
        def _():
            pages_ref[i, 0] = other_ref[chip, pl.ds(row, PAGE), 0:width]
            pages_ref[i, 1] = other_ref[chip, pl.ds(row, PAGE), width : 2 * width]

    scan_keys(
        lengths_ref, q_ref, mine_ref, other_ref, (pb + 1) * row_tokens + kv * rows, pb * row_tokens, core, acc, top, total
    )
    part_ref[0:HD, :] = (acc[...] / jnp.maximum(total[...], 1e-30)).astype(jnp.bfloat16)
    stats = split_three(top[...]) + split_three(total[...])
    stats.append(jnp.zeros((STAT_ROWS - len(stats), acc.shape[1]), jnp.bfloat16))
    part_ref[HD : HD + STAT_ROWS, :] = jnp.concatenate(stats, axis=0)


def own_kernel(at_ref, lengths_ref, q_ref, mine_ref, other_ref, acc, top, total):
    pb, kv, n_kv = at_ref[0], at_ref[1], at_ref[3]
    core = lax.rem(kv, 2)
    rows = q_ref.shape[0]
    row_tokens = n_kv * rows
    scan_keys(
        lengths_ref, q_ref, mine_ref, other_ref, pb * row_tokens + kv * rows, pb * row_tokens, core, acc, top, total
    )


def join_kernel(acc_ref, top_ref, total_ref, part_ref, out_ref):
    part = part_ref[0:HD, :].astype(jnp.float32)
    stats = part_ref[HD : HD + STAT_ROWS, :].astype(jnp.float32)
    part_top = stats[0:1] + stats[1:2] + stats[2:3]
    part_total = stats[3:4] + stats[4:5] + stats[5:6]
    part_top = jnp.where(part_total > 0.0, part_top, LOWEST)
    top = jnp.maximum(top_ref[...], part_top)
    own = jnp.exp2(top_ref[...] - top)
    weight = jnp.where(part_total > 0.0, jnp.exp2(part_top - top) * part_total, 0.0)
    inverse = 1.0 / (total_ref[...] * own + weight)
    own = own * inverse
    weight = weight * inverse
    rows = out_ref.shape[0]
    for i in range(out_ref.shape[1] // HD):
        at = slice(i * rows, (i + 1) * rows)
        mixed = acc_ref[:, at] * own[:, at] + part[:, at] * weight[:, at]
        out_ref[:, i * HD : (i + 1) * HD] = jnp.transpose(mixed).astype(jnp.bfloat16)


SMEM = pl.BlockSpec(memory_space=pltpu.SMEM)
VMEM = pl.BlockSpec(memory_space=pltpu.VMEM)
PARAMS = pltpu.CompilerParams(vmem_limit_bytes=40 * 1024 * 1024)


def cost(flops, nbytes):
    return pl.CostEstimate(flops=flops, bytes_accessed=nbytes, transcendentals=0)


def body(queries, keys, values, doc_lengths, page_table):
    rows = queries.shape[0]
    n_head = lax.axis_size("head")
    n_pb = lax.axis_size("pb")
    n_kv = lax.axis_size("kv")
    chips = n_kv // 2
    width = keys.shape[1]
    columns = queries.shape[1]
    lanes = columns // HD * rows
    n_slots = rows // PAGE
    at = jnp.stack([lax.axis_index("pb"), lax.axis_index("kv"), n_pb, n_kv, n_head]).astype(jnp.int32)
    later = lax.ppermute(queries, "pb", [(i + 1, i) for i in range(n_pb - 1)])
    both = jnp.concatenate([keys, values], axis=1)
    sent = jnp.broadcast_to(both[None], (chips, *both.shape))
    ring = [[2 * i + core for i in range(chips)] for core in range(2)]
    mine = lax.all_to_all(sent, "kv", 0, 0, tiled=True, axis_index_groups=ring)
    other = lax.ppermute(mine, "kv", [(i, i ^ 1) for i in range(n_kv)])
    flops = 4 * columns * rows * n_kv * rows
    state = [(HD, lanes), (1, lanes), (1, lanes)]
    part, pages = pl.pallas_call(
        later_kernel,
        out_shape=(
            jax.ShapeDtypeStruct((HD + STAT_ROWS, lanes), jnp.bfloat16),
            jax.ShapeDtypeStruct((n_slots, 2, PAGE, width), jnp.bfloat16),
        ),
        in_specs=[SMEM, SMEM, SMEM, VMEM, VMEM, VMEM],
        out_specs=(VMEM, VMEM),
        scratch_shapes=[pltpu.VMEM(shape, jnp.float32) for shape in state],
        compiler_params=PARAMS,
        cost_estimate=cost(flops, 3 << 20),
        name="later_rows",
    )(at, doc_lengths, page_table, later, mine, other)
    back = lax.ppermute(part, "pb", [(i, i + 1) for i in range(n_pb - 1)])
    page_pool = lax.all_to_all(pages, "head", split_axis=0, concat_axis=3, tiled=True)
    own = pl.pallas_call(
        own_kernel,
        out_shape=tuple(jax.ShapeDtypeStruct(shape, jnp.float32) for shape in state),
        in_specs=[SMEM, SMEM, VMEM, VMEM, VMEM],
        out_specs=(VMEM, VMEM, VMEM),
        compiler_params=PARAMS,
        cost_estimate=cost(flops, 3 << 20),
        name="own_row",
    )(at, doc_lengths, queries, mine, other)
    attended = pl.pallas_call(
        join_kernel,
        out_shape=jax.ShapeDtypeStruct((rows, columns), jnp.bfloat16),
        in_specs=[VMEM] * 4,
        out_specs=VMEM,
        compiler_params=PARAMS,
        cost_estimate=cost(1 << 20, 1 << 20),
        name="join_rows",
    )(*own, back)
    return (attended, page_pool)


def solution(mesh):
    in_specs = (P(("pb", "kv"), "head"), P(("pb", "kv"), "head"), P(("pb", "kv"), "head"), P(), P())
    out_specs = (P(("pb", "kv"), "head"), P(("head", "pb", "kv"), None, None, None))
    return jax.shard_map(body, mesh=mesh, in_specs=in_specs, out_specs=out_specs, check_vma=False)
```

time: 205 us -> 75.3 us (0.37)
  the two profiles are of different devices: /device:TPU:67 before, /device:TPU:192 now
where the time goes in v1:
time: 75.3 us; the launch traced here: 74.9 us
  blocking collectives  35.8 us (48%)
  waiting for transfers between devices  14.9 us (20%)
  starting transfers between devices  13.4 us (18%)
  Pallas kernels  7.42 us (10%)
  local copies, waits for them, and re-layouts  1.75 us (2%)
  other arithmetic  0.88 us (1%)
    all_to_all x1, blocking collectives, body(): mine = lax.all_to_all(sent, 'kv', 0, 0, tiled=True, axis_index_groups=ring)  35.8 us
    ppermute x1, waiting for transfers between devices, body(): later = lax.ppermute(queries, 'pb', [(i + 1, i) for i in range(n_pb - 1)])  10.4 us
    ppermute x1, starting transfers between devices, body(): back = lax.ppermute(part, 'pb', [(i, i + 1) for i in range(n_pb - 1)])  5.28 us
    pallas_call x1, Pallas kernels, body(): pl.pallas_call(later_kernel, out_shape=(jax.ShapeDtypeStruct((HD + STAT_R...  4.97 us
    all_to_all x1, waiting for transfers between devices, body(): lax.all_to_all(pages, 'head', split_axis=0, concat_axis=3, tiled=True)  4.51 us
    all_to_all x1, starting transfers between devices, body(): lax.all_to_all(pages, 'head', split_axis=0, concat_axis=3, tiled=True)  4.31 us
    ppermute x1, starting transfers between devices, body(): later = lax.ppermute(queries, 'pb', [(i + 1, i) for i in range(n_pb - 1)])  1.92 us
    ppermute x1, starting transfers between devices, body(): other = lax.ppermute(mine, 'kv', [(i, i ^ 1) for i in range(n_kv)])  1.91 us
  transfers between devices with their start and end apart: 4, of which 2 were waited for; matrix products, arithmetic and copies ran while one was open for 2% of the time, Pallas kernels for 2%

profile of v1, /device:TPU:192, one launch (start us, length us, event | category | flops | bytes accessed | tf_op | source)
XLA Modules:
  0.0 74.9 jit_solution(1532719069588478449)
XLA Ops:
  0.6 0.9 %pad_maximum_fusion = bf16[128,512]{1,0:T(8,128)(2,1)S(1)} fusion(bf16[128,256]{1,0:T(8,128)(2,1)} %param.7, bf16[128,256]{1,0:T(8,128)(2,1)} %param.6), kind=kLoop, calls=%fused_computation | loop fusion | flops 262144 | bytes 262144 | tf_op jit(solution)/shard_map/concatenate | solution.py:190
  1.5 0.1 broadcast_in_dim.2
  1.6 0.0 copy-start
  1.6 35.8 %all_to_all.23.mine_ref = bf16[8,128,512]{2,1,0:T(8,128)(2,1)S(1)} all-to-all(bf16[8,128,512]{2,1,0:T(8,128)(2,1)S(1)} %broadcast_in_dim.2), channel_id=1, replica_groups={{0,2,4,6,8,10,12,14},{1,3,5,7,9,11,13,15},{16,18,20,22,24,26,28,30},{17..., dimensions={0} | all-to-all | bytes 2097152 | tf_op jit(solution)/shard_map/all_to_all | solution.py:193
  37.4 1.9 %collective-permute-start = (bf16[8,128,512]{2,1,0:T(8,128)(2,1)S(1)}, bf16[8,128,512]{2,1,0:T(8,128)(2,1)S(1)}, u32[]{:S(2)}, u32[]{:S(2)}) collective-permute-start(bf16[8,128,512]{2,1,0:T(8,128)(2,1)S(1)} %all_to_all.23.mine_ref), channel_id=1, source_target_pairs={{0,1},{1,0},{2,3},{3,2},{4,5},{5,4},{6,7},{7,6},{8,9},{9,8},{10,11... | collective-permute-start | bytes 3145736 | tf_op jit(solution)/shard_map/ppermute | solution.py:194
  39.3 0.0 copy-done
  39.3 1.9 %collective-permute-start.1 = (bf16[128,1024]{1,0:T(8,128)(2,1)S(1)}, bf16[128,1024]{1,0:T(8,128)(2,1)S(1)}, u32[]{:S(2)}, u32[]{:S(2)}) collective-permute-start(bf16[128,1024]{1,0:T(8,128)(2,1)S(1)} %copy-done), channel_id=1, source_target_pairs={{16,0},{32,16},{48,32},{64,48},{80,64},{96,80},{112,96},{17,1},{33... | collective-permute-start | bytes 786440 | tf_op jit(solution)/shard_map/ppermute | solution.py:189
  41.2 0.0 copy-start.1
  41.3 0.0 copy-start.2
  41.3 0.1 stack.11.at_ref
  41.3 10.4 %collective-permute-done.1.q_ref = bf16[128,1024]{1,0:T(8,128)(2,1)S(1)} collective-permute-done((bf16[128,1024]{1,0:T(8,128)(2,1)S(1)}, bf16[128,1024]{1,0:T(8,128)(2,1)S(1)}, u32[]{:S(2)}, u32[]{:S(2)}) %collective-permute-start.1) | collective-permute-done | bytes 262176 | tf_op jit(solution)/shard_map/ppermute | solution.py:189
  51.8 0.0 collective-permute-done.other_ref
  51.8 0.0 copy-done.1
  51.8 0.0 copy-done.2
  51.8 5.0 %later_rows.1 = (bf16[144,1024]{1,0:T(8,128)(2,1)S(1)}, bf16[8,2,16,256]{3,2,1,0:T(8,128)(2,1)}) custom-call(s32[5]{0:T(128)S(1)} %stack.11.at_ref, s32[17]{0:T(128)S(1)} %copy-done.2, s32[1024]{0:T(1024)S(1)} %copy-done.1, bf16[128,1024]{1,0:T(8,128)(2,1)S(1)} %collective-permute-done.1.q_ref, bf16[8,128,512]{2,1,0:T(8,128)(2,1)S(1)} %all_to_all.23.mine_ref, ...), custom_call_target="tpu_custom_call" | custom-call | flops 1073741824 | bytes 3145728 | tf_op jit(solution)/shard_map/later_rows/pallas_call | solution.py:197
  56.7 5.3 %collective-permute-start.2 = (bf16[144,1024]{1,0:T(8,128)(2,1)S(1)}, bf16[144,1024]{1,0:T(8,128)(2,1)S(1)}, u32[]{:S(2)}, u32[]{:S(2)}) collective-permute-start(bf16[144,1024]{1,0:T(8,128)(2,1)S(1)} %get-tuple-element.10), channel_id=1, source_target_pairs={{0,16},{16,32},{32,48},{48,64},{64,80},{80,96},{96,112},{1,17},{17... | collective-permute-start | bytes 884744 | tf_op jit(solution)/shard_map/ppermute | solution.py:210
  62.0 4.3 %all-to-all-start.1 = ((bf16[8,2,16,256]{3,2,1,0:T(8,128)(2,1)}), bf16[8,2,16,256]{3,2,1,0:T(8,128)(2,1)}, u32[]{:S(2)}, u32[]{:S(2)}) async-start(bf16[8,2,16,256]{3,2,1,0:T(8,128)(2,1)} %get-tuple-element.11), calls=%async_computation.1 | async-start | bytes 262144 | tf_op jit(solution)/shard_map/all_to_all | solution.py:211
  66.3 1.6 %own_row.1 = (f32[128,1024]{1,0:T(8,128)S(1)}, f32[1,1024]{1,0:T(1,128)S(1)}, f32[1,1024]{1,0:T(1,128)S(1)}) custom-call(s32[5]{0:T(128)S(1)} %stack.11.at_ref, s32[17]{0:T(128)S(1)} %copy-done.2, bf16[128,1024]{1,0:T(8,128)(2,1)S(1)} %copy-done, bf16[8,128,512]{2,1,0:T(8,128)(2,1)S(1)} %all_to_all.23.mine_ref, ...), custom_call_target="tpu_custom_call" | custom-call | flops 1073741824 | bytes 3145728 | tf_op jit(solution)/shard_map/own_row/pallas_call | solution.py:212
  67.9 4.5 %all-to-all-done.1 = bf16[8,2,16,256]{3,2,1,0:T(8,128)(2,1)} async-done(((bf16[8,2,16,256]{3,2,1,0:T(8,128)(2,1)}), bf16[8,2,16,256]{3,2,1,0:T(8,128)(2,1)}, u32[]{:S(2)}, u32[]{:S(2)}) %all-to-all-start.1) | async-done | bytes 131104 | tf_op jit(solution)/shard_map/all_to_all | solution.py:211
  72.4 1.6 %copy.8 = bf16[4,2,2,2,8,256]{5,4,0,3,2,1:T(8,128)(2,1)} copy(bf16[4,2,2,2,8,256]{5,4,3,2,1,0:T(8,128)(2,1)} %bitcast.5) | data formatting | bytes 262144 | tf_op jit(solution)/shard_map/all_to_all | solution.py:211
  74.0 0.0 collective-permute-done.2.part_ref
  74.0 0.9 %join_rows.1 = bf16[128,1024]{1,0:T(8,128)(2,1)} custom-call(f32[128,1024]{1,0:T(8,128)S(1)} %get-tuple-element.7.acc_ref, f32[1,1024]{1,0:T(1,128)S(1)} %get-tuple-element.8.top_ref, f32[1,1024]{1,0:T(1,128)S(1)} %get-tuple-element.9.total_ref, bf16[144,1024]{1,0:T(8,128)(2,1)S(1)} %collective-permute-done.2.part_ref), custom_call_target="tpu_custom_call" | custom-call | flops 1048576 | bytes 1048576 | tf_op jit(solution)/shard_map/join_rows/pallas_call | solution.py:221
Async XLA Ops:
  1.6 37.7 %copy-start = (bf16[128,1024]{1,0:T(8,128)(2,1)S(1)}, bf16[128,1024]{1,0:T(8,128)(2,1)}, u32[]{:S(2)}) copy-start(bf16[128,1024]{1,0:T(8,128)(2,1)} %q_ref.1) | copy-start | bytes 786436
  37.4 14.4 %collective-permute-start = (bf16[8,128,512]{2,1,0:T(8,128)(2,1)S(1)}, bf16[8,128,512]{2,1,0:T(8,128)(2,1)S(1)}, u32[]{:S(2)}, u32[]{:S(2)}) collective-permute-start(bf16[8,128,512]{2,1,0:T(8,128)(2,1)S(1)} %all_to_all.23.mine_ref), channel_id=1, source_target_pairs={{0,1},{1,0},{2,3},{3,2},{4,5},{5,4},{6,7},{7,6},{8,9},{9,8},{10,11... | collective-permute-start | bytes 3145736 | tf_op jit(solution)/shard_map/ppermute | solution.py:194
  39.3 12.5 %collective-permute-start.1 = (bf16[128,1024]{1,0:T(8,128)(2,1)S(1)}, bf16[128,1024]{1,0:T(8,128)(2,1)S(1)}, u32[]{:S(2)}, u32[]{:S(2)}) collective-permute-start(bf16[128,1024]{1,0:T(8,128)(2,1)S(1)} %copy-done), channel_id=1, source_target_pairs={{16,0},{32,16},{48,32},{64,48},{80,64},{96,80},{112,96},{17,1},{33... | collective-permute-start | bytes 786440 | tf_op jit(solution)/shard_map/ppermute | solution.py:189
  41.2 10.5 %copy-start.1 = (s32[1024]{0:T(1024)S(1)}, s32[1024]{0:T(1024)}, u32[]{:S(2)}) copy-start(s32[1024]{0:T(1024)} %table_ref.1) | copy-start | bytes 12292
  41.3 10.5 %copy-start.2 = (s32[17]{0:T(128)S(1)}, s32[17]{0:T(128)}, u32[]{:S(2)}) copy-start(s32[17]{0:T(128)} %lengths_ref.3) | copy-start | bytes 208
  56.7 17.3 %collective-permute-start.2 = (bf16[144,1024]{1,0:T(8,128)(2,1)S(1)}, bf16[144,1024]{1,0:T(8,128)(2,1)S(1)}, u32[]{:S(2)}, u32[]{:S(2)}) collective-permute-start(bf16[144,1024]{1,0:T(8,128)(2,1)S(1)} %get-tuple-element.10), channel_id=1, source_target_pairs={{0,16},{16,32},{32,48},{48,64},{64,80},{80,96},{96,112},{1,17},{17... | collective-permute-start | bytes 884744 | tf_op jit(solution)/shard_map/ppermute | solution.py:210
  62.0 10.4 %all-to-all-start.1 = ((bf16[8,2,16,256]{3,2,1,0:T(8,128)(2,1)}), bf16[8,2,16,256]{3,2,1,0:T(8,128)(2,1)}, u32[]{:S(2)}, u32[]{:S(2)}) async-start(bf16[8,2,16,256]{3,2,1,0:T(8,128)(2,1)} %get-tuple-element.11), calls=%async_computation.1 | async-start | bytes 262144 | tf_op jit(solution)/shard_map/all_to_all | solution.py:211

commit v2 on v1

v2 whole, which is shorter than its diff:
```python
import math

import jax
import jax.numpy as jnp
from jax import lax
from jax.experimental import pallas as pl
from jax.experimental.pallas import tpu as pltpu
from jax.sharding import PartitionSpec as P

HD = 128
PAGE = 16
SPAN = 2
LOWEST = -1e30
STAT_ROWS = 16
FACTOR = HD**-0.5 * math.log2(math.e)


def doc_start(lengths_ref, position):
    bound = jnp.int32(0)
    start = jnp.zeros_like(position)
    for i in range(lengths_ref.shape[0]):
        bound = bound + lengths_ref[i]
        start = jnp.where(bound <= position, bound, start)
    return start


def turn_kernel(*refs):
    for q_ref, out_ref in zip(refs[: len(refs) // 2], refs[len(refs) // 2 :], strict=True):
        rows = q_ref.shape[0]
        for i in range(q_ref.shape[1] // HD):
            out_ref[:, i * rows : (i + 1) * rows] = jnp.transpose(q_ref[:, i * HD : (i + 1) * HD])


def scan_keys(lengths_ref, q_ref, mine_ref, other_ref, q_base, k_base, core, acc, top, total, kept):
    rows = mine_ref.shape[1]
    width = mine_ref.shape[2] // 2
    groups = width // HD
    lanes = q_ref.shape[1] // groups
    heads = lanes // rows
    tile = 2 * rows * SPAN
    count = mine_ref.shape[0] // SPAN
    acc[...] = jnp.zeros_like(acc)
    top[...] = jnp.full_like(top, LOWEST)
    total[...] = jnp.zeros_like(total)
    first_start = doc_start(lengths_ref, q_base)
    last_start = doc_start(lengths_ref, q_base + rows - 1)
    q_pos = q_base + lax.broadcasted_iota(jnp.int32, (1, rows), 1)
    q_start = doc_start(lengths_ref, q_pos)
    low_tile = jnp.clip(lax.div(first_start - k_base, tile), 0, count)
    high_tile = jnp.clip(lax.div(q_base + rows - 1 - k_base, tile) + 1, 0, count)

    def columns(at, cols):
        parts = []
        for chip in range(SPAN):
            parts += [mine_ref[at * SPAN + chip, :, cols], other_ref[at * SPAN + chip, :, cols]]
        return jnp.concatenate(parts, axis=0)

    def score(at, masked):
        if masked:
            row = lax.broadcasted_iota(jnp.int32, (2 * rows, rows), 0)
            k_pos = k_base + at * tile + jnp.where(row < rows, row + core * rows, row - core * rows)
            k_pos = jnp.concatenate([k_pos + chip * 2 * rows for chip in range(SPAN)], axis=0)
            seen = (k_pos <= q_pos) & (k_pos >= q_start)
            seen = jnp.concatenate([seen] * heads, axis=1)
        for g in range(groups):
            where = slice(g * lanes, (g + 1) * lanes)
            keys = columns(at, slice(g * HD, (g + 1) * HD))
            scores = jnp.dot(keys, q_ref[:, where], preferred_element_type=jnp.float32)
            if masked:
                scores = jnp.where(seen, scores, LOWEST)
            kept[at, g] = scores
            top[:, where] = jnp.maximum(top[:, where], jnp.max(scores, axis=0, keepdims=True))

    def first_pass(at, carry):
        low = k_base + at * tile
        whole = (low + tile - 1 <= q_base) & (low >= last_start)

        @pl.when(whole)
        def _():
            score(at, False)

        @pl.when(jnp.logical_not(whole))
        def _():
            score(at, True)

        return carry

    def second_pass(at, carry):
        for g in range(groups):
            where = slice(g * lanes, (g + 1) * lanes)
            peak = jnp.maximum(top[:, where], 0.1 * LOWEST) * FACTOR
            weights = jnp.exp2(kept[at, g] * FACTOR - peak)
            total[:, where] = total[:, where] + jnp.sum(weights, axis=0, keepdims=True)
            values = columns(at, slice(width + g * HD, width + (g + 1) * HD))
            acc[:, where] = acc[:, where] + lax.dot_general(
                values, weights.astype(jnp.bfloat16), (((0,), (0,)), ((), ())), preferred_element_type=jnp.float32
            )
        return carry

    lax.fori_loop(low_tile, high_tile, first_pass, 0)
    lax.fori_loop(low_tile, high_tile, second_pass, 0)


def split_three(value):
    high = value.astype(jnp.bfloat16)
    rest = value - high.astype(jnp.float32)
    middle = rest.astype(jnp.bfloat16)
    low = (rest - middle.astype(jnp.float32)).astype(jnp.bfloat16)
    return [high, middle, low]


def later_kernel(at_ref, lengths_ref, q_ref, mine_ref, other_ref, part_ref, acc, top, total, kept):
    pb, kv, n_kv = at_ref[0], at_ref[1], at_ref[3]
    rows = mine_ref.shape[1]
    row_tokens = n_kv * rows
    scan_keys(
        lengths_ref, q_ref, mine_ref, other_ref, (pb + 1) * row_tokens + kv * rows, pb * row_tokens, lax.rem(kv, 2),
        acc, top, total, kept,
    )
    part_ref[0:HD, :] = (acc[...] / jnp.maximum(total[...], 1e-30)).astype(jnp.bfloat16)
    stats = split_three(top[...]) + split_three(total[...])
    stats.append(jnp.zeros((STAT_ROWS - len(stats), acc.shape[1]), jnp.bfloat16))
    part_ref[HD : HD + STAT_ROWS, :] = jnp.concatenate(stats, axis=0)


def own_kernel(at_ref, lengths_ref, q_ref, mine_ref, other_ref, acc, top, total, kept):
    pb, kv, n_kv = at_ref[0], at_ref[1], at_ref[3]
    rows = mine_ref.shape[1]
    row_tokens = n_kv * rows
    scan_keys(
        lengths_ref, q_ref, mine_ref, other_ref, pb * row_tokens + kv * rows, pb * row_tokens, lax.rem(kv, 2),
        acc, top, total, kept,
    )


def pick_kernel(at_ref, table_ref, mine_ref, other_ref, pages_ref):
    pb, kv, n_pb, n_kv, n_head = at_ref[0], at_ref[1], at_ref[2], at_ref[3], at_ref[4]
    core = lax.rem(kv, 2)
    rows = mine_ref.shape[1]
    n_slots = pages_ref.shape[0]
    width = pages_ref.shape[3]
    row_pages = n_kv * rows // PAGE
    slot_rows = row_pages // n_head
    per = n_slots // 4
    for i in range(n_slots):
        slot = (i // per) * (n_pb * slot_rows) + pb * slot_rows + kv * per + i % per
        page = table_ref[slot] - pb * row_pages
        block_pages = rows // PAGE
        block = lax.div(page, block_pages)
        chip = lax.div(block, 2)
        row = pl.multiple_of(lax.rem(page, block_pages) * PAGE, PAGE)
        own = lax.rem(block, 2) == core
        for half in range(2):
            cols = slice(half * width, (half + 1) * width)
            pages_ref[i, half] = jnp.where(
                own, mine_ref[chip, pl.ds(row, PAGE), cols], other_ref[chip, pl.ds(row, PAGE), cols]
            )


def join_kernel(acc_ref, top_ref, total_ref, part_ref, pages_ref, out_ref, pool_ref):
    part = part_ref[0:HD, :].astype(jnp.float32)
    stats = part_ref[HD : HD + STAT_ROWS, :].astype(jnp.float32)
    part_top = stats[0:1] + stats[1:2] + stats[2:3]
    part_total = stats[3:4] + stats[4:5] + stats[5:6]
    part_top = jnp.where(part_total > 0.0, part_top, LOWEST)
    top = jnp.maximum(top_ref[...], part_top)
    own = jnp.exp2((top_ref[...] - top) * FACTOR)
    weight = jnp.where(part_total > 0.0, jnp.exp2((part_top - top) * FACTOR) * part_total, 0.0)
    inverse = 1.0 / (total_ref[...] * own + weight)
    own = own * inverse
    weight = weight * inverse
    rows = out_ref.shape[0]
    for i in range(out_ref.shape[1] // HD):
        at = slice(i * rows, (i + 1) * rows)
        mixed = acc_ref[:, at] * own[:, at] + part[:, at] * weight[:, at]
        out_ref[:, i * HD : (i + 1) * HD] = jnp.transpose(mixed).astype(jnp.bfloat16)
    slots = pool_ref.shape[0]
    width = pages_ref.shape[3]
    for i in range(pages_ref.shape[0] // slots):
        pool_ref[:, :, :, i * width : (i + 1) * width] = pages_ref[i * slots : (i + 1) * slots]


SMEM = pl.BlockSpec(memory_space=pltpu.SMEM)
VMEM = pl.BlockSpec(memory_space=pltpu.VMEM)
PARAMS = pltpu.CompilerParams(vmem_limit_bytes=40 * 1024 * 1024)


def call(kernel, out_shape, in_specs, name, flops, scratch=()):
    several = isinstance(out_shape, tuple)
    return pl.pallas_call(
        kernel,
        out_shape=out_shape,
        in_specs=in_specs,
        out_specs=(VMEM,) * len(out_shape) if several else VMEM,
        scratch_shapes=scratch,
        compiler_params=PARAMS,
        cost_estimate=pl.CostEstimate(flops=flops, bytes_accessed=3 << 20, transcendentals=0),
        name=name,
    )


def body(queries, keys, values, doc_lengths, page_table):
    rows = queries.shape[0]
    n_head = lax.axis_size("head")
    n_pb = lax.axis_size("pb")
    n_kv = lax.axis_size("kv")
    chips = n_kv // 2
    width = keys.shape[1]
    columns = queries.shape[1]
    lanes = columns // HD * rows
    n_slots = rows // PAGE
    shape = jax.ShapeDtypeStruct
    at = jnp.stack([lax.axis_index("pb"), lax.axis_index("kv"), n_pb, n_kv, n_head]).astype(jnp.int32)
    later = lax.ppermute(queries, "pb", [(i + 1, i) for i in range(n_pb - 1)])
    both = jnp.concatenate([keys, values], axis=1)
    sent = jnp.broadcast_to(both[None], (chips, *both.shape))
    ring = [[2 * i + core for i in range(chips)] for core in range(2)]
    mine = lax.all_to_all(sent, "kv", 0, 0, tiled=True, axis_index_groups=ring)
    turned, later_turned = call(
        turn_kernel, (shape((HD, lanes), jnp.bfloat16),) * 2, [VMEM] * 2, "turn_queries", 1 << 20
    )(queries, later)
    mine, turned, later_turned = lax.optimization_barrier((mine, turned, later_turned))
    other = lax.ppermute(mine, "kv", [(i, i ^ 1) for i in range(n_kv)])
    flops = 4 * columns * rows * n_kv * rows
    state = [(HD, lanes), (1, lanes), (1, lanes)]
    kept = pltpu.VMEM((chips // SPAN, width // HD, 2 * rows * SPAN, lanes // (width // HD)), jnp.float32)
    part = call(
        later_kernel, shape((HD + STAT_ROWS, lanes), jnp.bfloat16), [SMEM, SMEM, VMEM, VMEM, VMEM], "later_rows", flops,
        [pltpu.VMEM(one, jnp.float32) for one in state] + [kept],
    )(at, doc_lengths, later_turned, mine, other)
    back = lax.ppermute(part, "pb", [(i, i + 1) for i in range(n_pb - 1)])
    pages = call(
        pick_kernel, shape((n_slots, 2, PAGE, width), jnp.bfloat16), [SMEM, SMEM, VMEM, VMEM], "pick_pages", 1 << 20
    )(at, page_table, mine, other)
    arrived = lax.all_to_all(pages, "head", split_axis=0, concat_axis=0, tiled=True)
    own = call(
        own_kernel, tuple(shape(one, jnp.float32) for one in state), [SMEM, SMEM, VMEM, VMEM, VMEM], "own_row", flops, [kept]
    )(at, doc_lengths, turned, mine, other)
    return call(
        join_kernel,
        (shape((rows, columns), jnp.bfloat16), shape((n_slots // n_head, 2, PAGE, n_head * width), jnp.bfloat16)),
        [VMEM] * 5,
        "join_rows",
        1 << 20,
    )(*own, back, arrived)


def solution(mesh):
    in_specs = (P(("pb", "kv"), "head"), P(("pb", "kv"), "head"), P(("pb", "kv"), "head"), P(), P())
    out_specs = (P(("pb", "kv"), "head"), P(("head", "pb", "kv"), None, None, None))
    return jax.shard_map(body, mesh=mesh, in_specs=in_specs, out_specs=out_specs, check_vma=False)
```

time: 75.3 us -> 65.1 us (0.86)
  blocking collectives: 35.8 us -> 0 us
  waiting for transfers between devices: 14.9 us -> 31.9 us
  starting transfers between devices: 13.4 us -> 21.8 us
  local copies, waits for them, and re-layouts: 1.75 us -> 2.81 us
  Pallas kernels: 7.42 us -> 6.63 us
    all_to_all x1 -> x0, blocking collectives: 35.8 us -> none  [body(): mine = lax.all_to_all(sent, 'kv', 0, 0, tiled=True, axis_index_groups=ring)]
    all_to_all x1 -> x2, waiting for transfers between devices: 4.51 us -> 19.8 us  [the longest x1 16.3 us: body(): mine = lax.all_to_all(sent, 'kv', 0, 0, tiled=True, axis_index_groups=ring)]
    all_to_all x1 -> x2, starting transfers between devices: 4.31 us -> 11.5 us  [the longest x1 7.23 us: body(): mine = lax.all_to_all(sent, 'kv', 0, 0, tiled=True, axis_index_groups=ring)]
    ppermute x1, waiting for transfers between devices: 0.01 us -> 2.52 us  [body(): other = lax.ppermute(mine, 'kv', [(i, i ^ 1) for i in range(n_kv)])]
    unnamed x6 -> x10, local copies, waits for them, and re-layouts: 0.02 us -> 1.66 us
    all_to_all x1 -> x0, local copies, waits for them, and re-layouts: 1.57 us -> none  [body(): lax.all_to_all(pages, 'head', split_axis=0, concat_axis=3, tiled=True)]
    ppermute x1, starting transfers between devices: 5.28 us -> 6.47 us  [body(): back = lax.ppermute(part, 'pb', [(i, i + 1) for i in range(n_pb - 1)])]
    broadcast_in_dim x1, local copies, waits for them, and re-layouts: 0.08 us -> 1.06 us  [body(): sent = jnp.broadcast_to(both[None], (chips, *both.shape))]
  transfers between devices with their start and end apart: 4 -> 5, of which waited for: 2 -> 4; matrix products, arithmetic and copies ran while one was open for 2% -> 0% of each run, Pallas kernels for 2% -> 5%
where the time goes in v2:
time: 65.1 us; the launch traced here: 64.7 us
  waiting for transfers between devices  31.9 us (49%)
  starting transfers between devices  21.8 us (33%)
  Pallas kernels  6.63 us (10%)
  local copies, waits for them, and re-layouts  2.81 us (4%)
  other arithmetic  0.88 us (1%)
  between operations  0.72 us (1%)
    all_to_all x1, waiting for transfers between devices, body(): mine = lax.all_to_all(sent, 'kv', 0, 0, tiled=True, axis_index_groups=ring)  16.3 us
    ppermute x1, waiting for transfers between devices, body(): later = lax.ppermute(queries, 'pb', [(i + 1, i) for i in range(n_pb - 1)])  9.58 us
    all_to_all x1, starting transfers between devices, body(): mine = lax.all_to_all(sent, 'kv', 0, 0, tiled=True, axis_index_groups=ring)  7.23 us
    ppermute x1, starting transfers between devices, body(): back = lax.ppermute(part, 'pb', [(i, i + 1) for i in range(n_pb - 1)])  6.47 us
    all_to_all x1, starting transfers between devices, body(): lax.all_to_all(pages, 'head', split_axis=0, concat_axis=0, tiled=True)  4.3 us
    all_to_all x1, waiting for transfers between devices, body(): lax.all_to_all(pages, 'head', split_axis=0, concat_axis=0, tiled=True)  3.45 us
    pallas_call x1, Pallas kernels, body(): call(later_kernel, shape((HD + STAT_ROWS, lanes), jnp.bfloat16), [SMEM, S...  2.62 us
    ppermute x1, waiting for transfers between devices, body(): other = lax.ppermute(mine, 'kv', [(i, i ^ 1) for i in range(n_kv)])  2.52 us
  transfers between devices with their start and end apart: 5, of which 4 were waited for; matrix products, arithmetic and copies ran while one was open for 0% of the time, Pallas kernels for 5%

profile of v2, /device:TPU:192, one launch (start us, length us, event | category | flops | bytes accessed | tf_op | source)
XLA Modules:
  0.0 64.7 jit_solution(8293178612031381414)
XLA Ops:
  0.6 0.9 %pad_maximum_fusion = bf16[128,512]{1,0:T(8,128)(2,1)S(1)} fusion(bf16[128,256]{1,0:T(8,128)(2,1)} %param.7, bf16[128,256]{1,0:T(8,128)(2,1)} %param.6), kind=kLoop, calls=%fused_computation | loop fusion | flops 262144 | bytes 262144 | tf_op jit(solution)/shard_map/concatenate | solution.py:215
  1.5 1.1 %broadcast_in_dim.2 = bf16[8,128,512]{2,1,0:T(8,128)(2,1)} broadcast(bf16[128,512]{1,0:T(8,128)(2,1)S(1)} %pad_maximum_fusion), dimensions={1,2} | broadcast | bytes 1179648 | tf_op jit(solution)/shard_map/broadcast_in_dim | solution.py:216
  2.6 0.0 copy-start
  2.6 7.2 %all-to-all-start = ((bf16[8,128,512]{2,1,0:T(8,128)(2,1)}), bf16[8,128,512]{2,1,0:T(8,128)(2,1)S(1)}, u32[]{:S(2)}, u32[]{:S(2)}) async-start(bf16[8,128,512]{2,1,0:T(8,128)(2,1)} %broadcast_in_dim.2), calls=%async_computation | async-start | bytes 2097152 | tf_op jit(solution)/shard_map/all_to_all | solution.py:218
  9.8 0.0 copy-done
  9.8 1.9 %collective-permute-start = (bf16[128,1024]{1,0:T(8,128)(2,1)S(1)}, bf16[128,1024]{1,0:T(8,128)(2,1)S(1)}, u32[]{:S(2)}, u32[]{:S(2)}) collective-permute-start(bf16[128,1024]{1,0:T(8,128)(2,1)S(1)} %copy-done), channel_id=1, source_target_pairs={{16,0},{32,16},{48,32},{64,48},{80,64},{96,80},{112,96},{17,1},{33... | collective-permute-start | bytes 786440 | tf_op jit(solution)/shard_map/ppermute | solution.py:214
  11.7 9.6 %collective-permute-done.refs_1_ = bf16[128,1024]{1,0:T(8,128)(2,1)S(1)} collective-permute-done((bf16[128,1024]{1,0:T(8,128)(2,1)S(1)}, bf16[128,1024]{1,0:T(8,128)(2,1)S(1)}, u32[]{:S(2)}, u32[]{:S(2)}) %collective-permute-start) | collective-permute-done | bytes 262176 | tf_op jit(solution)/shard_map/ppermute | solution.py:214
  21.3 0.2 turn_queries.1
  21.5 0.0 copy-start.2
  21.5 0.7 %copy-done.2 = bf16[128,1024]{1,0:T(8,128)(2,1)} copy-done((bf16[128,1024]{1,0:T(8,128)(2,1)}, bf16[128,1024]{1,0:T(8,128)(2,1)S(1)}, u32[]{:S(2)}) %copy-start.2) | copy-done | bytes 262168
  22.2 16.3 %all-to-all-done.mine_ref = bf16[8,128,512]{2,1,0:T(8,128)(2,1)S(1)} async-done(((bf16[8,128,512]{2,1,0:T(8,128)(2,1)}), bf16[8,128,512]{2,1,0:T(8,128)(2,1)S(1)}, u32[]{:S(2)}, u32[]{:S(2)}) %all-to-all-start) | async-done | bytes 1048608 | tf_op jit(solution)/shard_map/all_to_all | solution.py:218
  38.5 1.9 %collective-permute-start.1 = (bf16[8,128,512]{2,1,0:T(8,128)(2,1)S(1)}, bf16[8,128,512]{2,1,0:T(8,128)(2,1)S(1)}, u32[]{:S(2)}, u32[]{:S(2)}) collective-permute-start(bf16[8,128,512]{2,1,0:T(8,128)(2,1)S(1)} %all-to-all-done.mine_ref), channel_id=1, source_target_pairs={{0,1},{1,0},{2,3},{3,2},{4,5},{5,4},{6,7},{7,6},{8,9},{9,8},{10,11... | collective-permute-start | bytes 3145736 | tf_op jit(solution)/shard_map/ppermute | solution.py:223
  40.5 0.0 copy-start.4
  40.5 0.1 stack.11.at_ref
  40.6 0.0 copy-start.1
  40.6 2.5 %collective-permute-done.1.other_ref = bf16[8,128,512]{2,1,0:T(8,128)(2,1)S(1)} collective-permute-done((bf16[8,128,512]{2,1,0:T(8,128)(2,1)S(1)}, bf16[8,128,512]{2,1,0:T(8,128)(2,1)S(1)}, u32[]{:S(2)}, u32[]{:S(2)}) %collective-permute-start.1) | collective-permute-done | bytes 1048608 | tf_op jit(solution)/shard_map/ppermute | solution.py:223
  43.1 0.0 copy-done.4
  43.1 2.6 %later_rows.1 = bf16[144,1024]{1,0:T(8,128)(2,1)S(1)} custom-call(s32[5]{0:T(128)S(1)} %stack.11.at_ref, s32[17]{0:T(128)S(1)} %copy-done.4, bf16[128,1024]{1,0:T(8,128)(2,1)S(1)} %get-tuple-element.17.q_ref, bf16[8,128,512]{2,1,0:T(8,128)(2,1)S(1)} %all-to-all-done.mine_ref, bf16[8,128,512]{2,1,0:T(8,128)(2,1)S(1)} %collective-permute-done.1.other_ref), custom_call_target="tpu_custom_call" | custom-call | flops 1073741824 | bytes 3145728 | tf_op jit(solution)/shard_map/later_rows/pallas_call | solution.py:227
  45.7 6.5 %collective-permute-start.2 = (bf16[144,1024]{1,0:T(8,128)(2,1)S(1)}, bf16[144,1024]{1,0:T(8,128)(2,1)S(1)}, u32[]{:S(2)}, u32[]{:S(2)}) collective-permute-start(bf16[144,1024]{1,0:T(8,128)(2,1)S(1)} %later_rows.1), channel_id=1, source_target_pairs={{0,16},{16,32},{32,48},{48,64},{64,80},{80,96},{96,112},{1,17},{17... | collective-permute-start | bytes 884744 | tf_op jit(solution)/shard_map/ppermute | solution.py:231
  52.2 0.0 copy-done.1
  52.2 1.4 %pick_pages.1 = bf16[8,2,16,256]{3,2,1,0:T(8,128)(2,1)} custom-call(s32[5]{0:T(128)S(1)} %stack.11.at_ref, s32[1024]{0:T(1024)S(1)} %copy-done.1, bf16[8,128,512]{2,1,0:T(8,128)(2,1)S(1)} %all-to-all-done.mine_ref, bf16[8,128,512]{2,1,0:T(8,128)(2,1)S(1)} %collective-permute-done.1.other_ref), custom_call_target="tpu_custom_call" | custom-call | flops 1048576 | bytes 3145728 | tf_op jit(solution)/shard_map/pick_pages/pallas_call | solution.py:232
  53.6 4.3 %all-to-all-start.1 = ((bf16[8,2,16,256]{3,2,1,0:T(8,128)(2,1)}), bf16[8,2,16,256]{3,2,1,0:T(8,128)(2,1)S(1)}, u32[]{:S(2)}, u32[]{:S(2)}) async-start(bf16[8,2,16,256]{3,2,1,0:T(8,128)(2,1)} %pick_pages.1), calls=%async_computation.1 | async-start | bytes 262144 | tf_op jit(solution)/shard_map/all_to_all | solution.py:235
  57.9 0.0 copy-start.3
  57.9 0.9 %copy-done.3 = bf16[128,1024]{1,0:T(8,128)(2,1)S(1)} copy-done((bf16[128,1024]{1,0:T(8,128)(2,1)S(1)}, bf16[128,1024]{1,0:T(8,128)(2,1)}, u32[]{:S(2)}) %copy-start.3) | copy-done | bytes 262168
  58.8 1.6 %own_row.1 = (f32[128,1024]{1,0:T(8,128)S(1)}, f32[1,1024]{1,0:T(1,128)S(1)}, f32[1,1024]{1,0:T(1,128)S(1)}) custom-call(s32[5]{0:T(128)S(1)} %stack.11.at_ref, s32[17]{0:T(128)S(1)} %copy-done.4, bf16[128,1024]{1,0:T(8,128)(2,1)S(1)} %copy-done.3, bf16[8,128,512]{2,1,0:T(8,128)(2,1)S(1)} %all-to-all-done.mine_ref, ...), custom_call_target="tpu_custom_call" | custom-call | flops 1073741824 | bytes 3145728 | tf_op jit(solution)/shard_map/own_row/pallas_call | solution.py:236
  60.4 3.5 %all-to-all-done.1.pages_ref = bf16[8,2,16,256]{3,2,1,0:T(8,128)(2,1)S(1)} async-done(((bf16[8,2,16,256]{3,2,1,0:T(8,128)(2,1)}), bf16[8,2,16,256]{3,2,1,0:T(8,128)(2,1)S(1)}, u32[]{:S(2)}, u32[]{:S(2)}) %all-to-all-start.1) | async-done | bytes 131104 | tf_op jit(solution)/shard_map/all_to_all | solution.py:235
  63.8 0.0 collective-permute-done.2.part_ref
  63.8 0.9 %join_rows.1 = (bf16[128,1024]{1,0:T(8,128)(2,1)}, bf16[2,2,16,1024]{3,2,1,0:T(8,128)(2,1)}) custom-call(f32[128,1024]{1,0:T(8,128)S(1)} %get-tuple-element.14.acc_ref, f32[1,1024]{1,0:T(1,128)S(1)} %get-tuple-element.15.top_ref, f32[1,1024]{1,0:T(1,128)S(1)} %get-tuple-element.16.total_ref, bf16[144,1024]{1,0:T(8,128)(2,1)S(1)} %collective-permute-done.2.part_ref, ...), custom_call_target="tpu_custom_call" | custom-call | flops 1048576 | bytes 3145728 | tf_op jit(solution)/shard_map/join_rows/pallas_call | solution.py:239
Async XLA Ops:
  2.6 7.2 %copy-start = (bf16[128,1024]{1,0:T(8,128)(2,1)S(1)}, bf16[128,1024]{1,0:T(8,128)(2,1)}, u32[]{:S(2)}) copy-start(bf16[128,1024]{1,0:T(8,128)(2,1)} %refs_0_.1) | copy-start | bytes 786436
  2.6 36.0 %all-to-all-start = ((bf16[8,128,512]{2,1,0:T(8,128)(2,1)}), bf16[8,128,512]{2,1,0:T(8,128)(2,1)S(1)}, u32[]{:S(2)}, u32[]{:S(2)}) async-start(bf16[8,128,512]{2,1,0:T(8,128)(2,1)} %broadcast_in_dim.2), calls=%async_computation | async-start | bytes 2097152 | tf_op jit(solution)/shard_map/all_to_all | solution.py:218
  9.8 11.5 %collective-permute-start = (bf16[128,1024]{1,0:T(8,128)(2,1)S(1)}, bf16[128,1024]{1,0:T(8,128)(2,1)S(1)}, u32[]{:S(2)}, u32[]{:S(2)}) collective-permute-start(bf16[128,1024]{1,0:T(8,128)(2,1)S(1)} %copy-done), channel_id=1, source_target_pairs={{16,0},{32,16},{48,32},{64,48},{80,64},{96,80},{112,96},{17,1},{33... | collective-permute-start | bytes 786440 | tf_op jit(solution)/shard_map/ppermute | solution.py:214
  21.5 0.7 %copy-start.2 = (bf16[128,1024]{1,0:T(8,128)(2,1)}, bf16[128,1024]{1,0:T(8,128)(2,1)S(1)}, u32[]{:S(2)}) copy-start(bf16[128,1024]{1,0:T(8,128)(2,1)S(1)} %get-tuple-element.12.q_ref) | copy-start | bytes 786436
  38.5 4.5 %collective-permute-start.1 = (bf16[8,128,512]{2,1,0:T(8,128)(2,1)S(1)}, bf16[8,128,512]{2,1,0:T(8,128)(2,1)S(1)}, u32[]{:S(2)}, u32[]{:S(2)}) collective-permute-start(bf16[8,128,512]{2,1,0:T(8,128)(2,1)S(1)} %all-to-all-done.mine_ref), channel_id=1, source_target_pairs={{0,1},{1,0},{2,3},{3,2},{4,5},{5,4},{6,7},{7,6},{8,9},{9,8},{10,11... | collective-permute-start | bytes 3145736 | tf_op jit(solution)/shard_map/ppermute | solution.py:223
  40.5 2.6 %copy-start.4 = (s32[17]{0:T(128)S(1)}, s32[17]{0:T(128)}, u32[]{:S(2)}) copy-start(s32[17]{0:T(128)} %lengths_ref.3) | copy-start | bytes 208
  40.6 11.6 %copy-start.1 = (s32[1024]{0:T(1024)S(1)}, s32[1024]{0:T(1024)}, u32[]{:S(2)}) copy-start(s32[1024]{0:T(1024)} %table_ref.1) | copy-start | bytes 12292
  45.7 18.1 %collective-permute-start.2 = (bf16[144,1024]{1,0:T(8,128)(2,1)S(1)}, bf16[144,1024]{1,0:T(8,128)(2,1)S(1)}, u32[]{:S(2)}, u32[]{:S(2)}) collective-permute-start(bf16[144,1024]{1,0:T(8,128)(2,1)S(1)} %later_rows.1), channel_id=1, source_target_pairs={{0,16},{16,32},{32,48},{48,64},{64,80},{80,96},{96,112},{1,17},{17... | collective-permute-start | bytes 884744 | tf_op jit(solution)/shard_map/ppermute | solution.py:231
  53.6 10.3 %all-to-all-start.1 = ((bf16[8,2,16,256]{3,2,1,0:T(8,128)(2,1)}), bf16[8,2,16,256]{3,2,1,0:T(8,128)(2,1)S(1)}, u32[]{:S(2)}, u32[]{:S(2)}) async-start(bf16[8,2,16,256]{3,2,1,0:T(8,128)(2,1)} %pick_pages.1), calls=%async_computation.1 | async-start | bytes 262144 | tf_op jit(solution)/shard_map/all_to_all | solution.py:235
  57.9 0.9 %copy-start.3 = (bf16[128,1024]{1,0:T(8,128)(2,1)S(1)}, bf16[128,1024]{1,0:T(8,128)(2,1)}, u32[]{:S(2)}) copy-start(bf16[128,1024]{1,0:T(8,128)(2,1)} %copy-done.2) | copy-start | bytes 786436

commit v3 on v2

v3 whole, which is shorter than its diff:
```python
import math

import jax
import jax.numpy as jnp
from jax import lax
from jax.experimental import pallas as pl
from jax.experimental.pallas import tpu as pltpu
from jax.sharding import PartitionSpec as P

HD = 128
PAGE = 16
SPAN = 2
LOWEST = -1e30
STAT_ROWS = 16
FACTOR = HD**-0.5 * math.log2(math.e)


def doc_start(lengths_ref, position):
    bound = jnp.int32(0)
    start = jnp.zeros_like(position)
    for i in range(lengths_ref.shape[0]):
        bound = bound + lengths_ref[i]
        start = jnp.where(bound <= position, bound, start)
    return start


def spread_kernel(keys_ref, values_ref, out_ref, both, sems):
    width = keys_ref.shape[1]
    copies = [
        pltpu.make_async_copy(keys_ref, both.at[:, 0:width], sems.at[0]),
        pltpu.make_async_copy(values_ref, both.at[:, width : 2 * width], sems.at[1]),
    ]
    for copy in copies:
        copy.start()
    for copy in copies:
        copy.wait()
    for chip in range(out_ref.shape[0]):
        group = chip % 2 * HD
        out_ref[chip, :, 0:HD] = both[:, group : group + HD]
        out_ref[chip, :, HD : 2 * HD] = both[:, width + group : width + group + HD]


def turn_kernel(at_ref, q_ref, keep_ref, give_ref):
    group = lax.rem(lax.div(at_ref[1], 2), 2)
    rows = q_ref.shape[0]
    heads = keep_ref.shape[1] // rows
    for out_ref, one in ((keep_ref, group), (give_ref, 1 - group)):
        for h in range(heads):
            cols = pl.ds(pl.multiple_of((one * heads + h) * HD, HD), HD)
            out_ref[:, h * rows : (h + 1) * rows] = jnp.transpose(q_ref[:, cols])


def scan_keys(lengths_ref, q_refs, mine_ref, other_ref, q_bases, k_base, core, acc, top, total, kept):
    rows = mine_ref.shape[1]
    lanes = q_refs[0].shape[1]
    heads = lanes // rows
    tile = 2 * rows * SPAN
    count = mine_ref.shape[0] // SPAN
    acc[...] = jnp.zeros_like(acc)
    top[...] = jnp.full_like(top, LOWEST)
    total[...] = jnp.zeros_like(total)
    q_low = jnp.minimum(*q_bases)
    q_high = jnp.maximum(*q_bases) + rows - 1
    first_start = doc_start(lengths_ref, q_low)
    last_start = doc_start(lengths_ref, q_high)
    q_pos = [base + lax.broadcasted_iota(jnp.int32, (1, rows), 1) for base in q_bases]
    q_start = [doc_start(lengths_ref, one) for one in q_pos]
    low_tile = jnp.clip(lax.div(first_start - k_base, tile), 0, count)
    high_tile = jnp.clip(lax.div(q_high - k_base, tile) + 1, 0, count)

    def columns(at, cols):
        parts = []
        for chip in range(SPAN):
            parts += [mine_ref[at * SPAN + chip, :, cols], other_ref[at * SPAN + chip, :, cols]]
        return jnp.concatenate(parts, axis=0)

    def score(at, masked):
        keys = columns(at, slice(0, HD))
        if masked:
            row = lax.broadcasted_iota(jnp.int32, (2 * rows, rows), 0)
            k_pos = k_base + at * tile + jnp.where(row < rows, row + core * rows, row - core * rows)
            k_pos = jnp.concatenate([k_pos + chip * 2 * rows for chip in range(SPAN)], axis=0)
        for i, q_ref in enumerate(q_refs):
            where = slice(i * lanes, (i + 1) * lanes)
            scores = jnp.dot(keys, q_ref[...], preferred_element_type=jnp.float32)
            if masked:
                seen = (k_pos <= q_pos[i]) & (k_pos >= q_start[i])
                scores = jnp.where(jnp.concatenate([seen] * heads, axis=1), scores, LOWEST)
            kept[at, i] = scores
            top[:, where] = jnp.maximum(top[:, where], jnp.max(scores, axis=0, keepdims=True))

    def first_pass(at, carry):
        low = k_base + at * tile
        whole = (low + tile - 1 <= q_low) & (low >= last_start)

        @pl.when(whole)
        def _():
            score(at, False)

        @pl.when(jnp.logical_not(whole))
        def _():
            score(at, True)

        return carry

    def second_pass(at, carry):
        values = columns(at, slice(HD, 2 * HD))
        for i in range(len(q_refs)):
            where = slice(i * lanes, (i + 1) * lanes)
            peak = jnp.maximum(top[:, where], 0.1 * LOWEST) * FACTOR
            weights = jnp.exp2(kept[at, i] * FACTOR - peak)
            total[:, where] = total[:, where] + jnp.sum(weights, axis=0, keepdims=True)
            acc[:, where] = acc[:, where] + lax.dot_general(
                values, weights.astype(jnp.bfloat16), (((0,), (0,)), ((), ())), preferred_element_type=jnp.float32
            )
        return carry

    lax.fori_loop(low_tile, high_tile, first_pass, 0)
    lax.fori_loop(low_tile, high_tile, second_pass, 0)


def split_three(value):
    high = value.astype(jnp.bfloat16)
    rest = value - high.astype(jnp.float32)
    middle = rest.astype(jnp.bfloat16)
    low = (rest - middle.astype(jnp.float32)).astype(jnp.bfloat16)
    return [high, middle, low]


def bases(at_ref, rows, later):
    pb, kv, n_kv = at_ref[0], at_ref[1], at_ref[3]
    row_tokens = n_kv * rows
    chip = lax.div(kv, 2)
    mate = (chip + 1 - 2 * lax.rem(chip, 2)) * 2 + lax.rem(kv, 2)
    q_row = (pb + later) * row_tokens
    return (q_row + kv * rows, q_row + mate * rows), pb * row_tokens, lax.rem(kv, 2)


def later_kernel(at_ref, lengths_ref, q_ref, mate_ref, mine_ref, other_ref, part_ref, acc, top, total, kept):
    q_bases, k_base, core = bases(at_ref, mine_ref.shape[1], 1)
    scan_keys(lengths_ref, (q_ref, mate_ref), mine_ref, other_ref, q_bases, k_base, core, acc, top, total, kept)
    part_ref[0:HD, :] = (acc[...] / jnp.maximum(total[...], 1e-30)).astype(jnp.bfloat16)
    stats = split_three(top[...]) + split_three(total[...])
    stats.append(jnp.zeros((STAT_ROWS - len(stats), acc.shape[1]), jnp.bfloat16))
    part_ref[HD : HD + STAT_ROWS, :] = jnp.concatenate(stats, axis=0)


def own_kernel(at_ref, lengths_ref, q_ref, mate_ref, mine_ref, other_ref, acc, top, total, kept):
    q_bases, k_base, core = bases(at_ref, mine_ref.shape[1], 0)
    scan_keys(lengths_ref, (q_ref, mate_ref), mine_ref, other_ref, q_bases, k_base, core, acc, top, total, kept)


def pick_kernel(at_ref, table_ref, mine_ref, other_ref, pages_ref):
    pb, kv, n_pb, n_kv, n_head = at_ref[0], at_ref[1], at_ref[2], at_ref[3], at_ref[4]
    core = lax.rem(kv, 2)
    rows = mine_ref.shape[1]
    n_slots = pages_ref.shape[0]
    row_pages = n_kv * rows // PAGE
    slot_rows = row_pages // n_head
    per = n_slots // 8
    first_chip = lax.div(kv, 4) * 2
    for i in range(n_slots):
        head, chip, which = i // (2 * per), i // per % 2, i % per
        slot = head * (n_pb * slot_rows) + pb * slot_rows + ((first_chip + chip) * 2 + core) * per + which
        page = table_ref[slot] - pb * row_pages
        block_pages = rows // PAGE
        block = lax.div(page, block_pages)
        held = lax.div(block, 2)
        row = pl.multiple_of(lax.rem(page, block_pages) * PAGE, PAGE)
        own = lax.rem(block, 2) == core
        for half in range(2):
            cols = slice(half * HD, (half + 1) * HD)
            pages_ref[i, half] = jnp.where(
                own, mine_ref[held, pl.ds(row, PAGE), cols], other_ref[held, pl.ds(row, PAGE), cols]
            )


def join_kernel(acc_ref, top_ref, total_ref, part_ref, own_ref, mate_ref):
    part = part_ref[0:HD, :].astype(jnp.float32)
    stats = part_ref[HD : HD + STAT_ROWS, :].astype(jnp.float32)
    part_total = stats[3:4] + stats[4:5] + stats[5:6]
    part_top = jnp.where(part_total > 0.0, stats[0:1] + stats[1:2] + stats[2:3], LOWEST)
    top = jnp.maximum(top_ref[...], part_top)
    own = jnp.exp2((top_ref[...] - top) * FACTOR)
    weight = jnp.where(part_total > 0.0, jnp.exp2((part_top - top) * FACTOR) * part_total, 0.0)
    inverse = 1.0 / (total_ref[...] * own + weight)
    own = own * inverse
    weight = weight * inverse
    rows = own_ref.shape[0]
    heads = own_ref.shape[1] // HD
    for i, out_ref in ((1, mate_ref), (0, own_ref)):
        for h in range(heads):
            at = slice((i * heads + h) * rows, (i * heads + h + 1) * rows)
            mixed = acc_ref[:, at] * own[:, at] + part[:, at] * weight[:, at]
            out_ref[:, h * HD : (h + 1) * HD] = jnp.transpose(mixed).astype(jnp.bfloat16)


def place_kernel(at_ref, own_ref, mate_ref, pages_ref, out_ref, pool_ref):
    group = lax.rem(lax.div(at_ref[1], 2), 2)
    width = own_ref.shape[1]
    out_ref[:, pl.ds(pl.multiple_of(group * width, HD), width)] = own_ref[...]
    out_ref[:, pl.ds(pl.multiple_of((1 - group) * width, HD), width)] = mate_ref[...]
    slots = pool_ref.shape[0]
    for i in range(pages_ref.shape[0] // slots):
        pool_ref[:, :, :, i * HD : (i + 1) * HD] = pages_ref[i * slots : (i + 1) * slots]


SMEM = pl.BlockSpec(memory_space=pltpu.SMEM)
VMEM = pl.BlockSpec(memory_space=pltpu.VMEM)
ANY = pl.BlockSpec(memory_space=pl.ANY)
MIB = 1 << 20


def call(kernel, out_shape, in_specs, name, flops, scratch=(), vmem=40 * MIB):
    several = isinstance(out_shape, tuple)
    return pl.pallas_call(
        kernel,
        out_shape=out_shape,
        in_specs=in_specs,
        out_specs=(VMEM,) * len(out_shape) if several else VMEM,
        scratch_shapes=scratch,
        compiler_params=pltpu.CompilerParams(vmem_limit_bytes=vmem),
        cost_estimate=pl.CostEstimate(flops=flops, bytes_accessed=3 << 20, transcendentals=0),
        name=name,
    )


def body(queries, keys, values, doc_lengths, page_table):
    rows = queries.shape[0]
    n_head = lax.axis_size("head")
    n_pb = lax.axis_size("pb")
    n_kv = lax.axis_size("kv")
    chips = n_kv // 2
    columns = queries.shape[1]
    lanes = columns // HD * rows // 2
    n_slots = rows // PAGE * 2
    shape = jax.ShapeDtypeStruct
    at = jnp.stack([lax.axis_index("pb"), lax.axis_index("kv"), n_pb, n_kv, n_head]).astype(jnp.int32)
    to_mate = [(i, i ^ 2) for i in range(n_kv)]

    sent = call(
        spread_kernel, shape((chips, rows, 2 * HD), jnp.bfloat16), [ANY] * 2, "spread_keys", 1 << 10,
        [pltpu.VMEM((rows, 2 * keys.shape[1]), jnp.bfloat16), pltpu.SemaphoreType.DMA((2,))], 60 * MIB,
    )(keys, values)
    ring = [[2 * i + core for i in range(chips)] for core in range(2)]
    mine = lax.all_to_all(sent, "kv", 0, 0, tiled=True, axis_index_groups=ring)
    half = shape((HD, lanes), jnp.bfloat16)
    keep, give = call(turn_kernel, (half, half), [SMEM, VMEM], "turn_queries", 1 << 20)(at, queries)
    mate = lax.ppermute(give, "kv", to_mate)
    later = lax.ppermute(keep, "pb", [(i + 1, i) for i in range(n_pb - 1)])
    steps = [((z + 1) * n_kv + (i ^ 2), z * n_kv + i) for z in range(n_pb - 1) for i in range(n_kv)]
    later_mate = lax.ppermute(give, ("pb", "kv"), steps)
    mine, mate, later, later_mate = lax.optimization_barrier((mine, mate, later, later_mate))
    other = lax.ppermute(mine, "kv", [(i, i ^ 1) for i in range(n_kv)])

    flops = 4 * columns * rows * n_kv * rows
    state = [(HD, 2 * lanes), (1, 2 * lanes), (1, 2 * lanes)]
    kept = pltpu.VMEM((chips // SPAN, 2, 2 * rows * SPAN, lanes), jnp.float32)
    scanned = [SMEM, SMEM, VMEM, VMEM, VMEM, VMEM]
    part = call(
        later_kernel, shape((HD + STAT_ROWS, 2 * lanes), jnp.bfloat16), scanned, "later_rows", flops,
        [pltpu.VMEM(one, jnp.float32) for one in state] + [kept],
    )(at, doc_lengths, later, later_mate, mine, other)
    back = lax.ppermute(part, "pb", [(i, i + 1) for i in range(n_pb - 1)])
    pages = call(
        pick_kernel, shape((n_slots, 2, PAGE, HD), jnp.bfloat16), [SMEM, SMEM, VMEM, VMEM], "pick_pages", 1 << 20
    )(at, page_table, mine, other)
    sharing = [
        [head * n_kv + (2 * pair + chip) * 2 + core for head in range(n_head) for chip in range(2)]
        for pair in range(chips // 2)
        for core in range(2)
    ]
    arrived = lax.all_to_all(pages, ("head", "kv"), 0, 0, tiled=True, axis_index_groups=sharing)
    own = call(
        own_kernel, tuple(shape(one, jnp.float32) for one in state), scanned, "own_row", flops, [kept]
    )(at, doc_lengths, keep, mate, mine, other)
    out = shape((rows, columns // 2), jnp.bfloat16)
    own_out, mate_out = call(join_kernel, (out, out), [VMEM] * 4, "join_rows", 1 << 20)(*own, back)
    mate_out = lax.ppermute(mate_out, "kv", to_mate)
    pool = shape((n_slots // (2 * n_head), 2, PAGE, 2 * n_head * HD), jnp.bfloat16)
    return call(
        place_kernel, (shape((rows, columns), jnp.bfloat16), pool), [SMEM] + [VMEM] * 3, "place", 1 << 10
    )(at, own_out, mate_out, arrived)


def solution(mesh):
    in_specs = (P(("pb", "kv"), "head"), P(("pb", "kv"), "head"), P(("pb", "kv"), "head"), P(), P())
    out_specs = (P(("pb", "kv"), "head"), P(("head", "pb", "kv"), None, None, None))
    return jax.shard_map(body, mesh=mesh, in_specs=in_specs, out_specs=out_specs, check_vma=False)
```

time: 65.1 us -> 60.5 us (0.929)
  the two profiles are of different devices: /device:TPU:192 before, /device:TPU:184 now
where the time goes in v3:
time: 60.5 us; the launch traced here: 60 us
  starting transfers between devices  30.3 us (50%)
  waiting for transfers between devices  18.3 us (30%)
  Pallas kernels  10.6 us (18%)
  between operations  0.77 us (1%)
    ppermute x1, waiting for transfers between devices, body(): mate = lax.ppermute(give, 'kv', to_mate)  7.91 us
    all_to_all x1, starting transfers between devices, body(): mine = lax.all_to_all(sent, 'kv', 0, 0, tiled=True, axis_index_groups=ring)  7.01 us
    all_to_all x1, starting transfers between devices, body(): lax.all_to_all(pages, ('head', 'kv'), 0, 0, tiled=True, axis_index_groups...  5.76 us
    ppermute x1, starting transfers between devices, body(): back = lax.ppermute(part, 'pb', [(i, i + 1) for i in range(n_pb - 1)])  5.49 us
    ppermute x1, waiting for transfers between devices, body(): mate_out = lax.ppermute(mate_out, 'kv', to_mate)  4.92 us
    pallas_call x1, Pallas kernels, body(): call(own_kernel, tuple((shape(one, jnp.float32) for one in state)), scann...  4.52 us
    ppermute x1, waiting for transfers between devices, body(): later_mate = lax.ppermute(give, ('pb', 'kv'), steps)  3.57 us
    ppermute x1, starting transfers between devices, body(): mate = lax.ppermute(give, 'kv', to_mate)  3.37 us
  transfers between devices with their start and end apart: 8, of which 4 were waited for; matrix products, arithmetic and copies ran while one was open for 0% of the time, Pallas kernels for 11%

profile of v3, /device:TPU:184, one launch (start us, length us, event | category | flops | bytes accessed | tf_op | source)
XLA Modules:
  0.0 60.0 jit_solution(1099476467266343988)
XLA Ops:
  0.6 1.7 %spread_keys.1 = bf16[8,128,256]{2,1,0:T(8,128)(2,1)} custom-call(bf16[128,256]{1,0:T(8,128)(2,1)} %keys_ref.1, bf16[128,256]{1,0:T(8,128)(2,1)} %values_ref.1), custom_call_target="tpu_custom_call" | custom-call | flops 1024 | bytes 3145728 | tf_op jit(solution)/shard_map/spread_keys/pallas_call | solution.py:241
  2.4 0.0 copy-start
  2.4 7.0 %all-to-all-start = ((bf16[8,128,256]{2,1,0:T(8,128)(2,1)}), bf16[8,128,256]{2,1,0:T(8,128)(2,1)S(1)}, u32[]{:S(2)}, u32[]{:S(2)}) async-start(bf16[8,128,256]{2,1,0:T(8,128)(2,1)} %spread_keys.1), calls=%async_computation | async-start | bytes 1048576 | tf_op jit(solution)/shard_map/all_to_all | solution.py:246
  9.4 0.1 stack.11.at_ref
  9.5 0.0 copy-done
  9.5 0.7 %turn_queries.1 = (bf16[128,512]{1,0:T(8,128)(2,1)S(1)}, bf16[128,512]{1,0:T(8,128)(2,1)S(1)}) custom-call(s32[5]{0:T(128)S(1)} %stack.11.at_ref, bf16[128,1024]{1,0:T(8,128)(2,1)S(1)} %copy-done), custom_call_target="tpu_custom_call" | custom-call | flops 1048576 | bytes 3145728 | tf_op jit(solution)/shard_map/turn_queries/pallas_call | solution.py:248
  10.2 0.0 copy-start.2
  10.2 3.4 %collective-permute-start = (bf16[128,512]{1,0:T(8,128)(2,1)S(1)}, bf16[128,512]{1,0:T(8,128)(2,1)S(1)}, u32[]{:S(2)}, u32[]{:S(2)}) collective-permute-start(bf16[128,512]{1,0:T(8,128)(2,1)S(1)} %get-tuple-element.14), channel_id=1, source_target_pairs={{0,2},{1,3},{2,0},{3,1},{4,6},{5,7},{6,4},{7,5},{8,10},{9,11},{10,... | collective-permute-start | bytes 393224 | tf_op jit(solution)/shard_map/ppermute | solution.py:249
  13.6 0.0 copy-start.1
  13.6 1.9 %collective-permute-start.1 = (bf16[128,512]{1,0:T(8,128)(2,1)S(1)}, bf16[128,512]{1,0:T(8,128)(2,1)S(1)}, u32[]{:S(2)}, u32[]{:S(2)}) collective-permute-start(bf16[128,512]{1,0:T(8,128)(2,1)S(1)} %get-tuple-element.13.q_ref), channel_id=1, source_target_pairs={{16,0},{32,16},{48,32},{64,48},{80,64},{96,80},{112,96},{17,1},{33... | collective-permute-start | bytes 393224 | tf_op jit(solution)/shard_map/ppermute | solution.py:250
  15.5 2.9 %collective-permute-start.2 = (bf16[128,512]{1,0:T(8,128)(2,1)S(1)}, bf16[128,512]{1,0:T(8,128)(2,1)S(1)}, u32[]{:S(2)}, u32[]{:S(2)}) collective-permute-start(bf16[128,512]{1,0:T(8,128)(2,1)S(1)} %get-tuple-element.14), channel_id=1, source_target_pairs={{18,0},{19,1},{16,2},{17,3},{22,4},{23,5},{20,6},{21,7},{26,8},{27... | collective-permute-start | bytes 393224 | tf_op jit(solution)/shard_map/ppermute | solution.py:252
  18.4 7.9 %collective-permute-done.mate_ref = bf16[128,512]{1,0:T(8,128)(2,1)S(1)} collective-permute-done((bf16[128,512]{1,0:T(8,128)(2,1)S(1)}, bf16[128,512]{1,0:T(8,128)(2,1)S(1)}, u32[]{:S(2)}, u32[]{:S(2)}) %collective-permute-start) | collective-permute-done | bytes 131104 | tf_op jit(solution)/shard_map/ppermute | solution.py:249
  26.3 0.0 collective-permute-done.1.q_ref
  26.3 3.6 %collective-permute-done.2.mate_ref = bf16[128,512]{1,0:T(8,128)(2,1)S(1)} collective-permute-done((bf16[128,512]{1,0:T(8,128)(2,1)S(1)}, bf16[128,512]{1,0:T(8,128)(2,1)S(1)}, u32[]{:S(2)}, u32[]{:S(2)}) %collective-permute-start.2) | collective-permute-done | bytes 131104 | tf_op jit(solution)/shard_map/ppermute | solution.py:252
  29.9 0.0 all-to-all-done.mine_ref
  29.9 1.9 %collective-permute-start.3 = (bf16[8,128,256]{2,1,0:T(8,128)(2,1)S(1)}, bf16[8,128,256]{2,1,0:T(8,128)(2,1)S(1)}, u32[]{:S(2)}, u32[]{:S(2)}) collective-permute-start(bf16[8,128,256]{2,1,0:T(8,128)(2,1)S(1)} %all-to-all-done.mine_ref), channel_id=1, source_target_pairs={{0,1},{1,0},{2,3},{3,2},{4,5},{5,4},{6,7},{7,6},{8,9},{9,8},{10,11... | collective-permute-start | bytes 1572872 | tf_op jit(solution)/shard_map/ppermute | solution.py:254
  31.8 1.9 %collective-permute-done.3.other_ref = bf16[8,128,256]{2,1,0:T(8,128)(2,1)S(1)} collective-permute-done((bf16[8,128,256]{2,1,0:T(8,128)(2,1)S(1)}, bf16[8,128,256]{2,1,0:T(8,128)(2,1)S(1)}, u32[]{:S(2)}, u32[]{:S(2)}) %collective-permute-start.3) | collective-permute-done | bytes 524320 | tf_op jit(solution)/shard_map/ppermute | solution.py:254
  33.7 0.0 copy-done.2
  33.7 0.7 %later_rows.1 = bf16[144,1024]{1,0:T(8,128)(2,1)S(1)} custom-call(s32[5]{0:T(128)S(1)} %stack.11.at_ref, s32[17]{0:T(128)S(1)} %copy-done.2, bf16[128,512]{1,0:T(8,128)(2,1)S(1)} %collective-permute-done.1.q_ref, bf16[128,512]{1,0:T(8,128)(2,1)S(1)} %collective-permute-done.2.mate_ref, bf16[8,128,256]{2,1,0:T(8,128)(2,1)S(1)} %all-to-all-done.mine_ref, ...), custom_call_target="tpu_custom_call" | custom-call | flops 1073741824 | bytes 3145728 | tf_op jit(solution)/shard_map/later_rows/pallas_call | solution.py:260
  34.4 5.5 %collective-permute-start.4 = (bf16[144,1024]{1,0:T(8,128)(2,1)S(1)}, bf16[144,1024]{1,0:T(8,128)(2,1)S(1)}, u32[]{:S(2)}, u32[]{:S(2)}) collective-permute-start(bf16[144,1024]{1,0:T(8,128)(2,1)S(1)} %later_rows.1), channel_id=1, source_target_pairs={{0,16},{16,32},{32,48},{48,64},{64,80},{80,96},{96,112},{1,17},{17... | collective-permute-start | bytes 884744 | tf_op jit(solution)/shard_map/ppermute | solution.py:264
  39.9 0.0 copy-done.1
  39.9 1.4 %pick_pages.1 = bf16[16,2,16,128]{3,2,1,0:T(8,128)(2,1)} custom-call(s32[5]{0:T(128)S(1)} %stack.11.at_ref, s32[1024]{0:T(1024)S(1)} %copy-done.1, bf16[8,128,256]{2,1,0:T(8,128)(2,1)S(1)} %all-to-all-done.mine_ref, bf16[8,128,256]{2,1,0:T(8,128)(2,1)S(1)} %collective-permute-done.3.other_ref), custom_call_target="tpu_custom_call" | custom-call | flops 1048576 | bytes 3145728 | tf_op jit(solution)/shard_map/pick_pages/pallas_call | solution.py:265
  41.3 5.8 %all-to-all-start.1 = ((bf16[16,2,16,128]{3,2,1,0:T(8,128)(2,1)}), bf16[16,2,16,128]{3,2,1,0:T(8,128)(2,1)S(1)}, u32[]{:S(2)}, u32[]{:S(2)}) async-start(bf16[16,2,16,128]{3,2,1,0:T(8,128)(2,1)} %pick_pages.1), calls=%async_computation.1 | async-start | bytes 262144 | tf_op jit(solution)/shard_map/all_to_all | solution.py:273
  47.1 4.5 %own_row.1 = (f32[128,1024]{1,0:T(8,128)S(1)}, f32[1,1024]{1,0:T(1,128)S(1)}, f32[1,1024]{1,0:T(1,128)S(1)}) custom-call(s32[5]{0:T(128)S(1)} %stack.11.at_ref, s32[17]{0:T(128)S(1)} %copy-done.2, bf16[128,512]{1,0:T(8,128)(2,1)S(1)} %get-tuple-element.13.q_ref, bf16[128,512]{1,0:T(8,128)(2,1)S(1)} %collective-permute-done.mate_ref, ...), custom_call_target="tpu_custom_call" | custom-call | flops 1073741824 | bytes 3145728 | tf_op jit(solution)/shard_map/own_row/pallas_call | solution.py:274
  51.6 0.0 collective-permute-done.4.part_ref
  51.6 0.2 join_rows.1
  51.8 1.9 %collective-permute-start.5 = (bf16[128,512]{1,0:T(8,128)(2,1)S(1)}, bf16[128,512]{1,0:T(8,128)(2,1)S(1)}, u32[]{:S(2)}, u32[]{:S(2)}) collective-permute-start(bf16[128,512]{1,0:T(8,128)(2,1)S(1)} %get-tuple-element.23), channel_id=1, source_target_pairs={{0,2},{1,3},{2,0},{3,1},{4,6},{5,7},{6,4},{7,5},{8,10},{9,11},{10,... | collective-permute-start | bytes 393224 | tf_op jit(solution)/shard_map/ppermute | solution.py:279
  53.8 0.0 all-to-all-done.1.pages_ref
  53.8 4.9 %collective-permute-done.5.mate_ref = bf16[128,512]{1,0:T(8,128)(2,1)S(1)} collective-permute-done((bf16[128,512]{1,0:T(8,128)(2,1)S(1)}, bf16[128,512]{1,0:T(8,128)(2,1)S(1)}, u32[]{:S(2)}, u32[]{:S(2)}) %collective-permute-start.5) | collective-permute-done | bytes 131104 | tf_op jit(solution)/shard_map/ppermute | solution.py:279
  58.7 1.3 %place.1 = (bf16[128,1024]{1,0:T(8,128)(2,1)}, bf16[2,2,16,1024]{3,2,1,0:T(8,128)(2,1)}) custom-call(s32[5]{0:T(128)S(1)} %stack.11.at_ref, bf16[128,512]{1,0:T(8,128)(2,1)S(1)} %get-tuple-element.22.own_ref, bf16[128,512]{1,0:T(8,128)(2,1)S(1)} %collective-permute-done.5.mate_ref, bf16[16,2,16,128]{3,2,1,0:T(8,128)(2,1)S(1)} %all-to-all-done.1.pages_ref), custom_call_target="tpu_custom_call" | custom-call | flops 1024 | bytes 3145728 | tf_op jit(solution)/shard_map/place/pallas_call | solution.py:281
Async XLA Ops:
  2.4 7.1 %copy-start = (bf16[128,1024]{1,0:T(8,128)(2,1)S(1)}, bf16[128,1024]{1,0:T(8,128)(2,1)}, u32[]{:S(2)}) copy-start(bf16[128,1024]{1,0:T(8,128)(2,1)} %q_ref.1) | copy-start | bytes 786436
  2.4 27.5 %all-to-all-start = ((bf16[8,128,256]{2,1,0:T(8,128)(2,1)}), bf16[8,128,256]{2,1,0:T(8,128)(2,1)S(1)}, u32[]{:S(2)}, u32[]{:S(2)}) async-start(bf16[8,128,256]{2,1,0:T(8,128)(2,1)} %spread_keys.1), calls=%async_computation | async-start | bytes 1048576 | tf_op jit(solution)/shard_map/all_to_all | solution.py:246
  10.2 23.5 %copy-start.2 = (s32[17]{0:T(128)S(1)}, s32[17]{0:T(128)}, u32[]{:S(2)}) copy-start(s32[17]{0:T(128)} %lengths_ref.3) | copy-start | bytes 208
  10.2 16.1 %collective-permute-start = (bf16[128,512]{1,0:T(8,128)(2,1)S(1)}, bf16[128,512]{1,0:T(8,128)(2,1)S(1)}, u32[]{:S(2)}, u32[]{:S(2)}) collective-permute-start(bf16[128,512]{1,0:T(8,128)(2,1)S(1)} %get-tuple-element.14), channel_id=1, source_target_pairs={{0,2},{1,3},{2,0},{3,1},{4,6},{5,7},{6,4},{7,5},{8,10},{9,11},{10,... | collective-permute-start | bytes 393224 | tf_op jit(solution)/shard_map/ppermute | solution.py:249
  13.6 26.3 %copy-start.1 = (s32[1024]{0:T(1024)S(1)}, s32[1024]{0:T(1024)}, u32[]{:S(2)}) copy-start(s32[1024]{0:T(1024)} %table_ref.1) | copy-start | bytes 12292
  13.6 12.8 %collective-permute-start.1 = (bf16[128,512]{1,0:T(8,128)(2,1)S(1)}, bf16[128,512]{1,0:T(8,128)(2,1)S(1)}, u32[]{:S(2)}, u32[]{:S(2)}) collective-permute-start(bf16[128,512]{1,0:T(8,128)(2,1)S(1)} %get-tuple-element.13.q_ref), channel_id=1, source_target_pairs={{16,0},{32,16},{48,32},{64,48},{80,64},{96,80},{112,96},{17,1},{33... | collective-permute-start | bytes 393224 | tf_op jit(solution)/shard_map/ppermute | solution.py:250
  15.5 14.4 %collective-permute-start.2 = (bf16[128,512]{1,0:T(8,128)(2,1)S(1)}, bf16[128,512]{1,0:T(8,128)(2,1)S(1)}, u32[]{:S(2)}, u32[]{:S(2)}) collective-permute-start(bf16[128,512]{1,0:T(8,128)(2,1)S(1)} %get-tuple-element.14), channel_id=1, source_target_pairs={{18,0},{19,1},{16,2},{17,3},{22,4},{23,5},{20,6},{21,7},{26,8},{27... | collective-permute-start | bytes 393224 | tf_op jit(solution)/shard_map/ppermute | solution.py:252
  29.9 3.8 %collective-permute-start.3 = (bf16[8,128,256]{2,1,0:T(8,128)(2,1)S(1)}, bf16[8,128,256]{2,1,0:T(8,128)(2,1)S(1)}, u32[]{:S(2)}, u32[]{:S(2)}) collective-permute-start(bf16[8,128,256]{2,1,0:T(8,128)(2,1)S(1)} %all-to-all-done.mine_ref), channel_id=1, source_target_pairs={{0,1},{1,0},{2,3},{3,2},{4,5},{5,4},{6,7},{7,6},{8,9},{9,8},{10,11... | collective-permute-start | bytes 1572872 | tf_op jit(solution)/shard_map/ppermute | solution.py:254
  34.4 17.2 %collective-permute-start.4 = (bf16[144,1024]{1,0:T(8,128)(2,1)S(1)}, bf16[144,1024]{1,0:T(8,128)(2,1)S(1)}, u32[]{:S(2)}, u32[]{:S(2)}) collective-permute-start(bf16[144,1024]{1,0:T(8,128)(2,1)S(1)} %later_rows.1), channel_id=1, source_target_pairs={{0,16},{16,32},{32,48},{48,64},{64,80},{80,96},{96,112},{1,17},{17... | collective-permute-start | bytes 884744 | tf_op jit(solution)/shard_map/ppermute | solution.py:264
  41.3 12.4 %all-to-all-start.1 = ((bf16[16,2,16,128]{3,2,1,0:T(8,128)(2,1)}), bf16[16,2,16,128]{3,2,1,0:T(8,128)(2,1)S(1)}, u32[]{:S(2)}, u32[]{:S(2)}) async-start(bf16[16,2,16,128]{3,2,1,0:T(8,128)(2,1)} %pick_pages.1), calls=%async_computation.1 | async-start | bytes 262144 | tf_op jit(solution)/shard_map/all_to_all | solution.py:273
  51.8 6.9 %collective-permute-start.5 = (bf16[128,512]{1,0:T(8,128)(2,1)S(1)}, bf16[128,512]{1,0:T(8,128)(2,1)S(1)}, u32[]{:S(2)}, u32[]{:S(2)}) collective-permute-start(bf16[128,512]{1,0:T(8,128)(2,1)S(1)} %get-tuple-element.23), channel_id=1, source_target_pairs={{0,2},{1,3},{2,0},{3,1},{4,6},{5,7},{6,4},{7,5},{8,10},{9,11},{10,... | collective-permute-start | bytes 393224 | tf_op jit(solution)/shard_map/ppermute | solution.py:279

commit v4 on v3

v4 whole, which is shorter than its diff:
```python
import functools
import math

import jax
import jax.numpy as jnp
from jax import lax
from jax.experimental import pallas as pl
from jax.experimental.pallas import tpu as pltpu
from jax.sharding import PartitionSpec as P

HD = 128
PAGE = 16
SPAN = 2
LOWEST = -1e30
STAT_ROWS = 16
LONG = 10**11
FACTOR = HD**-0.5 * math.log2(math.e)


def doc_start(lengths_ref, position):
    bound = jnp.int32(0)
    start = jnp.zeros_like(position)
    for i in range(lengths_ref.shape[0]):
        bound = bound + lengths_ref[i]
        start = jnp.where(bound <= position, bound, start)
    return start


def spread_kernel(keys_ref, values_ref, out_ref, keys, values, both, sems):
    loads = [
        pltpu.make_async_copy(keys_ref, keys, sems.at[0]),
        pltpu.make_async_copy(values_ref, values, sems.at[1]),
    ]
    for copy in loads:
        copy.start()
    for copy in loads:
        copy.wait()
    copies = []
    for group in range(2):
        cols = slice(group * HD, (group + 1) * HD)
        both[group, :, 0:HD] = keys[:, cols]
        both[group, :, HD : 2 * HD] = values[:, cols]
        for chip in range(group, out_ref.shape[0], 2):
            copies.append(pltpu.make_async_copy(both.at[group], out_ref.at[chip], sems.at[2 + chip]))
            copies[-1].start()
    for copy in copies:
        copy.wait()


def turn_kernel(q_ref, keep_ref, give_ref):
    group = lax.rem(lax.div(lax.axis_index("kv"), 2), 2)
    rows = q_ref.shape[0]
    heads = keep_ref.shape[1] // rows
    for out_ref, one in ((keep_ref, group), (give_ref, 1 - group)):
        for h in range(heads):
            cols = pl.ds(pl.multiple_of((one * heads + h) * HD, HD), HD)
            out_ref[:, h * rows : (h + 1) * rows] = jnp.transpose(q_ref[:, cols])


def scan_keys(lengths_ref, q_refs, mine_ref, other_ref, q_bases, k_base, core, acc, top, total, kept, SPAN=SPAN):
    rows = mine_ref.shape[1]
    lanes = q_refs[0].shape[1]
    heads = lanes // rows
    tile = 2 * rows * SPAN
    count = mine_ref.shape[0] // SPAN
    acc[...] = jnp.zeros_like(acc)
    top[...] = jnp.full_like(top, LOWEST)
    total[...] = jnp.zeros_like(total)
    q_low = functools.reduce(jnp.minimum, q_bases)
    q_high = functools.reduce(jnp.maximum, q_bases) + rows - 1
    first_start = doc_start(lengths_ref, q_low)
    last_start = doc_start(lengths_ref, q_high)
    q_pos = [base + lax.broadcasted_iota(jnp.int32, (1, rows), 1) for base in q_bases]
    q_start = [doc_start(lengths_ref, one) for one in q_pos]
    low_tile = jnp.clip(lax.div(first_start - k_base, tile), 0, count)
    high_tile = jnp.clip(lax.div(q_high - k_base, tile) + 1, 0, count)

    def columns(at, cols):
        parts = []
        for chip in range(SPAN):
            parts += [mine_ref[at * SPAN + chip, :, cols], other_ref[at * SPAN + chip, :, cols]]
        return jnp.concatenate(parts, axis=0)

    def score(at, masked):
        keys = columns(at, slice(0, HD))
        if masked:
            row = lax.broadcasted_iota(jnp.int32, (2 * rows, rows), 0)
            k_pos = k_base + at * tile + jnp.where(row < rows, row + core * rows, row - core * rows)
            k_pos = jnp.concatenate([k_pos + chip * 2 * rows for chip in range(SPAN)], axis=0)
        for i, q_ref in enumerate(q_refs):
            where = slice(i * lanes, (i + 1) * lanes)
            scores = jnp.dot(keys, q_ref[...], preferred_element_type=jnp.float32)
            if masked:
                seen = (k_pos <= q_pos[i]) & (k_pos >= q_start[i])
                scores = jnp.where(jnp.concatenate([seen] * heads, axis=1), scores, LOWEST)
            kept[at, i] = scores
            top[:, where] = jnp.maximum(top[:, where], jnp.max(scores, axis=0, keepdims=True))

    def first_pass(at, carry):
        low = k_base + at * tile
        whole = (low + tile - 1 <= q_low) & (low >= last_start)

        @pl.when(whole)
        def _():
            score(at, False)

        @pl.when(jnp.logical_not(whole))
        def _():
            score(at, True)

        return carry

    def second_pass(at, carry):
        values = columns(at, slice(HD, 2 * HD))
        for i in range(len(q_refs)):
            where = slice(i * lanes, (i + 1) * lanes)
            peak = jnp.maximum(top[:, where], 0.1 * LOWEST) * FACTOR
            weights = jnp.exp2(kept[at, i] * FACTOR - peak)
            total[:, where] = total[:, where] + jnp.sum(weights, axis=0, keepdims=True)
            acc[:, where] = acc[:, where] + lax.dot_general(
                values, weights.astype(jnp.bfloat16), (((0,), (0,)), ((), ())), preferred_element_type=jnp.float32
            )
        return carry

    lax.fori_loop(low_tile, high_tile, first_pass, 0)
    lax.fori_loop(low_tile, high_tile, second_pass, 0)


def split_three(value):
    high = value.astype(jnp.bfloat16)
    rest = value - high.astype(jnp.float32)
    middle = rest.astype(jnp.bfloat16)
    low = (rest - middle.astype(jnp.float32)).astype(jnp.bfloat16)
    return [high, middle, low]


def bases(rows, later):
    pb, kv = lax.axis_index("pb"), lax.axis_index("kv")
    row_tokens = lax.axis_size("kv") * rows
    chip = lax.div(kv, 2)
    mate = (chip + 1 - 2 * lax.rem(chip, 2)) * 2 + lax.rem(kv, 2)
    q_row = (pb + later) * row_tokens
    return (q_row + kv * rows, q_row + mate * rows), pb * row_tokens, lax.rem(kv, 2)


def pick_pages(table_ref, mine_ref, other_ref, pages_ref):
    pb, kv = lax.axis_index("pb"), lax.axis_index("kv")
    n_head, n_pb, n_kv = lax.axis_size("head"), lax.axis_size("pb"), lax.axis_size("kv")
    core = lax.rem(kv, 2)
    rows = mine_ref.shape[1]
    n_slots = pages_ref.shape[0]
    row_pages = n_kv * rows // PAGE
    slot_rows = row_pages // n_head
    per = n_slots // 8
    first_chip = lax.div(kv, 4) * 2
    for i in range(n_slots):
        head, chip, which = i // (2 * per), i // per % 2, i % per
        slot = head * (n_pb * slot_rows) + pb * slot_rows + ((first_chip + chip) * 2 + core) * per + which
        page = table_ref[slot] - pb * row_pages
        block_pages = rows // PAGE
        block = lax.div(page, block_pages)
        held = lax.div(block, 2)
        row = pl.multiple_of(lax.rem(page, block_pages) * PAGE, PAGE)
        own = lax.rem(block, 2) == core
        for half in range(2):
            cols = slice(half * HD, (half + 1) * HD)
            pages_ref[i, half] = jnp.where(
                own, mine_ref[held, pl.ds(row, PAGE), cols], other_ref[held, pl.ds(row, PAGE), cols]
            )


def later_kernel(
    lengths_ref, table_ref, q_ref, mate_ref, mine_ref, other_ref, part_ref, pages_ref, acc, top, total, kept
):
    pick_pages(table_ref, mine_ref, other_ref, pages_ref)
    q_bases, k_base, core = bases(mine_ref.shape[1], 1)
    scan_keys(lengths_ref, (q_ref, mate_ref), mine_ref, other_ref, q_bases, k_base, core, acc, top, total, kept)
    part_ref[0:HD, :] = (acc[...] / jnp.maximum(total[...], 1e-30)).astype(jnp.bfloat16)
    stats = split_three(top[...]) + split_three(total[...])
    stats.append(jnp.zeros((STAT_ROWS - len(stats), acc.shape[1]), jnp.bfloat16))
    part_ref[HD : HD + STAT_ROWS, :] = jnp.concatenate(stats, axis=0)


def join(acc, top, total, part_ref, which, out_ref):
    rows = out_ref.shape[0]
    lanes = acc.shape[1]
    at = slice(which * lanes, (which + 1) * lanes)
    part = part_ref[0:HD, at].astype(jnp.float32)
    stats = part_ref[HD : HD + STAT_ROWS, at].astype(jnp.float32)
    part_total = stats[3:4] + stats[4:5] + stats[5:6]
    part_top = jnp.where(part_total > 0.0, stats[0:1] + stats[1:2] + stats[2:3], LOWEST)
    peak = jnp.maximum(top[...], part_top)
    own = jnp.exp2((top[...] - peak) * FACTOR)
    weight = jnp.where(part_total > 0.0, jnp.exp2((part_top - peak) * FACTOR) * part_total, 0.0)
    inverse = 1.0 / (total[...] * own + weight)
    mixed = acc[...] * (own * inverse) + part * (weight * inverse)
    for h in range(lanes // rows):
        out_ref[:, h * HD : (h + 1) * HD] = jnp.transpose(mixed[:, h * rows : (h + 1) * rows]).astype(jnp.bfloat16)


def mate_kernel(lengths_ref, q_ref, mine_ref, other_ref, acc, top, total, kept):
    q_bases, k_base, core = bases(mine_ref.shape[1], 0)
    scan_keys(lengths_ref, (q_ref,), mine_ref, other_ref, q_bases[1:], k_base, core, acc, top, total, kept)


def mate_join_kernel(acc, top, total, part_ref, out_ref):
    join(acc, top, total, part_ref, 1, out_ref)


def own_kernel(lengths_ref, q_ref, mine_ref, other_ref, part_ref, out_ref, acc, top, total, kept):
    q_bases, k_base, core = bases(mine_ref.shape[1], 0)
    scan_keys(lengths_ref, (q_ref,), mine_ref, other_ref, q_bases[:1], k_base, core, acc, top, total, kept)
    join(acc, top, total, part_ref, 0, out_ref)


def place_kernel(own_ref, mate_ref, pages_ref, out_ref, pool_ref):
    group = lax.rem(lax.div(lax.axis_index("kv"), 2), 2)
    width = own_ref.shape[1]
    out_ref[:, pl.ds(pl.multiple_of(group * width, HD), width)] = own_ref[...]
    out_ref[:, pl.ds(pl.multiple_of((1 - group) * width, HD), width)] = mate_ref[...]
    slots = pool_ref.shape[0]
    for i in range(pages_ref.shape[0] // slots):
        pool_ref[:, :, :, i * HD : (i + 1) * HD] = pages_ref[i * slots : (i + 1) * slots]


SMEM = pl.BlockSpec(memory_space=pltpu.SMEM)
VMEM = pl.BlockSpec(memory_space=pltpu.VMEM)
ANY = pl.BlockSpec(memory_space=pl.ANY)
MIB = 1 << 20


def call(kernel, out_shape, in_specs, name, flops, scratch=(), vmem=40 * MIB, out=None):
    several = isinstance(out_shape, tuple)
    return pl.pallas_call(
        kernel,
        out_shape=out_shape,
        in_specs=in_specs,
        out_specs=out or ((VMEM,) * len(out_shape) if several else VMEM),
        scratch_shapes=scratch,
        compiler_params=pltpu.CompilerParams(vmem_limit_bytes=vmem),
        cost_estimate=pl.CostEstimate(flops=flops, bytes_accessed=3 << 20, transcendentals=0),
        name=name,
    )


def body(queries, keys, values, doc_lengths, page_table):
    rows = queries.shape[0]
    n_head = lax.axis_size("head")
    n_pb = lax.axis_size("pb")
    n_kv = lax.axis_size("kv")
    chips = n_kv // 2
    columns = queries.shape[1]
    lanes = columns // HD * rows // 2
    n_slots = rows // PAGE * 2
    shape = jax.ShapeDtypeStruct
    to_mate = [(i, i ^ 2) for i in range(n_kv)]

    local = [pltpu.VMEM(keys.shape, jnp.bfloat16)] * 2 + [pltpu.VMEM((2, rows, 2 * HD), jnp.bfloat16)]
    sent = call(
        spread_kernel, shape((chips, rows, 2 * HD), jnp.bfloat16), [ANY] * 2, "spread_keys", 1 << 10,
        local + [pltpu.SemaphoreType.DMA((2 + chips,))], 60 * MIB, ANY,
    )(keys, values)
    ring = [[2 * i + core for i in range(chips)] for core in range(2)]
    mine = lax.all_to_all(sent, "kv", 0, 0, tiled=True, axis_index_groups=ring)
    half = shape((HD, lanes), jnp.bfloat16)
    keep, give = call(turn_kernel, (half, half), [VMEM], "turn_queries", 1 << 20)(queries)
    mate = lax.ppermute(give, "kv", to_mate)
    later = lax.ppermute(keep, "pb", [(i + 1, i) for i in range(n_pb - 1)])
    steps = [((z + 1) * n_kv + (i ^ 2), z * n_kv + i) for z in range(n_pb - 1) for i in range(n_kv)]
    later_mate = lax.ppermute(give, ("pb", "kv"), steps)
    mine, later, later_mate = lax.optimization_barrier((mine, later, later_mate))
    other = lax.ppermute(mine, "kv", [(i, i ^ 1) for i in range(n_kv)])

    def scratch(sets):
        state = [(HD, sets * lanes), (1, sets * lanes), (1, sets * lanes)]
        kept = pltpu.VMEM((chips // SPAN, sets, 2 * rows * SPAN, lanes), jnp.float32)
        return [shape(one, jnp.float32) for one in state], [pltpu.VMEM(one, jnp.float32) for one in state], kept

    _, state, kept = scratch(2)
    part, pages = call(
        later_kernel,
        (shape((HD + STAT_ROWS, 2 * lanes), jnp.bfloat16), shape((n_slots, 2, PAGE, HD), jnp.bfloat16)),
        [SMEM] * 2 + [VMEM] * 4, "later_rows", LONG, state + [kept],
    )(doc_lengths, page_table, later, later_mate, mine, other)
    back = lax.ppermute(part, "pb", [(i, i + 1) for i in range(n_pb - 1)])
    sharing = [
        [head * n_kv + (2 * pair + chip) * 2 + core for head in range(n_head) for chip in range(2)]
        for pair in range(chips // 2)
        for core in range(2)
    ]
    arrived = lax.all_to_all(pages, ("head", "kv"), 0, 0, tiled=True, axis_index_groups=sharing)
    shapes, state, kept = scratch(1)
    out = shape((rows, columns // 2), jnp.bfloat16)
    mate_own = call(mate_kernel, tuple(shapes), [SMEM] + [VMEM] * 3, "mate_row", LONG, [kept])(
        doc_lengths, mate, mine, other
    )
    mate_out = call(mate_join_kernel, out, [VMEM] * 4, "mate_join", 1 << 20)(*mate_own, back)
    mate_out = lax.ppermute(mate_out, "kv", to_mate)
    own_out = call(own_kernel, out, [SMEM] + [VMEM] * 4, "own_row", 1 << 30, state + [kept])(
        doc_lengths, keep, mine, other, back
    )
    pool = shape((n_slots // (2 * n_head), 2, PAGE, 2 * n_head * HD), jnp.bfloat16)
    return call(
        place_kernel, (shape((rows, columns), jnp.bfloat16), pool), [VMEM] * 3, "place", 1 << 10
    )(own_out, mate_out, arrived)


def solution(mesh):
    in_specs = (P(("pb", "kv"), "head"), P(("pb", "kv"), "head"), P(("pb", "kv"), "head"), P(), P())
    out_specs = (P(("pb", "kv"), "head"), P(("head", "pb", "kv"), None, None, None))
    return jax.shard_map(body, mesh=mesh, in_specs=in_specs, out_specs=out_specs, check_vma=False)
```

time: 60.5 us -> 57.7 us (0.954)
  the two profiles are of different devices: /device:TPU:184 before, /device:TPU:152 now
where the time goes in v4:
time: 57.7 us; the launch traced here: 57.2 us
  starting transfers between devices  33.8 us (59%)
  waiting for transfers between devices  14.4 us (25%)
  Pallas kernels  7.57 us (13%)
  between operations  0.79 us (1%)
  local copies, waits for them, and re-layouts  0.67 us (1%)
    ppermute x1, waiting for transfers between devices, body(): later_mate = lax.ppermute(give, ('pb', 'kv'), steps)  9.09 us
    ppermute x1, starting transfers between devices, body(): back = lax.ppermute(part, 'pb', [(i, i + 1) for i in range(n_pb - 1)])  8.44 us
    all_to_all x1, starting transfers between devices, body(): mine = lax.all_to_all(sent, 'kv', 0, 0, tiled=True, axis_index_groups=ring)  7.46 us
    all_to_all x1, starting transfers between devices, body(): lax.all_to_all(pages, ('head', 'kv'), 0, 0, tiled=True, axis_index_groups...  5.77 us
    ppermute x1, starting transfers between devices, body(): mate = lax.ppermute(give, 'kv', to_mate)  3.54 us
    ppermute x1, waiting for transfers between devices, body(): mate_out = lax.ppermute(mate_out, 'kv', to_mate)  3.18 us
    ppermute x1, starting transfers between devices, body(): later_mate = lax.ppermute(give, ('pb', 'kv'), steps)  2.87 us
    ppermute x1, starting transfers between devices, body(): later = lax.ppermute(keep, 'pb', [(i + 1, i) for i in range(n_pb - 1)])  1.92 us
  transfers between devices with their start and end apart: 8, of which 4 were waited for; matrix products, arithmetic and copies ran while one was open for 0% of the time, Pallas kernels for 9%

profile of v4, /device:TPU:152, one launch (start us, length us, event | category | flops | bytes accessed | tf_op | source)
XLA Modules:
  0.0 57.2 jit_solution(16104910967638449886)
XLA Ops:
  0.6 1.8 %spread_keys.1 = bf16[8,128,256]{2,1,0:T(8,128)(2,1)} custom-call(bf16[128,256]{1,0:T(8,128)(2,1)} %keys_ref.1, bf16[128,256]{1,0:T(8,128)(2,1)} %values_ref.1), custom_call_target="tpu_custom_call" | custom-call | flops 1024 | bytes 3145728 | tf_op jit(solution)/shard_map/spread_keys/pallas_call | solution.py:259
  2.4 0.0 copy-start
  2.4 7.5 %all-to-all-start = ((bf16[8,128,256]{2,1,0:T(8,128)(2,1)}), bf16[8,128,256]{2,1,0:T(8,128)(2,1)S(1)}, u32[]{:S(2)}, u32[]{:S(2)}) async-start(bf16[8,128,256]{2,1,0:T(8,128)(2,1)} %spread_keys.1), calls=%async_computation | async-start | bytes 1048576 | tf_op jit(solution)/shard_map/all_to_all | solution.py:264
  9.9 0.0 copy-done
  9.9 0.0 copy-start.3
  9.9 0.1 turn_queries.1
  10.0 0.0 copy-start.4
  10.0 1.9 %collective-permute-start = (bf16[128,512]{1,0:T(8,128)(2,1)S(1)}, bf16[128,512]{1,0:T(8,128)(2,1)S(1)}, u32[]{:S(2)}, u32[]{:S(2)}) collective-permute-start(bf16[128,512]{1,0:T(8,128)(2,1)S(1)} %get-tuple-element.12.q_ref), channel_id=1, source_target_pairs={{16,0},{32,16},{48,32},{64,48},{80,64},{96,80},{112,96},{17,1},{33... | collective-permute-start | bytes 393224 | tf_op jit(solution)/shard_map/ppermute | solution.py:268
  12.0 0.0 copy-start.1
  12.0 0.6 %copy-done.1 = bf16[128,512]{1,0:T(8,128)(2,1)} copy-done((bf16[128,512]{1,0:T(8,128)(2,1)}, bf16[128,512]{1,0:T(8,128)(2,1)S(1)}, u32[]{:S(2)}) %copy-start.1) | copy-done | bytes 131096
  12.6 2.9 %collective-permute-start.1 = (bf16[128,512]{1,0:T(8,128)(2,1)S(1)}, bf16[128,512]{1,0:T(8,128)(2,1)S(1)}, u32[]{:S(2)}, u32[]{:S(2)}) collective-permute-start(bf16[128,512]{1,0:T(8,128)(2,1)S(1)} %get-tuple-element.13), channel_id=1, source_target_pairs={{18,0},{19,1},{16,2},{17,3},{22,4},{23,5},{20,6},{21,7},{26,8},{27... | collective-permute-start | bytes 393224 | tf_op jit(solution)/shard_map/ppermute | solution.py:270
  15.5 1.8 %collective-permute-done.q_ref = bf16[128,512]{1,0:T(8,128)(2,1)S(1)} collective-permute-done((bf16[128,512]{1,0:T(8,128)(2,1)S(1)}, bf16[128,512]{1,0:T(8,128)(2,1)S(1)}, u32[]{:S(2)}, u32[]{:S(2)}) %collective-permute-start) | collective-permute-done | bytes 131104 | tf_op jit(solution)/shard_map/ppermute | solution.py:268
  17.2 9.1 %collective-permute-done.1.mate_ref = bf16[128,512]{1,0:T(8,128)(2,1)S(1)} collective-permute-done((bf16[128,512]{1,0:T(8,128)(2,1)S(1)}, bf16[128,512]{1,0:T(8,128)(2,1)S(1)}, u32[]{:S(2)}, u32[]{:S(2)}) %collective-permute-start.1) | collective-permute-done | bytes 131104 | tf_op jit(solution)/shard_map/ppermute | solution.py:270
  26.3 0.0 all-to-all-done.mine_ref
  26.3 1.9 %collective-permute-start.2 = (bf16[8,128,256]{2,1,0:T(8,128)(2,1)S(1)}, bf16[8,128,256]{2,1,0:T(8,128)(2,1)S(1)}, u32[]{:S(2)}, u32[]{:S(2)}) collective-permute-start(bf16[8,128,256]{2,1,0:T(8,128)(2,1)S(1)} %all-to-all-done.mine_ref), channel_id=1, source_target_pairs={{0,1},{1,0},{2,3},{3,2},{4,5},{5,4},{6,7},{7,6},{8,9},{9,8},{10,11... | collective-permute-start | bytes 1572872 | tf_op jit(solution)/shard_map/ppermute | solution.py:272
  28.3 3.5 %collective-permute-start.4 = (bf16[128,512]{1,0:T(8,128)(2,1)S(1)}, bf16[128,512]{1,0:T(8,128)(2,1)S(1)}, u32[]{:S(2)}, u32[]{:S(2)}) collective-permute-start(bf16[128,512]{1,0:T(8,128)(2,1)S(1)} %get-tuple-element.13), channel_id=1, source_target_pairs={{0,2},{1,3},{2,0},{3,1},{4,6},{5,7},{6,4},{7,5},{8,10},{9,11},{10,... | collective-permute-start | bytes 393224 | tf_op jit(solution)/shard_map/ppermute | solution.py:267
  31.8 0.0 collective-permute-done.2.other_ref
  31.8 0.0 copy-done.3
  31.8 0.0 copy-done.4
  31.8 1.5 %later_rows.1 = (bf16[144,1024]{1,0:T(8,128)(2,1)S(1)}, bf16[16,2,16,128]{3,2,1,0:T(8,128)(2,1)}) custom-call(s32[17]{0:T(128)S(1)} %copy-done.4, s32[1024]{0:T(1024)S(1)} %copy-done.3, bf16[128,512]{1,0:T(8,128)(2,1)S(1)} %collective-permute-done.q_ref, bf16[128,512]{1,0:T(8,128)(2,1)S(1)} %collective-permute-done.1.mate_ref, ...), custom_call_target="tpu_custom_call" | custom-call | flops 99999997952 | bytes 3145728 | tf_op jit(solution)/shard_map/later_rows/pallas_call | solution.py:280
  33.3 8.4 %collective-permute-start.3 = (bf16[144,1024]{1,0:T(8,128)(2,1)S(1)}, bf16[144,1024]{1,0:T(8,128)(2,1)S(1)}, u32[]{:S(2)}, u32[]{:S(2)}) collective-permute-start(bf16[144,1024]{1,0:T(8,128)(2,1)S(1)} %get-tuple-element.17), channel_id=1, source_target_pairs={{0,16},{16,32},{32,48},{48,64},{64,80},{80,96},{96,112},{1,17},{17... | collective-permute-start | bytes 884744 | tf_op jit(solution)/shard_map/ppermute | solution.py:285
  41.8 5.8 %all-to-all-start.1 = ((bf16[16,2,16,128]{3,2,1,0:T(8,128)(2,1)}), bf16[16,2,16,128]{3,2,1,0:T(8,128)(2,1)S(1)}, u32[]{:S(2)}, u32[]{:S(2)}) async-start(bf16[16,2,16,128]{3,2,1,0:T(8,128)(2,1)} %get-tuple-element.21), calls=%async_computation.1 | async-start | bytes 262144 | tf_op jit(solution)/shard_map/all_to_all | solution.py:291
  47.5 0.0 collective-permute-done.4.q_ref
  47.5 1.9 %mate_row.1 = (f32[128,512]{1,0:T(8,128)S(1)}, f32[1,512]{1,0:T(1,128)S(1)}, f32[1,512]{1,0:T(1,128)S(1)}) custom-call(s32[17]{0:T(128)S(1)} %copy-done.4, bf16[128,512]{1,0:T(8,128)(2,1)S(1)} %collective-permute-done.4.q_ref, bf16[8,128,256]{2,1,0:T(8,128)(2,1)S(1)} %all-to-all-done.mine_ref, bf16[8,128,256]{2,1,0:T(8,128)(2,1)S(1)} %collective-permute-done.2.other_ref), custom_call_target="tpu_custom_call" | custom-call | flops 99999997952 | bytes 3145728 | tf_op jit(solution)/shard_map/mate_row/pallas_call | solution.py:294
  49.4 0.0 collective-permute-done.3.part_ref
  49.4 0.0 copy-start.2
  49.4 0.1 mate_join.1
  49.6 1.9 %collective-permute-start.5 = (bf16[128,512]{1,0:T(8,128)(2,1)S(1)}, bf16[128,512]{1,0:T(8,128)(2,1)S(1)}, u32[]{:S(2)}, u32[]{:S(2)}) collective-permute-start(bf16[128,512]{1,0:T(8,128)(2,1)S(1)} %mate_join.1), channel_id=1, source_target_pairs={{0,2},{1,3},{2,0},{3,1},{4,6},{5,7},{6,4},{7,5},{8,10},{9,11},{10,... | collective-permute-start | bytes 393224 | tf_op jit(solution)/shard_map/ppermute | solution.py:298
  51.5 0.0 copy-done.2
  51.5 1.4 %own_row.1.own_ref = bf16[128,512]{1,0:T(8,128)(2,1)S(1)} custom-call(s32[17]{0:T(128)S(1)} %copy-done.4, bf16[128,512]{1,0:T(8,128)(2,1)S(1)} %copy-done.2, bf16[8,128,256]{2,1,0:T(8,128)(2,1)S(1)} %all-to-all-done.mine_ref, bf16[8,128,256]{2,1,0:T(8,128)(2,1)S(1)} %collective-permute-done.2.other_ref, bf16[144,1024]{1,0:T(8,128)(2,1)S(1)} %collective-permute-done.3.part_ref), custom_call_target="tpu_custom_call" | custom-call | flops 1073741824 | bytes 3145728 | tf_op jit(solution)/shard_map/own_row/pallas_call | solution.py:299
  52.9 0.3 all-to-all-done.1.pages_ref
  53.3 3.2 %collective-permute-done.5.mate_ref = bf16[128,512]{1,0:T(8,128)(2,1)S(1)} collective-permute-done((bf16[128,512]{1,0:T(8,128)(2,1)S(1)}, bf16[128,512]{1,0:T(8,128)(2,1)S(1)}, u32[]{:S(2)}, u32[]{:S(2)}) %collective-permute-start.5) | collective-permute-done | bytes 131104 | tf_op jit(solution)/shard_map/ppermute | solution.py:298
  56.5 0.8 %place.1 = (bf16[128,1024]{1,0:T(8,128)(2,1)}, bf16[2,2,16,1024]{3,2,1,0:T(8,128)(2,1)}) custom-call(bf16[128,512]{1,0:T(8,128)(2,1)S(1)} %own_row.1.own_ref, bf16[128,512]{1,0:T(8,128)(2,1)S(1)} %collective-permute-done.5.mate_ref, bf16[16,2,16,128]{3,2,1,0:T(8,128)(2,1)S(1)} %all-to-all-done.1.pages_ref), custom_call_target="tpu_custom_call" | custom-call | flops 1024 | bytes 3145728 | tf_op jit(solution)/shard_map/place/pallas_call | solution.py:303
Async XLA Ops:
  2.4 7.5 %copy-start = (bf16[128,1024]{1,0:T(8,128)(2,1)S(1)}, bf16[128,1024]{1,0:T(8,128)(2,1)}, u32[]{:S(2)}) copy-start(bf16[128,1024]{1,0:T(8,128)(2,1)} %q_ref.1) | copy-start | bytes 786436
  2.4 23.9 %all-to-all-start = ((bf16[8,128,256]{2,1,0:T(8,128)(2,1)}), bf16[8,128,256]{2,1,0:T(8,128)(2,1)S(1)}, u32[]{:S(2)}, u32[]{:S(2)}) async-start(bf16[8,128,256]{2,1,0:T(8,128)(2,1)} %spread_keys.1), calls=%async_computation | async-start | bytes 1048576 | tf_op jit(solution)/shard_map/all_to_all | solution.py:264
  9.9 21.9 %copy-start.3 = (s32[1024]{0:T(1024)S(1)}, s32[1024]{0:T(1024)}, u32[]{:S(2)}) copy-start(s32[1024]{0:T(1024)} %table_ref.1) | copy-start | bytes 12292
  10.0 21.8 %copy-start.4 = (s32[17]{0:T(128)S(1)}, s32[17]{0:T(128)}, u32[]{:S(2)}) copy-start(s32[17]{0:T(128)} %lengths_ref.5) | copy-start | bytes 208
  10.0 7.2 %collective-permute-start = (bf16[128,512]{1,0:T(8,128)(2,1)S(1)}, bf16[128,512]{1,0:T(8,128)(2,1)S(1)}, u32[]{:S(2)}, u32[]{:S(2)}) collective-permute-start(bf16[128,512]{1,0:T(8,128)(2,1)S(1)} %get-tuple-element.12.q_ref), channel_id=1, source_target_pairs={{16,0},{32,16},{48,32},{64,48},{80,64},{96,80},{112,96},{17,1},{33... | collective-permute-start | bytes 393224 | tf_op jit(solution)/shard_map/ppermute | solution.py:268
  12.0 0.7 %copy-start.1 = (bf16[128,512]{1,0:T(8,128)(2,1)}, bf16[128,512]{1,0:T(8,128)(2,1)S(1)}, u32[]{:S(2)}) copy-start(bf16[128,512]{1,0:T(8,128)(2,1)S(1)} %get-tuple-element.12.q_ref) | copy-start | bytes 393220
  12.6 13.7 %collective-permute-start.1 = (bf16[128,512]{1,0:T(8,128)(2,1)S(1)}, bf16[128,512]{1,0:T(8,128)(2,1)S(1)}, u32[]{:S(2)}, u32[]{:S(2)}) collective-permute-start(bf16[128,512]{1,0:T(8,128)(2,1)S(1)} %get-tuple-element.13), channel_id=1, source_target_pairs={{18,0},{19,1},{16,2},{17,3},{22,4},{23,5},{20,6},{21,7},{26,8},{27... | collective-permute-start | bytes 393224 | tf_op jit(solution)/shard_map/ppermute | solution.py:270
  26.3 5.5 %collective-permute-start.2 = (bf16[8,128,256]{2,1,0:T(8,128)(2,1)S(1)}, bf16[8,128,256]{2,1,0:T(8,128)(2,1)S(1)}, u32[]{:S(2)}, u32[]{:S(2)}) collective-permute-start(bf16[8,128,256]{2,1,0:T(8,128)(2,1)S(1)} %all-to-all-done.mine_ref), channel_id=1, source_target_pairs={{0,1},{1,0},{2,3},{3,2},{4,5},{5,4},{6,7},{7,6},{8,9},{9,8},{10,11... | collective-permute-start | bytes 1572872 | tf_op jit(solution)/shard_map/ppermute | solution.py:272
  28.3 19.3 %collective-permute-start.4 = (bf16[128,512]{1,0:T(8,128)(2,1)S(1)}, bf16[128,512]{1,0:T(8,128)(2,1)S(1)}, u32[]{:S(2)}, u32[]{:S(2)}) collective-permute-start(bf16[128,512]{1,0:T(8,128)(2,1)S(1)} %get-tuple-element.13), channel_id=1, source_target_pairs={{0,2},{1,3},{2,0},{3,1},{4,6},{5,7},{6,4},{7,5},{8,10},{9,11},{10,... | collective-permute-start | bytes 393224 | tf_op jit(solution)/shard_map/ppermute | solution.py:267
  33.3 16.1 %collective-permute-start.3 = (bf16[144,1024]{1,0:T(8,128)(2,1)S(1)}, bf16[144,1024]{1,0:T(8,128)(2,1)S(1)}, u32[]{:S(2)}, u32[]{:S(2)}) collective-permute-start(bf16[144,1024]{1,0:T(8,128)(2,1)S(1)} %get-tuple-element.17), channel_id=1, source_target_pairs={{0,16},{16,32},{32,48},{48,64},{64,80},{80,96},{96,112},{1,17},{17... | collective-permute-start | bytes 884744 | tf_op jit(solution)/shard_map/ppermute | solution.py:285
  41.8 11.5 %all-to-all-start.1 = ((bf16[16,2,16,128]{3,2,1,0:T(8,128)(2,1)}), bf16[16,2,16,128]{3,2,1,0:T(8,128)(2,1)S(1)}, u32[]{:S(2)}, u32[]{:S(2)}) async-start(bf16[16,2,16,128]{3,2,1,0:T(8,128)(2,1)} %get-tuple-element.21), calls=%async_computation.1 | async-start | bytes 262144 | tf_op jit(solution)/shard_map/all_to_all | solution.py:291
  49.4 2.1 %copy-start.2 = (bf16[128,512]{1,0:T(8,128)(2,1)S(1)}, bf16[128,512]{1,0:T(8,128)(2,1)}, u32[]{:S(2)}) copy-start(bf16[128,512]{1,0:T(8,128)(2,1)} %copy-done.1) | copy-start | bytes 393220
  49.6 6.9 %collective-permute-start.5 = (bf16[128,512]{1,0:T(8,128)(2,1)S(1)}, bf16[128,512]{1,0:T(8,128)(2,1)S(1)}, u32[]{:S(2)}, u32[]{:S(2)}) collective-permute-start(bf16[128,512]{1,0:T(8,128)(2,1)S(1)} %mate_join.1), channel_id=1, source_target_pairs={{0,2},{1,3},{2,0},{3,1},{4,6},{5,7},{6,4},{7,5},{8,10},{9,11},{10,... | collective-permute-start | bytes 393224 | tf_op jit(solution)/shard_map/ppermute | solution.py:298

commit v5 on v4

--- a/solution.py
+++ b/solution.py
@@ -13,6 +13,7 @@
 SPAN = 2
 LOWEST = -1e30
 STAT_ROWS = 16
+PLAN_PAGES = 7
 LONG = 10**11
 FACTOR = HD**-0.5 * math.log2(math.e)
 
@@ -47,7 +48,33 @@
         copy.wait()
 
 
-def turn_kernel(q_ref, keep_ref, give_ref):
+def bases(rows, later):
+    pb, kv = lax.axis_index("pb"), lax.axis_index("kv")
+    row_tokens = lax.axis_size("kv") * rows
+    chip = lax.div(kv, 2)
+    mate = (chip + 1 - 2 * lax.rem(chip, 2)) * 2 + lax.rem(kv, 2)
+    q_row = (pb + later) * row_tokens
+    return (q_row + kv * rows, q_row + mate * rows), pb * row_tokens, lax.rem(kv, 2)
+
+
+def page_codes(table_ref, rows, n_slots):
+    pb, kv = lax.axis_index("pb"), lax.axis_index("kv")
+    n_head, n_pb, n_kv = lax.axis_size("head"), lax.axis_size("pb"), lax.axis_size("kv")
+    row_pages = n_kv * rows // PAGE
+    slot_rows = row_pages // n_head
+    per = n_slots // (2 * n_head)
+    first_chip = lax.div(kv, 4) * 2
+    block_pages = rows // PAGE
+    for i in range(n_slots):
+        head, chip, which = i // (2 * per), i // per % 2, i % per
+        slot = head * (n_pb * slot_rows) + pb * slot_rows + ((first_chip + chip) * 2 + lax.rem(kv, 2)) * per + which
+        page = table_ref[slot] - pb * row_pages
+        block = lax.div(page, block_pages)
+        row = lax.div(block, 2) * rows + lax.rem(page, block_pages) * PAGE
+        yield 2 * row + (lax.rem(block, 2) == lax.rem(kv, 2)).astype(jnp.int32)
+
+
+def turn_kernel(lengths_ref, table_ref, q_ref, keep_ref, give_ref, plan_ref, *, n_slots):
     group = lax.rem(lax.div(lax.axis_index("kv"), 2), 2)
     rows = q_ref.shape[0]
     heads = keep_ref.shape[1] // rows
@@ -55,9 +82,16 @@
         for h in range(heads):
             cols = pl.ds(pl.multiple_of((one * heads + h) * HD, HD), HD)
             out_ref[:, h * rows : (h + 1) * rows] = jnp.transpose(q_ref[:, cols])
-
-
-def scan_keys(lengths_ref, q_refs, mine_ref, other_ref, q_bases, k_base, core, acc, top, total, kept, SPAN=SPAN):
+    lane = lax.broadcasted_iota(jnp.int32, (1, rows), 1)
+    plan = [doc_start(lengths_ref, base + lane) for later in range(2) for base in bases(rows, later)[0]]
+    pages = jnp.zeros((1, rows), jnp.int32)
+    for i, code in enumerate(page_codes(table_ref, rows, n_slots)):
+        pages = jnp.where(lane == i, code, pages)
+    plan += [pages] * (plan_ref.shape[0] - len(plan))
+    plan_ref[...] = jnp.concatenate(plan, axis=0)
+
+
+def scan_keys(plan_ref, sets, q_refs, mine_ref, other_ref, q_bases, k_base, core, acc, top, total, kept):
     rows = mine_ref.shape[1]
     lanes = q_refs[0].shape[1]
     heads = lanes // rows
@@ -68,10 +102,10 @@
     total[...] = jnp.zeros_like(total)
     q_low = functools.reduce(jnp.minimum, q_bases)
     q_high = functools.reduce(jnp.maximum, q_bases) + rows - 1
-    first_start = doc_start(lengths_ref, q_low)
-    last_start = doc_start(lengths_ref, q_high)
+    first_start = functools.reduce(jnp.minimum, [plan_ref[i, 0] for i in sets])
+    last_start = functools.reduce(jnp.maximum, [plan_ref[i, rows - 1] for i in sets])
     q_pos = [base + lax.broadcasted_iota(jnp.int32, (1, rows), 1) for base in q_bases]
-    q_start = [doc_start(lengths_ref, one) for one in q_pos]
+    q_start = [plan_ref[i : i + 1, :] for i in sets]
     low_tile = jnp.clip(lax.div(first_start - k_base, tile), 0, count)
     high_tile = jnp.clip(lax.div(q_high - k_base, tile) + 1, 0, count)
 
@@ -134,51 +168,34 @@
     return [high, middle, low]
 
 
-def bases(rows, later):
-    pb, kv = lax.axis_index("pb"), lax.axis_index("kv")
-    row_tokens = lax.axis_size("kv") * rows
-    chip = lax.div(kv, 2)
-    mate = (chip + 1 - 2 * lax.rem(chip, 2)) * 2 + lax.rem(kv, 2)
-    q_row = (pb + later) * row_tokens
-    return (q_row + kv * rows, q_row + mate * rows), pb * row_tokens, lax.rem(kv, 2)
-
-
-def pick_pages(table_ref, mine_ref, other_ref, pages_ref):
-    pb, kv = lax.axis_index("pb"), lax.axis_index("kv")
-    n_head, n_pb, n_kv = lax.axis_size("head"), lax.axis_size("pb"), lax.axis_size("kv")
-    core = lax.rem(kv, 2)
+def pick_pages(plan_ref, mine_ref, other_ref, pages_ref):
     rows = mine_ref.shape[1]
-    n_slots = pages_ref.shape[0]
-    row_pages = n_kv * rows // PAGE
-    slot_rows = row_pages // n_head
-    per = n_slots // 8
-    first_chip = lax.div(kv, 4) * 2
-    for i in range(n_slots):
-        head, chip, which = i // (2 * per), i // per % 2, i % per
-        slot = head * (n_pb * slot_rows) + pb * slot_rows + ((first_chip + chip) * 2 + core) * per + which
-        page = table_ref[slot] - pb * row_pages
-        block_pages = rows // PAGE
-        block = lax.div(page, block_pages)
-        held = lax.div(block, 2)
-        row = pl.multiple_of(lax.rem(page, block_pages) * PAGE, PAGE)
-        own = lax.rem(block, 2) == core
+    for i in range(pages_ref.shape[0]):
+        code = plan_ref[PLAN_PAGES, i]
+        own = lax.rem(code, 2) == 1
+        place = lax.div(code, 2)
+        chip = lax.div(place, rows)
+        row = pl.multiple_of(lax.rem(place, rows), PAGE)
         for half in range(2):
             cols = slice(half * HD, (half + 1) * HD)
             pages_ref[i, half] = jnp.where(
-                own, mine_ref[held, pl.ds(row, PAGE), cols], other_ref[held, pl.ds(row, PAGE), cols]
+                own, mine_ref[chip, pl.ds(row, PAGE), cols], other_ref[chip, pl.ds(row, PAGE), cols]
             )
 
 
 def later_kernel(
-    lengths_ref, table_ref, q_ref, mate_ref, mine_ref, other_ref, part_ref, pages_ref, acc, top, total, kept
+    plan_ref, q_ref, mate_ref, mine_ref, other_ref, part_ref, pages_ref, acc, top, total, kept, picked, sem
 ):
-    pick_pages(table_ref, mine_ref, other_ref, pages_ref)
+    pick_pages(plan_ref, mine_ref, other_ref, picked)
+    leave = pltpu.make_async_copy(picked, pages_ref, sem)
+    leave.start()
     q_bases, k_base, core = bases(mine_ref.shape[1], 1)
-    scan_keys(lengths_ref, (q_ref, mate_ref), mine_ref, other_ref, q_bases, k_base, core, acc, top, total, kept)
+    scan_keys(plan_ref, (2, 3), (q_ref, mate_ref), mine_ref, other_ref, q_bases, k_base, core, acc, top, total, kept)
     part_ref[0:HD, :] = (acc[...] / jnp.maximum(total[...], 1e-30)).astype(jnp.bfloat16)
     stats = split_three(top[...]) + split_three(total[...])
     stats.append(jnp.zeros((STAT_ROWS - len(stats), acc.shape[1]), jnp.bfloat16))
     part_ref[HD : HD + STAT_ROWS, :] = jnp.concatenate(stats, axis=0)
+    leave.wait()
 
 
 def join(acc, top, total, part_ref, which, out_ref):
@@ -198,18 +215,18 @@
         out_ref[:, h * HD : (h + 1) * HD] = jnp.transpose(mixed[:, h * rows : (h + 1) * rows]).astype(jnp.bfloat16)
 
 
-def mate_kernel(lengths_ref, q_ref, mine_ref, other_ref, acc, top, total, kept):
+def mate_kernel(plan_ref, q_ref, mine_ref, other_ref, acc, top, total, kept):
     q_bases, k_base, core = bases(mine_ref.shape[1], 0)
-    scan_keys(lengths_ref, (q_ref,), mine_ref, other_ref, q_bases[1:], k_base, core, acc, top, total, kept)
+    scan_keys(plan_ref, (1,), (q_ref,), mine_ref, other_ref, q_bases[1:], k_base, core, acc, top, total, kept)
 
 
 def mate_join_kernel(acc, top, total, part_ref, out_ref):
     join(acc, top, total, part_ref, 1, out_ref)
 
 
-def own_kernel(lengths_ref, q_ref, mine_ref, other_ref, part_ref, out_ref, acc, top, total, kept):
+def own_kernel(plan_ref, q_ref, mine_ref, other_ref, part_ref, out_ref, acc, top, total, kept):
     q_bases, k_base, core = bases(mine_ref.shape[1], 0)
-    scan_keys(lengths_ref, (q_ref,), mine_ref, other_ref, q_bases[:1], k_base, core, acc, top, total, kept)
+    scan_keys(plan_ref, (0,), (q_ref,), mine_ref, other_ref, q_bases[:1], k_base, core, acc, top, total, kept)
     join(acc, top, total, part_ref, 0, out_ref)
 
 
@@ -263,7 +280,11 @@
     ring = [[2 * i + core for i in range(chips)] for core in range(2)]
     mine = lax.all_to_all(sent, "kv", 0, 0, tiled=True, axis_index_groups=ring)
     half = shape((HD, lanes), jnp.bfloat16)
-    keep, give = call(turn_kernel, (half, half), [VMEM], "turn_queries", 1 << 20)(queries)
+    plan = shape((PLAN_PAGES + 1, rows), jnp.int32)
+    turn = functools.partial(turn_kernel, n_slots=n_slots)
+    keep, give, plan = call(turn, (half, half, plan), [SMEM, SMEM, VMEM], "turn_queries", 1 << 20)(
+        doc_lengths, page_table, queries
+    )
     mate = lax.ppermute(give, "kv", to_mate)
     later = lax.ppermute(keep, "pb", [(i + 1, i) for i in range(n_pb - 1)])
     steps = [((z + 1) * n_kv + (i ^ 2), z * n_kv + i) for z in range(n_pb - 1) for i in range(n_kv)]
@@ -280,8 +301,9 @@
     part, pages = call(
         later_kernel,
         (shape((HD + STAT_ROWS, 2 * lanes), jnp.bfloat16), shape((n_slots, 2, PAGE, HD), jnp.bfloat16)),
-        [SMEM] * 2 + [VMEM] * 4, "later_rows", LONG, state + [kept],
-    )(doc_lengths, page_table, later, later_mate, mine, other)
+        [VMEM] * 5, "later_rows", LONG,
+        state + [kept, pltpu.VMEM((n_slots, 2, PAGE, HD), jnp.bfloat16), pltpu.SemaphoreType.DMA], out=(VMEM, ANY),
+    )(plan, later, later_mate, mine, other)
     back = lax.ppermute(part, "pb", [(i, i + 1) for i in range(n_pb - 1)])
     sharing = [
         [head * n_kv + (2 * pair + chip) * 2 + core for head in range(n_head) for chip in range(2)]
@@ -291,13 +313,13 @@
     arrived = lax.all_to_all(pages, ("head", "kv"), 0, 0, tiled=True, axis_index_groups=sharing)
     shapes, state, kept = scratch(1)
     out = shape((rows, columns // 2), jnp.bfloat16)
-    mate_own = call(mate_kernel, tuple(shapes), [SMEM] + [VMEM] * 3, "mate_row", LONG, [kept])(
-        doc_lengths, mate, mine, other
+    mate_own = call(mate_kernel, tuple(shapes), [VMEM] * 4, "mate_row", LONG, [kept])(
+        plan, mate, mine, other
     )
     mate_out = call(mate_join_kernel, out, [VMEM] * 4, "mate_join", 1 << 20)(*mate_own, back)
     mate_out = lax.ppermute(mate_out, "kv", to_mate)
-    own_out = call(own_kernel, out, [SMEM] + [VMEM] * 4, "own_row", 1 << 30, state + [kept])(
-        doc_lengths, keep, mine, other, back
+    own_out = call(own_kernel, out, [VMEM] * 5, "own_row", 1 << 30, state + [kept])(
+        plan, keep, mine, other, back
     )
     pool = shape((n_slots // (2 * n_head), 2, PAGE, 2 * n_head * HD), jnp.bfloat16)
     return call(

time: 57.7 us -> 55.3 us (0.958)
  the two profiles are of different devices: /device:TPU:152 before, /device:TPU:260 now
where the time goes in v5:
time: 55.3 us; the launch traced here: 54.8 us
  starting transfers between devices  29.1 us (53%)
  waiting for transfers between devices  16.7 us (30%)
  Pallas kernels  7.5 us (14%)
  between operations  0.8 us (1%)
  local copies, waits for them, and re-layouts  0.67 us (1%)
    ppermute x1, waiting for transfers between devices, body(): later_mate = lax.ppermute(give, ('pb', 'kv'), steps)  9.54 us
    all_to_all x1, starting transfers between devices, body(): mine = lax.all_to_all(sent, 'kv', 0, 0, tiled=True, axis_index_groups=ring)  7.24 us
    all_to_all x1, starting transfers between devices, body(): lax.all_to_all(pages, ('head', 'kv'), 0, 0, tiled=True, axis_index_groups...  4.82 us
    ppermute x1, starting transfers between devices, body(): back = lax.ppermute(part, 'pb', [(i, i + 1) for i in range(n_pb - 1)])  4.37 us
    ppermute x1, waiting for transfers between devices, body(): mate_out = lax.ppermute(mate_out, 'kv', to_mate)  3.6 us
    ppermute x1, starting transfers between devices, body(): mate = lax.ppermute(give, 'kv', to_mate)  3.51 us
    ppermute x1, starting transfers between devices, body(): later_mate = lax.ppermute(give, ('pb', 'kv'), steps)  3 us
    ppermute x1, starting transfers between devices, body(): mate_out = lax.ppermute(mate_out, 'kv', to_mate)  2.33 us
  transfers between devices with their start and end apart: 8, of which 4 were waited for; matrix products, arithmetic and copies ran while one was open for 0% of the time, Pallas kernels for 9%

profile of v5, /device:TPU:260, one launch (start us, length us, event | category | flops | bytes accessed | tf_op | source)
XLA Modules:
  0.0 54.8 jit_solution(8001268277699760015)
XLA Ops:
  0.6 1.8 %spread_keys.1 = bf16[8,128,256]{2,1,0:T(8,128)(2,1)} custom-call(bf16[128,256]{1,0:T(8,128)(2,1)} %keys_ref.1, bf16[128,256]{1,0:T(8,128)(2,1)} %values_ref.1), custom_call_target="tpu_custom_call" | custom-call | flops 1024 | bytes 3145728 | tf_op jit(solution)/shard_map/spread_keys/pallas_call | solution.py:276
  2.4 0.0 copy-start
  2.4 0.0 copy-start.1
  2.4 0.0 copy-start.2
  2.4 7.2 %all-to-all-start = ((bf16[8,128,256]{2,1,0:T(8,128)(2,1)}), bf16[8,128,256]{2,1,0:T(8,128)(2,1)S(1)}, u32[]{:S(2)}, u32[]{:S(2)}) async-start(bf16[8,128,256]{2,1,0:T(8,128)(2,1)} %spread_keys.1), calls=%async_computation | async-start | bytes 1048576 | tf_op jit(solution)/shard_map/all_to_all | solution.py:281
  9.7 0.0 copy-done
  9.7 0.0 copy-done.1
  9.7 0.0 copy-done.2
  9.7 0.9 %turn_queries.1 = (bf16[128,512]{1,0:T(8,128)(2,1)S(1)}, bf16[128,512]{1,0:T(8,128)(2,1)S(1)}, s32[8,128]{1,0:T(8,128)S(1)}) custom-call(s32[17]{0:T(128)S(1)} %copy-done.2, s32[1024]{0:T(1024)S(1)} %copy-done.1, bf16[128,1024]{1,0:T(8,128)(2,1)S(1)} %copy-done), custom_call_target="tpu_custom_call" | custom-call | flops 1048576 | bytes 3145728 | tf_op jit(solution)/shard_map/turn_queries/pallas_call | solution.py:285
  10.6 1.9 %collective-permute-start = (bf16[128,512]{1,0:T(8,128)(2,1)S(1)}, bf16[128,512]{1,0:T(8,128)(2,1)S(1)}, u32[]{:S(2)}, u32[]{:S(2)}) collective-permute-start(bf16[128,512]{1,0:T(8,128)(2,1)S(1)} %get-tuple-element.14.q_ref), channel_id=1, source_target_pairs={{16,0},{32,16},{48,32},{64,48},{80,64},{96,80},{112,96},{17,1},{33... | collective-permute-start | bytes 393224 | tf_op jit(solution)/shard_map/ppermute | solution.py:289
  12.5 0.0 copy-start.3
  12.5 0.6 %copy-done.3 = bf16[128,512]{1,0:T(8,128)(2,1)} copy-done((bf16[128,512]{1,0:T(8,128)(2,1)}, bf16[128,512]{1,0:T(8,128)(2,1)S(1)}, u32[]{:S(2)}) %copy-start.3) | copy-done | bytes 131096
  13.2 3.0 %collective-permute-start.1 = (bf16[128,512]{1,0:T(8,128)(2,1)S(1)}, bf16[128,512]{1,0:T(8,128)(2,1)S(1)}, u32[]{:S(2)}, u32[]{:S(2)}) collective-permute-start(bf16[128,512]{1,0:T(8,128)(2,1)S(1)} %get-tuple-element.15), channel_id=1, source_target_pairs={{18,0},{19,1},{16,2},{17,3},{22,4},{23,5},{20,6},{21,7},{26,8},{27... | collective-permute-start | bytes 393224 | tf_op jit(solution)/shard_map/ppermute | solution.py:291
  16.2 1.3 %collective-permute-done.q_ref = bf16[128,512]{1,0:T(8,128)(2,1)S(1)} collective-permute-done((bf16[128,512]{1,0:T(8,128)(2,1)S(1)}, bf16[128,512]{1,0:T(8,128)(2,1)S(1)}, u32[]{:S(2)}, u32[]{:S(2)}) %collective-permute-start) | collective-permute-done | bytes 131104 | tf_op jit(solution)/shard_map/ppermute | solution.py:289
  17.4 9.5 %collective-permute-done.1.mate_ref = bf16[128,512]{1,0:T(8,128)(2,1)S(1)} collective-permute-done((bf16[128,512]{1,0:T(8,128)(2,1)S(1)}, bf16[128,512]{1,0:T(8,128)(2,1)S(1)}, u32[]{:S(2)}, u32[]{:S(2)}) %collective-permute-start.1) | collective-permute-done | bytes 131104 | tf_op jit(solution)/shard_map/ppermute | solution.py:291
  27.0 0.0 all-to-all-done.mine_ref
  27.0 1.9 %collective-permute-start.2 = (bf16[8,128,256]{2,1,0:T(8,128)(2,1)S(1)}, bf16[8,128,256]{2,1,0:T(8,128)(2,1)S(1)}, u32[]{:S(2)}, u32[]{:S(2)}) collective-permute-start(bf16[8,128,256]{2,1,0:T(8,128)(2,1)S(1)} %all-to-all-done.mine_ref), channel_id=1, source_target_pairs={{0,1},{1,0},{2,3},{3,2},{4,5},{5,4},{6,7},{7,6},{8,9},{9,8},{10,11... | collective-permute-start | bytes 1572872 | tf_op jit(solution)/shard_map/ppermute | solution.py:293
  28.9 3.5 %collective-permute-start.4 = (bf16[128,512]{1,0:T(8,128)(2,1)S(1)}, bf16[128,512]{1,0:T(8,128)(2,1)S(1)}, u32[]{:S(2)}, u32[]{:S(2)}) collective-permute-start(bf16[128,512]{1,0:T(8,128)(2,1)S(1)} %get-tuple-element.15), channel_id=1, source_target_pairs={{0,2},{1,3},{2,0},{3,1},{4,6},{5,7},{6,4},{7,5},{8,10},{9,11},{10,... | collective-permute-start | bytes 393224 | tf_op jit(solution)/shard_map/ppermute | solution.py:288
  32.4 0.0 collective-permute-done.2.other_ref
  32.4 2.3 %later_rows.1 = (bf16[144,1024]{1,0:T(8,128)(2,1)S(1)}, bf16[16,2,16,128]{3,2,1,0:T(8,128)(2,1)}) custom-call(s32[8,128]{1,0:T(8,128)S(1)} %get-tuple-element.13.plan_ref, bf16[128,512]{1,0:T(8,128)(2,1)S(1)} %collective-permute-done.q_ref, bf16[128,512]{1,0:T(8,128)(2,1)S(1)} %collective-permute-done.1.mate_ref, ...), custom_call_target="tpu_custom_call" | custom-call | flops 99999997952 | bytes 3145728 | tf_op jit(solution)/shard_map/later_rows/pallas_call | solution.py:301
  34.7 4.4 %collective-permute-start.3 = (bf16[144,1024]{1,0:T(8,128)(2,1)S(1)}, bf16[144,1024]{1,0:T(8,128)(2,1)S(1)}, u32[]{:S(2)}, u32[]{:S(2)}) collective-permute-start(bf16[144,1024]{1,0:T(8,128)(2,1)S(1)} %get-tuple-element.19), channel_id=1, source_target_pairs={{0,16},{16,32},{32,48},{48,64},{64,80},{80,96},{96,112},{1,17},{17... | collective-permute-start | bytes 884744 | tf_op jit(solution)/shard_map/ppermute | solution.py:307
  39.1 4.8 %all-to-all-start.1 = ((bf16[16,2,16,128]{3,2,1,0:T(8,128)(2,1)}), bf16[16,2,16,128]{3,2,1,0:T(8,128)(2,1)S(1)}, u32[]{:S(2)}, u32[]{:S(2)}) async-start(bf16[16,2,16,128]{3,2,1,0:T(8,128)(2,1)} %get-tuple-element.23), calls=%async_computation.1 | async-start | bytes 262144 | tf_op jit(solution)/shard_map/all_to_all | solution.py:313
  43.9 0.0 collective-permute-done.4.q_ref
  43.9 0.7 %mate_row.1 = (f32[128,512]{1,0:T(8,128)S(1)}, f32[1,512]{1,0:T(1,128)S(1)}, f32[1,512]{1,0:T(1,128)S(1)}) custom-call(s32[8,128]{1,0:T(8,128)S(1)} %get-tuple-element.13.plan_ref, bf16[128,512]{1,0:T(8,128)(2,1)S(1)} %collective-permute-done.4.q_ref, bf16[8,128,256]{2,1,0:T(8,128)(2,1)S(1)} %all-to-all-done.mine_ref, ...), custom_call_target="tpu_custom_call" | custom-call | flops 99999997952 | bytes 3145728 | tf_op jit(solution)/shard_map/mate_row/pallas_call | solution.py:316
  44.7 2.3 %collective-permute-done.3.part_ref = bf16[144,1024]{1,0:T(8,128)(2,1)S(1)} collective-permute-done((bf16[144,1024]{1,0:T(8,128)(2,1)S(1)}, bf16[144,1024]{1,0:T(8,128)(2,1)S(1)}, u32[]{:S(2)}, u32[]{:S(2)}) %collective-permute-start.3) | collective-permute-done | bytes 294944 | tf_op jit(solution)/shard_map/ppermute | solution.py:307
  47.0 0.0 copy-start.4
  47.0 0.1 mate_join.1
  47.1 2.3 %collective-permute-start.5 = (bf16[128,512]{1,0:T(8,128)(2,1)S(1)}, bf16[128,512]{1,0:T(8,128)(2,1)S(1)}, u32[]{:S(2)}, u32[]{:S(2)}) collective-permute-start(bf16[128,512]{1,0:T(8,128)(2,1)S(1)} %mate_join.1), channel_id=1, source_target_pairs={{0,2},{1,3},{2,0},{3,1},{4,6},{5,7},{6,4},{7,5},{8,10},{9,11},{10,... | collective-permute-start | bytes 393224 | tf_op jit(solution)/shard_map/ppermute | solution.py:320
  49.5 0.0 copy-done.4
  49.5 0.9 %own_row.1.own_ref = bf16[128,512]{1,0:T(8,128)(2,1)S(1)} custom-call(s32[8,128]{1,0:T(8,128)S(1)} %get-tuple-element.13.plan_ref, bf16[128,512]{1,0:T(8,128)(2,1)S(1)} %copy-done.4, bf16[8,128,256]{2,1,0:T(8,128)(2,1)S(1)} %all-to-all-done.mine_ref, bf16[8,128,256]{2,1,0:T(8,128)(2,1)S(1)} %collective-permute-done.2.other_ref, ...), custom_call_target="tpu_custom_call" | custom-call | flops 1073741824 | bytes 3145728 | tf_op jit(solution)/shard_map/own_row/pallas_call | solution.py:321
  50.4 0.0 all-to-all-done.1.pages_ref
  50.4 3.6 %collective-permute-done.5.mate_ref = bf16[128,512]{1,0:T(8,128)(2,1)S(1)} collective-permute-done((bf16[128,512]{1,0:T(8,128)(2,1)S(1)}, bf16[128,512]{1,0:T(8,128)(2,1)S(1)}, u32[]{:S(2)}, u32[]{:S(2)}) %collective-permute-start.5) | collective-permute-done | bytes 131104 | tf_op jit(solution)/shard_map/ppermute | solution.py:320
  54.0 0.8 %place.1 = (bf16[128,1024]{1,0:T(8,128)(2,1)}, bf16[2,2,16,1024]{3,2,1,0:T(8,128)(2,1)}) custom-call(bf16[128,512]{1,0:T(8,128)(2,1)S(1)} %own_row.1.own_ref, bf16[128,512]{1,0:T(8,128)(2,1)S(1)} %collective-permute-done.5.mate_ref, bf16[16,2,16,128]{3,2,1,0:T(8,128)(2,1)S(1)} %all-to-all-done.1.pages_ref), custom_call_target="tpu_custom_call" | custom-call | flops 1024 | bytes 3145728 | tf_op jit(solution)/shard_map/place/pallas_call | solution.py:325
Async XLA Ops:
  2.4 7.3 %copy-start = (bf16[128,1024]{1,0:T(8,128)(2,1)S(1)}, bf16[128,1024]{1,0:T(8,128)(2,1)}, u32[]{:S(2)}) copy-start(bf16[128,1024]{1,0:T(8,128)(2,1)} %q_ref.1) | copy-start | bytes 786436
  2.4 7.3 %copy-start.1 = (s32[1024]{0:T(1024)S(1)}, s32[1024]{0:T(1024)}, u32[]{:S(2)}) copy-start(s32[1024]{0:T(1024)} %table_ref.1) | copy-start | bytes 12292
  2.4 7.3 %copy-start.2 = (s32[17]{0:T(128)S(1)}, s32[17]{0:T(128)}, u32[]{:S(2)}) copy-start(s32[17]{0:T(128)} %lengths_ref.1) | copy-start | bytes 208
  2.4 24.6 %all-to-all-start = ((bf16[8,128,256]{2,1,0:T(8,128)(2,1)}), bf16[8,128,256]{2,1,0:T(8,128)(2,1)S(1)}, u32[]{:S(2)}, u32[]{:S(2)}) async-start(bf16[8,128,256]{2,1,0:T(8,128)(2,1)} %spread_keys.1), calls=%async_computation | async-start | bytes 1048576 | tf_op jit(solution)/shard_map/all_to_all | solution.py:281
  10.6 6.9 %collective-permute-start = (bf16[128,512]{1,0:T(8,128)(2,1)S(1)}, bf16[128,512]{1,0:T(8,128)(2,1)S(1)}, u32[]{:S(2)}, u32[]{:S(2)}) collective-permute-start(bf16[128,512]{1,0:T(8,128)(2,1)S(1)} %get-tuple-element.14.q_ref), channel_id=1, source_target_pairs={{16,0},{32,16},{48,32},{64,48},{80,64},{96,80},{112,96},{17,1},{33... | collective-permute-start | bytes 393224 | tf_op jit(solution)/shard_map/ppermute | solution.py:289
  12.5 0.7 %copy-start.3 = (bf16[128,512]{1,0:T(8,128)(2,1)}, bf16[128,512]{1,0:T(8,128)(2,1)S(1)}, u32[]{:S(2)}) copy-start(bf16[128,512]{1,0:T(8,128)(2,1)S(1)} %get-tuple-element.14.q_ref) | copy-start | bytes 393220
  13.2 13.8 %collective-permute-start.1 = (bf16[128,512]{1,0:T(8,128)(2,1)S(1)}, bf16[128,512]{1,0:T(8,128)(2,1)S(1)}, u32[]{:S(2)}, u32[]{:S(2)}) collective-permute-start(bf16[128,512]{1,0:T(8,128)(2,1)S(1)} %get-tuple-element.15), channel_id=1, source_target_pairs={{18,0},{19,1},{16,2},{17,3},{22,4},{23,5},{20,6},{21,7},{26,8},{27... | collective-permute-start | bytes 393224 | tf_op jit(solution)/shard_map/ppermute | solution.py:291
  27.0 5.4 %collective-permute-start.2 = (bf16[8,128,256]{2,1,0:T(8,128)(2,1)S(1)}, bf16[8,128,256]{2,1,0:T(8,128)(2,1)S(1)}, u32[]{:S(2)}, u32[]{:S(2)}) collective-permute-start(bf16[8,128,256]{2,1,0:T(8,128)(2,1)S(1)} %all-to-all-done.mine_ref), channel_id=1, source_target_pairs={{0,1},{1,0},{2,3},{3,2},{4,5},{5,4},{6,7},{7,6},{8,9},{9,8},{10,11... | collective-permute-start | bytes 1572872 | tf_op jit(solution)/shard_map/ppermute | solution.py:293
  28.9 15.0 %collective-permute-start.4 = (bf16[128,512]{1,0:T(8,128)(2,1)S(1)}, bf16[128,512]{1,0:T(8,128)(2,1)S(1)}, u32[]{:S(2)}, u32[]{:S(2)}) collective-permute-start(bf16[128,512]{1,0:T(8,128)(2,1)S(1)} %get-tuple-element.15), channel_id=1, source_target_pairs={{0,2},{1,3},{2,0},{3,1},{4,6},{5,7},{6,4},{7,5},{8,10},{9,11},{10,... | collective-permute-start | bytes 393224 | tf_op jit(solution)/shard_map/ppermute | solution.py:288
  34.7 12.2 %collective-permute-start.3 = (bf16[144,1024]{1,0:T(8,128)(2,1)S(1)}, bf16[144,1024]{1,0:T(8,128)(2,1)S(1)}, u32[]{:S(2)}, u32[]{:S(2)}) collective-permute-start(bf16[144,1024]{1,0:T(8,128)(2,1)S(1)} %get-tuple-element.19), channel_id=1, source_target_pairs={{0,16},{16,32},{32,48},{48,64},{64,80},{80,96},{96,112},{1,17},{17... | collective-permute-start | bytes 884744 | tf_op jit(solution)/shard_map/ppermute | solution.py:307
  39.1 11.3 %all-to-all-start.1 = ((bf16[16,2,16,128]{3,2,1,0:T(8,128)(2,1)}), bf16[16,2,16,128]{3,2,1,0:T(8,128)(2,1)S(1)}, u32[]{:S(2)}, u32[]{:S(2)}) async-start(bf16[16,2,16,128]{3,2,1,0:T(8,128)(2,1)} %get-tuple-element.23), calls=%async_computation.1 | async-start | bytes 262144 | tf_op jit(solution)/shard_map/all_to_all | solution.py:313
  47.0 2.5 %copy-start.4 = (bf16[128,512]{1,0:T(8,128)(2,1)S(1)}, bf16[128,512]{1,0:T(8,128)(2,1)}, u32[]{:S(2)}) copy-start(bf16[128,512]{1,0:T(8,128)(2,1)} %copy-done.3) | copy-start | bytes 393220
  47.1 6.9 %collective-permute-start.5 = (bf16[128,512]{1,0:T(8,128)(2,1)S(1)}, bf16[128,512]{1,0:T(8,128)(2,1)S(1)}, u32[]{:S(2)}, u32[]{:S(2)}) collective-permute-start(bf16[128,512]{1,0:T(8,128)(2,1)S(1)} %mate_join.1), channel_id=1, source_target_pairs={{0,2},{1,3},{2,0},{3,1},{4,6},{5,7},{6,4},{7,5},{8,10},{9,11},{10,... | collective-permute-start | bytes 393224 | tf_op jit(solution)/shard_map/ppermute | solution.py:320

commit v6 on v5

--- a/solution.py
+++ b/solution.py
@@ -74,14 +74,19 @@
         yield 2 * row + (lax.rem(block, 2) == lax.rem(kv, 2)).astype(jnp.int32)
 
 
+def turn(q_ref, group, out_ref):
+    rows = q_ref.shape[0]
+    heads = out_ref.shape[1] // rows
+    for h in range(heads):
+        cols = pl.ds(pl.multiple_of((group * heads + h) * HD, HD), HD)
+        out_ref[:, h * rows : (h + 1) * rows] = jnp.transpose(q_ref[:, cols])
+
+
 def turn_kernel(lengths_ref, table_ref, q_ref, keep_ref, give_ref, plan_ref, *, n_slots):
     group = lax.rem(lax.div(lax.axis_index("kv"), 2), 2)
     rows = q_ref.shape[0]
-    heads = keep_ref.shape[1] // rows
-    for out_ref, one in ((keep_ref, group), (give_ref, 1 - group)):
-        for h in range(heads):
-            cols = pl.ds(pl.multiple_of((one * heads + h) * HD, HD), HD)
-            out_ref[:, h * rows : (h + 1) * rows] = jnp.transpose(q_ref[:, cols])
+    turn(q_ref, group, keep_ref)
+    turn(q_ref, 1 - group, give_ref)
     lane = lax.broadcasted_iota(jnp.int32, (1, rows), 1)
     plan = [doc_start(lengths_ref, base + lane) for later in range(2) for base in bases(rows, later)[0]]
     pages = jnp.zeros((1, rows), jnp.int32)
@@ -91,12 +96,13 @@
     plan_ref[...] = jnp.concatenate(plan, axis=0)
 
 
-def scan_keys(plan_ref, sets, q_refs, mine_ref, other_ref, q_bases, k_base, core, acc, top, total, kept):
-    rows = mine_ref.shape[1]
+def scan_keys(plan_ref, sets, q_refs, blocks, q_bases, k_base, acc, top, total, kept):
+    rows = plan_ref.shape[1]
     lanes = q_refs[0].shape[1]
     heads = lanes // rows
     tile = 2 * rows * SPAN
-    count = mine_ref.shape[0] // SPAN
+    count = blocks[0][0].shape[0] // SPAN
+    size = len(blocks) * rows * SPAN
     acc[...] = jnp.zeros_like(acc)
     top[...] = jnp.full_like(top, LOWEST)
     total[...] = jnp.zeros_like(total)
@@ -110,54 +116,56 @@
     high_tile = jnp.clip(lax.div(q_high - k_base, tile) + 1, 0, count)
 
     def columns(at, cols):
-        parts = []
-        for chip in range(SPAN):
-            parts += [mine_ref[at * SPAN + chip, :, cols], other_ref[at * SPAN + chip, :, cols]]
+        parts = [ref[at * SPAN + chip, :, cols] for chip in range(SPAN) for ref, _ in blocks]
         return jnp.concatenate(parts, axis=0)
 
-    def score(at, masked):
-        keys = columns(at, slice(0, HD))
+    def score(at, masked, several, carry):
+        keys = jnp.concatenate([columns(at + i, slice(0, HD)) for i in range(several)], axis=0)
         if masked:
-            row = lax.broadcasted_iota(jnp.int32, (2 * rows, rows), 0)
-            k_pos = k_base + at * tile + jnp.where(row < rows, row + core * rows, row - core * rows)
-            k_pos = jnp.concatenate([k_pos + chip * 2 * rows for chip in range(SPAN)], axis=0)
+            row = k_base + at * tile + lax.broadcasted_iota(jnp.int32, (rows, rows), 0)
+            k_pos = [row + (2 * chip + core) * rows for chip in range(SPAN) for _, core in blocks]
+            k_pos = jnp.concatenate(k_pos, axis=0)
         for i, q_ref in enumerate(q_refs):
             where = slice(i * lanes, (i + 1) * lanes)
             scores = jnp.dot(keys, q_ref[...], preferred_element_type=jnp.float32)
             if masked:
                 seen = (k_pos <= q_pos[i]) & (k_pos >= q_start[i])
                 scores = jnp.where(jnp.concatenate([seen] * heads, axis=1), scores, LOWEST)
-            kept[at, i] = scores
+            for more in range(several):
+                kept[at + more, i] = scores[more * size : (more + 1) * size]
             top[:, where] = jnp.maximum(top[:, where], jnp.max(scores, axis=0, keepdims=True))
-
-    def first_pass(at, carry):
-        low = k_base + at * tile
-        whole = (low + tile - 1 <= q_low) & (low >= last_start)
-
-        @pl.when(whole)
-        def _():
-            score(at, False)
-
-        @pl.when(jnp.logical_not(whole))
-        def _():
-            score(at, True)
-
         return carry
 
-    def second_pass(at, carry):
-        values = columns(at, slice(HD, 2 * HD))
+    def second_pass(at, carry, several=1):
+        values = jnp.concatenate([columns(at + i, slice(HD, 2 * HD)) for i in range(several)], axis=0)
         for i in range(len(q_refs)):
             where = slice(i * lanes, (i + 1) * lanes)
             peak = jnp.maximum(top[:, where], 0.1 * LOWEST) * FACTOR
-            weights = jnp.exp2(kept[at, i] * FACTOR - peak)
+            scores = jnp.concatenate([kept[at + more, i] for more in range(several)], axis=0)
+            weights = jnp.exp2(scores * FACTOR - peak)
             total[:, where] = total[:, where] + jnp.sum(weights, axis=0, keepdims=True)
             acc[:, where] = acc[:, where] + lax.dot_general(
                 values, weights.astype(jnp.bfloat16), (((0,), (0,)), ((), ())), preferred_element_type=jnp.float32
             )
         return carry
 
-    lax.fori_loop(low_tile, high_tile, first_pass, 0)
-    lax.fori_loop(low_tile, high_tile, second_pass, 0)
+    tiles = jnp.clip(lax.div(last_start - k_base + tile - 1, tile), low_tile, high_tile)
+    ends = jnp.clip(lax.div(q_low + 1 - k_base, tile), tiles, high_tile)
+    lax.fori_loop(low_tile, tiles, lambda at, carry: score(at, True, 1, carry), 0)
+    whole_pairs = lax.div(ends - tiles, 2)
+    lax.fori_loop(0, whole_pairs, lambda i, carry: score(tiles + 2 * i, False, 2, carry), 0)
+
+    @pl.when(tiles + 2 * whole_pairs < ends)
+    def _():
+        score(ends - 1, False, 1, 0)
+
+    lax.fori_loop(ends, high_tile, lambda at, carry: score(at, True, 1, carry), 0)
+    pairs = lax.div(high_tile - low_tile, 2)
+    lax.fori_loop(0, pairs, lambda i, carry: second_pass(low_tile + 2 * i, carry, 2), 0)
+
+    @pl.when(low_tile + 2 * pairs < high_tile)
+    def _():
+        second_pass(high_tile - 1, 0)
 
 
 def split_three(value):
@@ -190,7 +198,8 @@
     leave = pltpu.make_async_copy(picked, pages_ref, sem)
     leave.start()
     q_bases, k_base, core = bases(mine_ref.shape[1], 1)
-    scan_keys(plan_ref, (2, 3), (q_ref, mate_ref), mine_ref, other_ref, q_bases, k_base, core, acc, top, total, kept)
+    blocks = ((mine_ref, core), (other_ref, 1 - core))
+    scan_keys(plan_ref, (2, 3), (q_ref, mate_ref), blocks, q_bases, k_base, acc, top, total, kept)
     part_ref[0:HD, :] = (acc[...] / jnp.maximum(total[...], 1e-30)).astype(jnp.bfloat16)
     stats = split_three(top[...]) + split_three(total[...])
     stats.append(jnp.zeros((STAT_ROWS - len(stats), acc.shape[1]), jnp.bfloat16))
@@ -217,16 +226,19 @@
 
 def mate_kernel(plan_ref, q_ref, mine_ref, other_ref, acc, top, total, kept):
     q_bases, k_base, core = bases(mine_ref.shape[1], 0)
-    scan_keys(plan_ref, (1,), (q_ref,), mine_ref, other_ref, q_bases[1:], k_base, core, acc, top, total, kept)
+    blocks = ((mine_ref, core), (other_ref, 1 - core))
+    scan_keys(plan_ref, (1,), (q_ref,), blocks, q_bases[1:], k_base, acc, top, total, kept)
 
 
 def mate_join_kernel(acc, top, total, part_ref, out_ref):
     join(acc, top, total, part_ref, 1, out_ref)
 
 
-def own_kernel(plan_ref, q_ref, mine_ref, other_ref, part_ref, out_ref, acc, top, total, kept):
+def own_kernel(plan_ref, q_ref, mine_ref, other_ref, part_ref, out_ref, acc, top, total, kept, turned):
+    turn(q_ref, lax.rem(lax.div(lax.axis_index("kv"), 2), 2), turned)
     q_bases, k_base, core = bases(mine_ref.shape[1], 0)
-    scan_keys(plan_ref, (0,), (q_ref,), mine_ref, other_ref, q_bases[:1], k_base, core, acc, top, total, kept)
+    blocks = ((mine_ref, core), (other_ref, 1 - core))
+    scan_keys(plan_ref, (0,), (turned,), blocks, q_bases[:1], k_base, acc, top, total, kept)
     join(acc, top, total, part_ref, 0, out_ref)
 
 
@@ -318,8 +330,8 @@
     )
     mate_out = call(mate_join_kernel, out, [VMEM] * 4, "mate_join", 1 << 20)(*mate_own, back)
     mate_out = lax.ppermute(mate_out, "kv", to_mate)
-    own_out = call(own_kernel, out, [VMEM] * 5, "own_row", 1 << 30, state + [kept])(
-        plan, keep, mine, other, back
+    own_out = call(own_kernel, out, [VMEM] * 5, "own_row", 1 << 30, state + [kept, pltpu.VMEM((HD, lanes), jnp.bfloat16)])(
+        plan, queries, mine, other, back
     )
     pool = shape((n_slots // (2 * n_head), 2, PAGE, 2 * n_head * HD), jnp.bfloat16)
     return call(

time: 55.3 us -> 55.8 us (level)
  the two profiles are of different devices: /device:TPU:260 before, /device:TPU:152 now
where the time goes in v6:
time: 55.8 us; the launch traced here: 55.4 us
  starting transfers between devices  33.1 us (59%)
  waiting for transfers between devices  14.8 us (27%)
  Pallas kernels  6.68 us (12%)
  between operations  0.79 us (1%)
    ppermute x1, waiting for transfers between devices, body(): later_mate = lax.ppermute(give, ('pb', 'kv'), steps)  10.8 us
    ppermute x1, starting transfers between devices, body(): back = lax.ppermute(part, 'pb', [(i, i + 1) for i in range(n_pb - 1)])  7.73 us
    all_to_all x1, starting transfers between devices, body(): mine = lax.all_to_all(sent, 'kv', 0, 0, tiled=True, axis_index_groups=ring)  7.46 us
    all_to_all x1, starting transfers between devices, body(): lax.all_to_all(pages, ('head', 'kv'), 0, 0, tiled=True, axis_index_groups...  5.76 us
    ppermute x1, starting transfers between devices, body(): mate = lax.ppermute(give, 'kv', to_mate)  3.54 us
    ppermute x1, waiting for transfers between devices, body(): mate_out = lax.ppermute(mate_out, 'kv', to_mate)  2.89 us
    ppermute x1, starting transfers between devices, body(): later = lax.ppermute(keep, 'pb', [(i + 1, i) for i in range(n_pb - 1)])  2.88 us
    ppermute x1, starting transfers between devices, body(): later_mate = lax.ppermute(give, ('pb', 'kv'), steps)  1.92 us
  transfers between devices with their start and end apart: 8, of which 3 were waited for; matrix products, arithmetic and copies ran while one was open for 0% of the time, Pallas kernels for 7%

profile of v6, /device:TPU:152, one launch (start us, length us, event | category | flops | bytes accessed | tf_op | source)
XLA Modules:
  0.0 55.4 jit_solution(3463219720670304318)
XLA Ops:
  0.6 1.8 %spread_keys.1 = bf16[8,128,256]{2,1,0:T(8,128)(2,1)} custom-call(bf16[128,256]{1,0:T(8,128)(2,1)} %keys_ref.1, bf16[128,256]{1,0:T(8,128)(2,1)} %values_ref.1), custom_call_target="tpu_custom_call" | custom-call | flops 1024 | bytes 3145728 | tf_op jit(solution)/shard_map/spread_keys/pallas_call | solution.py:288
  2.4 0.0 copy-start
  2.4 0.0 copy-start.2
  2.4 0.0 copy-start.3
  2.4 7.5 %all-to-all-start = ((bf16[8,128,256]{2,1,0:T(8,128)(2,1)}), bf16[8,128,256]{2,1,0:T(8,128)(2,1)S(1)}, u32[]{:S(2)}, u32[]{:S(2)}) async-start(bf16[8,128,256]{2,1,0:T(8,128)(2,1)} %spread_keys.1), calls=%async_computation | async-start | bytes 1048576 | tf_op jit(solution)/shard_map/all_to_all | solution.py:293
  9.9 0.0 copy-done
  9.9 0.0 copy-done.2
  9.9 0.0 copy-done.3
  9.9 0.9 %turn_queries.1 = (bf16[128,512]{1,0:T(8,128)(2,1)S(1)}, bf16[128,512]{1,0:T(8,128)(2,1)S(1)}, s32[8,128]{1,0:T(8,128)S(1)}) custom-call(s32[17]{0:T(128)S(1)} %copy-done.3, s32[1024]{0:T(1024)S(1)} %copy-done.2, bf16[128,1024]{1,0:T(8,128)(2,1)S(1)} %copy-done), custom_call_target="tpu_custom_call" | custom-call | flops 1048576 | bytes 3145728 | tf_op jit(solution)/shard_map/turn_queries/pallas_call | solution.py:297
  10.8 1.9 %collective-permute-start.1 = (bf16[128,512]{1,0:T(8,128)(2,1)S(1)}, bf16[128,512]{1,0:T(8,128)(2,1)S(1)}, u32[]{:S(2)}, u32[]{:S(2)}) collective-permute-start(bf16[128,512]{1,0:T(8,128)(2,1)S(1)} %get-tuple-element.15), channel_id=1, source_target_pairs={{18,0},{19,1},{16,2},{17,3},{22,4},{23,5},{20,6},{21,7},{26,8},{27... | collective-permute-start | bytes 393224 | tf_op jit(solution)/shard_map/ppermute | solution.py:303
  12.7 2.9 %collective-permute-start = (bf16[128,512]{1,0:T(8,128)(2,1)S(1)}, bf16[128,512]{1,0:T(8,128)(2,1)S(1)}, u32[]{:S(2)}, u32[]{:S(2)}) collective-permute-start(bf16[128,512]{1,0:T(8,128)(2,1)S(1)} %get-tuple-element.14), channel_id=1, source_target_pairs={{16,0},{32,16},{48,32},{64,48},{80,64},{96,80},{112,96},{17,1},{33... | collective-permute-start | bytes 393224 | tf_op jit(solution)/shard_map/ppermute | solution.py:301
  15.6 10.8 %collective-permute-done.1.mate_ref = bf16[128,512]{1,0:T(8,128)(2,1)S(1)} collective-permute-done((bf16[128,512]{1,0:T(8,128)(2,1)S(1)}, bf16[128,512]{1,0:T(8,128)(2,1)S(1)}, u32[]{:S(2)}, u32[]{:S(2)}) %collective-permute-start.1) | collective-permute-done | bytes 131104 | tf_op jit(solution)/shard_map/ppermute | solution.py:303
  26.4 0.0 collective-permute-done.q_ref
  26.4 0.0 all-to-all-done.mine_ref
  26.4 1.9 %collective-permute-start.2 = (bf16[8,128,256]{2,1,0:T(8,128)(2,1)S(1)}, bf16[8,128,256]{2,1,0:T(8,128)(2,1)S(1)}, u32[]{:S(2)}, u32[]{:S(2)}) collective-permute-start(bf16[8,128,256]{2,1,0:T(8,128)(2,1)S(1)} %all-to-all-done.mine_ref), channel_id=1, source_target_pairs={{0,1},{1,0},{2,3},{3,2},{4,5},{5,4},{6,7},{7,6},{8,9},{9,8},{10,11... | collective-permute-start | bytes 1572872 | tf_op jit(solution)/shard_map/ppermute | solution.py:305
  28.3 3.5 %collective-permute-start.4 = (bf16[128,512]{1,0:T(8,128)(2,1)S(1)}, bf16[128,512]{1,0:T(8,128)(2,1)S(1)}, u32[]{:S(2)}, u32[]{:S(2)}) collective-permute-start(bf16[128,512]{1,0:T(8,128)(2,1)S(1)} %get-tuple-element.15), channel_id=1, source_target_pairs={{0,2},{1,3},{2,0},{3,1},{4,6},{5,7},{6,4},{7,5},{8,10},{9,11},{10,... | collective-permute-start | bytes 393224 | tf_op jit(solution)/shard_map/ppermute | solution.py:300
  31.8 0.0 collective-permute-done.2.other_ref
  31.9 0.9 %later_rows.1 = (bf16[144,1024]{1,0:T(8,128)(2,1)S(1)}, bf16[16,2,16,128]{3,2,1,0:T(8,128)(2,1)}) custom-call(s32[8,128]{1,0:T(8,128)S(1)} %get-tuple-element.13.plan_ref, bf16[128,512]{1,0:T(8,128)(2,1)S(1)} %collective-permute-done.q_ref, bf16[128,512]{1,0:T(8,128)(2,1)S(1)} %collective-permute-done.1.mate_ref, ...), custom_call_target="tpu_custom_call" | custom-call | flops 99999997952 | bytes 3145728 | tf_op jit(solution)/shard_map/later_rows/pallas_call | solution.py:313
  32.8 7.7 %collective-permute-start.3 = (bf16[144,1024]{1,0:T(8,128)(2,1)S(1)}, bf16[144,1024]{1,0:T(8,128)(2,1)S(1)}, u32[]{:S(2)}, u32[]{:S(2)}) collective-permute-start(bf16[144,1024]{1,0:T(8,128)(2,1)S(1)} %get-tuple-element.19), channel_id=1, source_target_pairs={{0,16},{16,32},{32,48},{48,64},{64,80},{80,96},{96,112},{1,17},{17... | collective-permute-start | bytes 884744 | tf_op jit(solution)/shard_map/ppermute | solution.py:319
  40.5 5.8 %all-to-all-start.1 = ((bf16[16,2,16,128]{3,2,1,0:T(8,128)(2,1)}), bf16[16,2,16,128]{3,2,1,0:T(8,128)(2,1)S(1)}, u32[]{:S(2)}, u32[]{:S(2)}) async-start(bf16[16,2,16,128]{3,2,1,0:T(8,128)(2,1)} %get-tuple-element.23), calls=%async_computation.1 | async-start | bytes 262144 | tf_op jit(solution)/shard_map/all_to_all | solution.py:325
  46.3 0.0 collective-permute-done.4.q_ref
  46.3 1.3 %mate_row.1 = (f32[128,512]{1,0:T(8,128)S(1)}, f32[1,512]{1,0:T(1,128)S(1)}, f32[1,512]{1,0:T(1,128)S(1)}) custom-call(s32[8,128]{1,0:T(8,128)S(1)} %get-tuple-element.13.plan_ref, bf16[128,512]{1,0:T(8,128)(2,1)S(1)} %collective-permute-done.4.q_ref, bf16[8,128,256]{2,1,0:T(8,128)(2,1)S(1)} %all-to-all-done.mine_ref, ...), custom_call_target="tpu_custom_call" | custom-call | flops 99999997952 | bytes 3145728 | tf_op jit(solution)/shard_map/mate_row/pallas_call | solution.py:328
  47.5 0.0 collective-permute-done.3.part_ref
  47.5 0.0 copy-start.1
  47.6 0.1 mate_join.1
  47.7 1.9 %collective-permute-start.5 = (bf16[128,512]{1,0:T(8,128)(2,1)S(1)}, bf16[128,512]{1,0:T(8,128)(2,1)S(1)}, u32[]{:S(2)}, u32[]{:S(2)}) collective-permute-start(bf16[128,512]{1,0:T(8,128)(2,1)S(1)} %mate_join.1), channel_id=1, source_target_pairs={{0,2},{1,3},{2,0},{3,1},{4,6},{5,7},{6,4},{7,5},{8,10},{9,11},{10,... | collective-permute-start | bytes 393224 | tf_op jit(solution)/shard_map/ppermute | solution.py:332
  49.6 0.0 copy-done.1
  49.7 0.9 %own_row.1.own_ref = bf16[128,512]{1,0:T(8,128)(2,1)S(1)} custom-call(s32[8,128]{1,0:T(8,128)S(1)} %get-tuple-element.13.plan_ref, bf16[128,1024]{1,0:T(8,128)(2,1)S(1)} %copy-done.1, bf16[8,128,256]{2,1,0:T(8,128)(2,1)S(1)} %all-to-all-done.mine_ref, bf16[8,128,256]{2,1,0:T(8,128)(2,1)S(1)} %collective-permute-done.2.other_ref, ...), custom_call_target="tpu_custom_call" | custom-call | flops 1073741824 | bytes 3145728 | tf_op jit(solution)/shard_map/own_row/pallas_call | solution.py:333
  50.6 1.1 %all-to-all-done.1.pages_ref = bf16[16,2,16,128]{3,2,1,0:T(8,128)(2,1)S(1)} async-done(((bf16[16,2,16,128]{3,2,1,0:T(8,128)(2,1)}), bf16[16,2,16,128]{3,2,1,0:T(8,128)(2,1)S(1)}, u32[]{:S(2)}, u32[]{:S(2)}) %all-to-all-start.1) | async-done | bytes 131104 | tf_op jit(solution)/shard_map/all_to_all | solution.py:325
  51.7 2.9 %collective-permute-done.5.mate_ref = bf16[128,512]{1,0:T(8,128)(2,1)S(1)} collective-permute-done((bf16[128,512]{1,0:T(8,128)(2,1)S(1)}, bf16[128,512]{1,0:T(8,128)(2,1)S(1)}, u32[]{:S(2)}, u32[]{:S(2)}) %collective-permute-start.5) | collective-permute-done | bytes 131104 | tf_op jit(solution)/shard_map/ppermute | solution.py:332
  54.6 0.8 %place.1 = (bf16[128,1024]{1,0:T(8,128)(2,1)}, bf16[2,2,16,1024]{3,2,1,0:T(8,128)(2,1)}) custom-call(bf16[128,512]{1,0:T(8,128)(2,1)S(1)} %own_row.1.own_ref, bf16[128,512]{1,0:T(8,128)(2,1)S(1)} %collective-permute-done.5.mate_ref, bf16[16,2,16,128]{3,2,1,0:T(8,128)(2,1)S(1)} %all-to-all-done.1.pages_ref), custom_call_target="tpu_custom_call" | custom-call | flops 1024 | bytes 3145728 | tf_op jit(solution)/shard_map/place/pallas_call | solution.py:337
Async XLA Ops:
  2.4 7.5 %copy-start = (bf16[128,1024]{1,0:T(8,128)(2,1)S(1)}, bf16[128,1024]{1,0:T(8,128)(2,1)}, u32[]{:S(2)}) copy-start(bf16[128,1024]{1,0:T(8,128)(2,1)} %q_ref.3) | copy-start | bytes 786436
  2.4 7.5 %copy-start.2 = (s32[1024]{0:T(1024)S(1)}, s32[1024]{0:T(1024)}, u32[]{:S(2)}) copy-start(s32[1024]{0:T(1024)} %table_ref.1) | copy-start | bytes 12292
  2.4 7.5 %copy-start.3 = (s32[17]{0:T(128)S(1)}, s32[17]{0:T(128)}, u32[]{:S(2)}) copy-start(s32[17]{0:T(128)} %lengths_ref.1) | copy-start | bytes 208
  2.4 23.9 %all-to-all-start = ((bf16[8,128,256]{2,1,0:T(8,128)(2,1)}), bf16[8,128,256]{2,1,0:T(8,128)(2,1)S(1)}, u32[]{:S(2)}, u32[]{:S(2)}) async-start(bf16[8,128,256]{2,1,0:T(8,128)(2,1)} %spread_keys.1), calls=%async_computation | async-start | bytes 1048576 | tf_op jit(solution)/shard_map/all_to_all | solution.py:293
  10.8 15.6 %collective-permute-start.1 = (bf16[128,512]{1,0:T(8,128)(2,1)S(1)}, bf16[128,512]{1,0:T(8,128)(2,1)S(1)}, u32[]{:S(2)}, u32[]{:S(2)}) collective-permute-start(bf16[128,512]{1,0:T(8,128)(2,1)S(1)} %get-tuple-element.15), channel_id=1, source_target_pairs={{18,0},{19,1},{16,2},{17,3},{22,4},{23,5},{20,6},{21,7},{26,8},{27... | collective-permute-start | bytes 393224 | tf_op jit(solution)/shard_map/ppermute | solution.py:303
  12.7 13.6 %collective-permute-start = (bf16[128,512]{1,0:T(8,128)(2,1)S(1)}, bf16[128,512]{1,0:T(8,128)(2,1)S(1)}, u32[]{:S(2)}, u32[]{:S(2)}) collective-permute-start(bf16[128,512]{1,0:T(8,128)(2,1)S(1)} %get-tuple-element.14), channel_id=1, source_target_pairs={{16,0},{32,16},{48,32},{64,48},{80,64},{96,80},{112,96},{17,1},{33... | collective-permute-start | bytes 393224 | tf_op jit(solution)/shard_map/ppermute | solution.py:301
  26.4 5.5 %collective-permute-start.2 = (bf16[8,128,256]{2,1,0:T(8,128)(2,1)S(1)}, bf16[8,128,256]{2,1,0:T(8,128)(2,1)S(1)}, u32[]{:S(2)}, u32[]{:S(2)}) collective-permute-start(bf16[8,128,256]{2,1,0:T(8,128)(2,1)S(1)} %all-to-all-done.mine_ref), channel_id=1, source_target_pairs={{0,1},{1,0},{2,3},{3,2},{4,5},{5,4},{6,7},{7,6},{8,9},{9,8},{10,11... | collective-permute-start | bytes 1572872 | tf_op jit(solution)/shard_map/ppermute | solution.py:305
  28.3 18.0 %collective-permute-start.4 = (bf16[128,512]{1,0:T(8,128)(2,1)S(1)}, bf16[128,512]{1,0:T(8,128)(2,1)S(1)}, u32[]{:S(2)}, u32[]{:S(2)}) collective-permute-start(bf16[128,512]{1,0:T(8,128)(2,1)S(1)} %get-tuple-element.15), channel_id=1, source_target_pairs={{0,2},{1,3},{2,0},{3,1},{4,6},{5,7},{6,4},{7,5},{8,10},{9,11},{10,... | collective-permute-start | bytes 393224 | tf_op jit(solution)/shard_map/ppermute | solution.py:300
  32.8 14.8 %collective-permute-start.3 = (bf16[144,1024]{1,0:T(8,128)(2,1)S(1)}, bf16[144,1024]{1,0:T(8,128)(2,1)S(1)}, u32[]{:S(2)}, u32[]{:S(2)}) collective-permute-start(bf16[144,1024]{1,0:T(8,128)(2,1)S(1)} %get-tuple-element.19), channel_id=1, source_target_pairs={{0,16},{16,32},{32,48},{48,64},{64,80},{80,96},{96,112},{1,17},{17... | collective-permute-start | bytes 884744 | tf_op jit(solution)/shard_map/ppermute | solution.py:319
  40.5 11.2 %all-to-all-start.1 = ((bf16[16,2,16,128]{3,2,1,0:T(8,128)(2,1)}), bf16[16,2,16,128]{3,2,1,0:T(8,128)(2,1)S(1)}, u32[]{:S(2)}, u32[]{:S(2)}) async-start(bf16[16,2,16,128]{3,2,1,0:T(8,128)(2,1)} %get-tuple-element.23), calls=%async_computation.1 | async-start | bytes 262144 | tf_op jit(solution)/shard_map/all_to_all | solution.py:325
  47.5 2.1 %copy-start.1 = (bf16[128,1024]{1,0:T(8,128)(2,1)S(1)}, bf16[128,1024]{1,0:T(8,128)(2,1)}, u32[]{:S(2)}) copy-start(bf16[128,1024]{1,0:T(8,128)(2,1)} %q_ref.3) | copy-start | bytes 786436
  47.7 6.9 %collective-permute-start.5 = (bf16[128,512]{1,0:T(8,128)(2,1)S(1)}, bf16[128,512]{1,0:T(8,128)(2,1)S(1)}, u32[]{:S(2)}, u32[]{:S(2)}) collective-permute-start(bf16[128,512]{1,0:T(8,128)(2,1)S(1)} %mate_join.1), channel_id=1, source_target_pairs={{0,2},{1,3},{2,0},{3,1},{4,6},{5,7},{6,4},{7,5},{8,10},{9,11},{10,... | collective-permute-start | bytes 393224 | tf_op jit(solution)/shard_map/ppermute | solution.py:332

commit v7 on v6

--- a/solution.py
+++ b/solution.py
@@ -74,6 +74,12 @@
         yield 2 * row + (lax.rem(block, 2) == lax.rem(kv, 2)).astype(jnp.int32)
 
 
+def beside_kernel(left_ref, right_ref, out_ref):
+    lanes = left_ref.shape[1]
+    out_ref[:, :lanes] = left_ref[...]
+    out_ref[:, lanes:] = right_ref[...]
+
+
 def turn(q_ref, group, out_ref):
     rows = q_ref.shape[0]
     heads = out_ref.shape[1] // rows
@@ -96,9 +102,9 @@
     plan_ref[...] = jnp.concatenate(plan, axis=0)
 
 
-def scan_keys(plan_ref, sets, q_refs, blocks, q_bases, k_base, acc, top, total, kept):
+def scan_keys(plan_ref, sets, q_ref, blocks, q_bases, k_base, acc, top, total, kept):
     rows = plan_ref.shape[1]
-    lanes = q_refs[0].shape[1]
+    lanes = q_ref.shape[1] // len(sets)
     heads = lanes // rows
     tile = 2 * rows * SPAN
     count = blocks[0][0].shape[0] // SPAN
@@ -125,9 +131,9 @@
             row = k_base + at * tile + lax.broadcasted_iota(jnp.int32, (rows, rows), 0)
             k_pos = [row + (2 * chip + core) * rows for chip in range(SPAN) for _, core in blocks]
             k_pos = jnp.concatenate(k_pos, axis=0)
-        for i, q_ref in enumerate(q_refs):
+        for i in range(len(sets)):
             where = slice(i * lanes, (i + 1) * lanes)
-            scores = jnp.dot(keys, q_ref[...], preferred_element_type=jnp.float32)
+            scores = jnp.dot(keys, q_ref[:, where], preferred_element_type=jnp.float32)
             if masked:
                 seen = (k_pos <= q_pos[i]) & (k_pos >= q_start[i])
                 scores = jnp.where(jnp.concatenate([seen] * heads, axis=1), scores, LOWEST)
@@ -138,7 +144,7 @@
 
     def second_pass(at, carry, several=1):
         values = jnp.concatenate([columns(at + i, slice(HD, 2 * HD)) for i in range(several)], axis=0)
-        for i in range(len(q_refs)):
+        for i in range(len(sets)):
             where = slice(i * lanes, (i + 1) * lanes)
             peak = jnp.maximum(top[:, where], 0.1 * LOWEST) * FACTOR
             scores = jnp.concatenate([kept[at + more, i] for more in range(several)], axis=0)
@@ -192,14 +198,14 @@
 
 
 def later_kernel(
-    plan_ref, q_ref, mate_ref, mine_ref, other_ref, part_ref, pages_ref, acc, top, total, kept, picked, sem
+    plan_ref, q_ref, mine_ref, other_ref, part_ref, pages_ref, acc, top, total, kept, picked, sem
 ):
     pick_pages(plan_ref, mine_ref, other_ref, picked)
     leave = pltpu.make_async_copy(picked, pages_ref, sem)
     leave.start()
     q_bases, k_base, core = bases(mine_ref.shape[1], 1)
     blocks = ((mine_ref, core), (other_ref, 1 - core))
-    scan_keys(plan_ref, (2, 3), (q_ref, mate_ref), blocks, q_bases, k_base, acc, top, total, kept)
+    scan_keys(plan_ref, (2, 3), q_ref, blocks, q_bases, k_base, acc, top, total, kept)
     part_ref[0:HD, :] = (acc[...] / jnp.maximum(total[...], 1e-30)).astype(jnp.bfloat16)
     stats = split_three(top[...]) + split_three(total[...])
     stats.append(jnp.zeros((STAT_ROWS - len(stats), acc.shape[1]), jnp.bfloat16))
@@ -227,7 +233,7 @@
 def mate_kernel(plan_ref, q_ref, mine_ref, other_ref, acc, top, total, kept):
     q_bases, k_base, core = bases(mine_ref.shape[1], 0)
     blocks = ((mine_ref, core), (other_ref, 1 - core))
-    scan_keys(plan_ref, (1,), (q_ref,), blocks, q_bases[1:], k_base, acc, top, total, kept)
+    scan_keys(plan_ref, (1,), q_ref, blocks, q_bases[1:], k_base, acc, top, total, kept)
 
 
 def mate_join_kernel(acc, top, total, part_ref, out_ref):
@@ -238,7 +244,7 @@
     turn(q_ref, lax.rem(lax.div(lax.axis_index("kv"), 2), 2), turned)
     q_bases, k_base, core = bases(mine_ref.shape[1], 0)
     blocks = ((mine_ref, core), (other_ref, 1 - core))
-    scan_keys(plan_ref, (0,), (turned,), blocks, q_bases[:1], k_base, acc, top, total, kept)
+    scan_keys(plan_ref, (0,), turned, blocks, q_bases[:1], k_base, acc, top, total, kept)
     join(acc, top, total, part_ref, 0, out_ref)
 
 
@@ -301,7 +307,8 @@
     later = lax.ppermute(keep, "pb", [(i + 1, i) for i in range(n_pb - 1)])
     steps = [((z + 1) * n_kv + (i ^ 2), z * n_kv + i) for z in range(n_pb - 1) for i in range(n_kv)]
     later_mate = lax.ppermute(give, ("pb", "kv"), steps)
-    mine, later, later_mate = lax.optimization_barrier((mine, later, later_mate))
+    mine, later = lax.optimization_barrier((mine, later))
+    later = call(beside_kernel, shape((HD, 2 * lanes), jnp.bfloat16), [VMEM] * 2, "beside", LONG)(later, later_mate)
     other = lax.ppermute(mine, "kv", [(i, i ^ 1) for i in range(n_kv)])
 
     def scratch(sets):
@@ -313,9 +320,9 @@
     part, pages = call(
         later_kernel,
         (shape((HD + STAT_ROWS, 2 * lanes), jnp.bfloat16), shape((n_slots, 2, PAGE, HD), jnp.bfloat16)),
-        [VMEM] * 5, "later_rows", LONG,
+        [VMEM] * 4, "later_rows", LONG,
         state + [kept, pltpu.VMEM((n_slots, 2, PAGE, HD), jnp.bfloat16), pltpu.SemaphoreType.DMA], out=(VMEM, ANY),
-    )(plan, later, later_mate, mine, other)
+    )(plan, later, mine, other)
     back = lax.ppermute(part, "pb", [(i, i + 1) for i in range(n_pb - 1)])
     sharing = [
         [head * n_kv + (2 * pair + chip) * 2 + core for head in range(n_head) for chip in range(2)]

time: 55.8 us -> 55.8 us (level)
  the two profiles are of different devices: /device:TPU:152 before, /device:TPU:194 now
where the time goes in v7:
time: 55.8 us; the launch traced here: 55.7 us
  starting transfers between devices  34.3 us (61%)
  waiting for transfers between devices  12.4 us (22%)
  Pallas kernels  8.21 us (15%)
  between operations  0.8 us (1%)
    ppermute x1, starting transfers between devices, body(): back = lax.ppermute(part, 'pb', [(i, i + 1) for i in range(n_pb - 1)])  8.15 us
    all_to_all x1, starting transfers between devices, body(): mine = lax.all_to_all(sent, 'kv', 0, 0, tiled=True, axis_index_groups=ring)  7.24 us
    all_to_all x1, waiting for transfers between devices, body(): mine = lax.all_to_all(sent, 'kv', 0, 0, tiled=True, axis_index_groups=ring)  7.07 us
    all_to_all x1, starting transfers between devices, body(): lax.all_to_all(pages, ('head', 'kv'), 0, 0, tiled=True, axis_index_groups...  5.88 us
    ppermute x1, starting transfers between devices, body(): mate_out = lax.ppermute(mate_out, 'kv', to_mate)  3.37 us
    ppermute x1, starting transfers between devices, body(): later_mate = lax.ppermute(give, ('pb', 'kv'), steps)  3.01 us
    ppermute x1, starting transfers between devices, body(): mate = lax.ppermute(give, 'kv', to_mate)  2.83 us
    ppermute x1, waiting for transfers between devices, body(): mate_out = lax.ppermute(mate_out, 'kv', to_mate)  2.53 us
  transfers between devices with their start and end apart: 8, of which 5 were waited for; matrix products, arithmetic and copies ran while one was open for 0% of the time, Pallas kernels for 10%

profile of v7, /device:TPU:194, one launch (start us, length us, event | category | flops | bytes accessed | tf_op | source)
XLA Modules:
  0.0 55.7 jit_solution(14091767278922332479)
XLA Ops:
  0.6 1.8 %spread_keys.1 = bf16[8,128,256]{2,1,0:T(8,128)(2,1)} custom-call(bf16[128,256]{1,0:T(8,128)(2,1)} %keys_ref.1, bf16[128,256]{1,0:T(8,128)(2,1)} %values_ref.1), custom_call_target="tpu_custom_call" | custom-call | flops 1024 | bytes 3145728 | tf_op jit(solution)/shard_map/spread_keys/pallas_call | solution.py:294
  2.4 0.0 copy-start
  2.4 0.0 copy-start.2
  2.4 0.0 copy-start.3
  2.4 7.2 %all-to-all-start = ((bf16[8,128,256]{2,1,0:T(8,128)(2,1)}), bf16[8,128,256]{2,1,0:T(8,128)(2,1)S(1)}, u32[]{:S(2)}, u32[]{:S(2)}) async-start(bf16[8,128,256]{2,1,0:T(8,128)(2,1)} %spread_keys.1), calls=%async_computation | async-start | bytes 1048576 | tf_op jit(solution)/shard_map/all_to_all | solution.py:299
  9.7 0.0 copy-done
  9.7 0.0 copy-done.2
  9.7 0.0 copy-done.3
  9.7 1.5 %turn_queries.1 = (bf16[128,512]{1,0:T(8,128)(2,1)S(1)}, bf16[128,512]{1,0:T(8,128)(2,1)}, s32[8,128]{1,0:T(8,128)S(1)}) custom-call(s32[17]{0:T(128)S(1)} %copy-done.3, s32[1024]{0:T(1024)S(1)} %copy-done.2, bf16[128,1024]{1,0:T(8,128)(2,1)S(1)} %copy-done), custom_call_target="tpu_custom_call" | custom-call | flops 1048576 | bytes 3145728 | tf_op jit(solution)/shard_map/turn_queries/pallas_call | solution.py:303
  11.2 1.9 %collective-permute-start = (bf16[128,512]{1,0:T(8,128)(2,1)S(1)}, bf16[128,512]{1,0:T(8,128)(2,1)S(1)}, u32[]{:S(2)}, u32[]{:S(2)}) collective-permute-start(bf16[128,512]{1,0:T(8,128)(2,1)S(1)} %get-tuple-element.13), channel_id=1, source_target_pairs={{16,0},{32,16},{48,32},{64,48},{80,64},{96,80},{112,96},{17,1},{33... | collective-permute-start | bytes 393224 | tf_op jit(solution)/shard_map/ppermute | solution.py:307
  13.2 3.0 %collective-permute-start.2 = (bf16[128,512]{1,0:T(8,128)(2,1)}, bf16[128,512]{1,0:T(8,128)(2,1)S(1)}, u32[]{:S(2)}, u32[]{:S(2)}) collective-permute-start(bf16[128,512]{1,0:T(8,128)(2,1)} %get-tuple-element.16), channel_id=1, source_target_pairs={{18,0},{19,1},{16,2},{17,3},{22,4},{23,5},{20,6},{21,7},{26,8},{27... | collective-permute-start | bytes 393224 | tf_op jit(solution)/shard_map/ppermute | solution.py:309
  16.2 2.8 %collective-permute-start.4 = (bf16[128,512]{1,0:T(8,128)(2,1)}, bf16[128,512]{1,0:T(8,128)(2,1)}, u32[]{:S(2)}, u32[]{:S(2)}) collective-permute-start(bf16[128,512]{1,0:T(8,128)(2,1)} %get-tuple-element.16), channel_id=1, source_target_pairs={{0,2},{1,3},{2,0},{3,1},{4,6},{5,7},{6,4},{7,5},{8,10},{9,11},{10,... | collective-permute-start | bytes 393224 | tf_op jit(solution)/shard_map/ppermute | solution.py:306
  19.0 0.9 %collective-permute-done.left_ref = bf16[128,512]{1,0:T(8,128)(2,1)S(1)} collective-permute-done((bf16[128,512]{1,0:T(8,128)(2,1)S(1)}, bf16[128,512]{1,0:T(8,128)(2,1)S(1)}, u32[]{:S(2)}, u32[]{:S(2)}) %collective-permute-start) | collective-permute-done | bytes 131104 | tf_op jit(solution)/shard_map/ppermute | solution.py:307
  19.9 7.1 %all-to-all-done.mine_ref = bf16[8,128,256]{2,1,0:T(8,128)(2,1)S(1)} async-done(((bf16[8,128,256]{2,1,0:T(8,128)(2,1)}), bf16[8,128,256]{2,1,0:T(8,128)(2,1)S(1)}, u32[]{:S(2)}, u32[]{:S(2)}) %all-to-all-start) | async-done | bytes 524320 | tf_op jit(solution)/shard_map/all_to_all | solution.py:299
  27.0 1.9 %collective-permute-start.1 = (bf16[8,128,256]{2,1,0:T(8,128)(2,1)S(1)}, bf16[8,128,256]{2,1,0:T(8,128)(2,1)S(1)}, u32[]{:S(2)}, u32[]{:S(2)}) collective-permute-start(bf16[8,128,256]{2,1,0:T(8,128)(2,1)S(1)} %all-to-all-done.mine_ref), channel_id=1, source_target_pairs={{0,1},{1,0},{2,3},{3,2},{4,5},{5,4},{6,7},{7,6},{8,9},{9,8},{10,11... | collective-permute-start | bytes 1572872 | tf_op jit(solution)/shard_map/ppermute | solution.py:312
  28.9 1.6 %collective-permute-done.2.right_ref = bf16[128,512]{1,0:T(8,128)(2,1)S(1)} collective-permute-done((bf16[128,512]{1,0:T(8,128)(2,1)}, bf16[128,512]{1,0:T(8,128)(2,1)S(1)}, u32[]{:S(2)}, u32[]{:S(2)}) %collective-permute-start.2) | collective-permute-done | bytes 131104 | tf_op jit(solution)/shard_map/ppermute | solution.py:309
  30.5 0.3 collective-permute-done.1.other_ref
  30.8 1.4 %later_rows.1 = (bf16[144,1024]{1,0:T(8,128)(2,1)S(1)}, bf16[16,2,16,128]{3,2,1,0:T(8,128)(2,1)}) custom-call(s32[8,128]{1,0:T(8,128)S(1)} %get-tuple-element.12.plan_ref, bf16[128,1024]{1,0:T(8,128)(2,1)S(1)} %beside.1.q_ref, bf16[8,128,256]{2,1,0:T(8,128)(2,1)S(1)} %all-to-all-done.mine_ref, bf16[8,128,256]{2,1,0:T(8,128)(2,1)S(1)} %collective-permute-done.1.other_ref), custom_call_target="tpu_custom_call" | custom-call | flops 99999997952 | bytes 3145728 | tf_op jit(solution)/shard_map/later_rows/pallas_call | solution.py:320
  32.2 8.2 %collective-permute-start.3 = (bf16[144,1024]{1,0:T(8,128)(2,1)S(1)}, bf16[144,1024]{1,0:T(8,128)(2,1)S(1)}, u32[]{:S(2)}, u32[]{:S(2)}) collective-permute-start(bf16[144,1024]{1,0:T(8,128)(2,1)S(1)} %get-tuple-element.17), channel_id=1, source_target_pairs={{0,16},{16,32},{32,48},{48,64},{64,80},{80,96},{96,112},{1,17},{17... | collective-permute-start | bytes 884744 | tf_op jit(solution)/shard_map/ppermute | solution.py:326
  40.3 5.9 %all-to-all-start.1 = ((bf16[16,2,16,128]{3,2,1,0:T(8,128)(2,1)}), bf16[16,2,16,128]{3,2,1,0:T(8,128)(2,1)S(1)}, u32[]{:S(2)}, u32[]{:S(2)}) async-start(bf16[16,2,16,128]{3,2,1,0:T(8,128)(2,1)} %get-tuple-element.21), calls=%async_computation.1 | async-start | bytes 262144 | tf_op jit(solution)/shard_map/all_to_all | solution.py:332
  46.2 0.0 collective-permute-done.4.q_ref
  46.2 1.7 %mate_row.1 = (f32[128,512]{1,0:T(8,128)S(1)}, f32[1,512]{1,0:T(1,128)S(1)}, f32[1,512]{1,0:T(1,128)S(1)}) custom-call(s32[8,128]{1,0:T(8,128)S(1)} %get-tuple-element.12.plan_ref, bf16[128,512]{1,0:T(8,128)(2,1)} %collective-permute-done.4.q_ref, bf16[8,128,256]{2,1,0:T(8,128)(2,1)S(1)} %all-to-all-done.mine_ref, ...), custom_call_target="tpu_custom_call" | custom-call | flops 99999997952 | bytes 3145728 | tf_op jit(solution)/shard_map/mate_row/pallas_call | solution.py:335
  47.9 0.0 collective-permute-done.3.part_ref
  47.9 0.0 copy-start.1
  47.9 0.1 mate_join.1
  48.1 3.4 %collective-permute-start.5 = (bf16[128,512]{1,0:T(8,128)(2,1)S(1)}, bf16[128,512]{1,0:T(8,128)(2,1)S(1)}, u32[]{:S(2)}, u32[]{:S(2)}) collective-permute-start(bf16[128,512]{1,0:T(8,128)(2,1)S(1)} %mate_join.1), channel_id=1, source_target_pairs={{0,2},{1,3},{2,0},{3,1},{4,6},{5,7},{6,4},{7,5},{8,10},{9,11},{10,... | collective-permute-start | bytes 393224 | tf_op jit(solution)/shard_map/ppermute | solution.py:339
  51.4 0.0 copy-done.1
  51.4 0.9 %own_row.1.own_ref = bf16[128,512]{1,0:T(8,128)(2,1)S(1)} custom-call(s32[8,128]{1,0:T(8,128)S(1)} %get-tuple-element.12.plan_ref, bf16[128,1024]{1,0:T(8,128)(2,1)S(1)} %copy-done.1, bf16[8,128,256]{2,1,0:T(8,128)(2,1)S(1)} %all-to-all-done.mine_ref, bf16[8,128,256]{2,1,0:T(8,128)(2,1)S(1)} %collective-permute-done.1.other_ref, ...), custom_call_target="tpu_custom_call" | custom-call | flops 1073741824 | bytes 3145728 | tf_op jit(solution)/shard_map/own_row/pallas_call | solution.py:340
  52.4 0.0 all-to-all-done.1.pages_ref
  52.4 2.5 %collective-permute-done.5.mate_ref = bf16[128,512]{1,0:T(8,128)(2,1)S(1)} collective-permute-done((bf16[128,512]{1,0:T(8,128)(2,1)S(1)}, bf16[128,512]{1,0:T(8,128)(2,1)S(1)}, u32[]{:S(2)}, u32[]{:S(2)}) %collective-permute-start.5) | collective-permute-done | bytes 131104 | tf_op jit(solution)/shard_map/ppermute | solution.py:339
  54.9 0.8 %place.1 = (bf16[128,1024]{1,0:T(8,128)(2,1)}, bf16[2,2,16,1024]{3,2,1,0:T(8,128)(2,1)}) custom-call(bf16[128,512]{1,0:T(8,128)(2,1)S(1)} %own_row.1.own_ref, bf16[128,512]{1,0:T(8,128)(2,1)S(1)} %collective-permute-done.5.mate_ref, bf16[16,2,16,128]{3,2,1,0:T(8,128)(2,1)S(1)} %all-to-all-done.1.pages_ref), custom_call_target="tpu_custom_call" | custom-call | flops 1024 | bytes 3145728 | tf_op jit(solution)/shard_map/place/pallas_call | solution.py:344
  (1 shorter events, 0.0 us)
Async XLA Ops:
  2.4 7.3 %copy-start = (bf16[128,1024]{1,0:T(8,128)(2,1)S(1)}, bf16[128,1024]{1,0:T(8,128)(2,1)}, u32[]{:S(2)}) copy-start(bf16[128,1024]{1,0:T(8,128)(2,1)} %q_ref.3) | copy-start | bytes 786436
  2.4 7.3 %copy-start.2 = (s32[1024]{0:T(1024)S(1)}, s32[1024]{0:T(1024)}, u32[]{:S(2)}) copy-start(s32[1024]{0:T(1024)} %table_ref.1) | copy-start | bytes 12292
  2.4 7.3 %copy-start.3 = (s32[17]{0:T(128)S(1)}, s32[17]{0:T(128)}, u32[]{:S(2)}) copy-start(s32[17]{0:T(128)} %lengths_ref.1) | copy-start | bytes 208
  2.4 24.6 %all-to-all-start = ((bf16[8,128,256]{2,1,0:T(8,128)(2,1)}), bf16[8,128,256]{2,1,0:T(8,128)(2,1)S(1)}, u32[]{:S(2)}, u32[]{:S(2)}) async-start(bf16[8,128,256]{2,1,0:T(8,128)(2,1)} %spread_keys.1), calls=%async_computation | async-start | bytes 1048576 | tf_op jit(solution)/shard_map/all_to_all | solution.py:299
  11.2 8.7 %collective-permute-start = (bf16[128,512]{1,0:T(8,128)(2,1)S(1)}, bf16[128,512]{1,0:T(8,128)(2,1)S(1)}, u32[]{:S(2)}, u32[]{:S(2)}) collective-permute-start(bf16[128,512]{1,0:T(8,128)(2,1)S(1)} %get-tuple-element.13), channel_id=1, source_target_pairs={{16,0},{32,16},{48,32},{64,48},{80,64},{96,80},{112,96},{17,1},{33... | collective-permute-start | bytes 393224 | tf_op jit(solution)/shard_map/ppermute | solution.py:307
  13.2 17.3 %collective-permute-start.2 = (bf16[128,512]{1,0:T(8,128)(2,1)}, bf16[128,512]{1,0:T(8,128)(2,1)S(1)}, u32[]{:S(2)}, u32[]{:S(2)}) collective-permute-start(bf16[128,512]{1,0:T(8,128)(2,1)} %get-tuple-element.16), channel_id=1, source_target_pairs={{18,0},{19,1},{16,2},{17,3},{22,4},{23,5},{20,6},{21,7},{26,8},{27... | collective-permute-start | bytes 393224 | tf_op jit(solution)/shard_map/ppermute | solution.py:309
  16.2 30.0 %collective-permute-start.4 = (bf16[128,512]{1,0:T(8,128)(2,1)}, bf16[128,512]{1,0:T(8,128)(2,1)}, u32[]{:S(2)}, u32[]{:S(2)}) collective-permute-start(bf16[128,512]{1,0:T(8,128)(2,1)} %get-tuple-element.16), channel_id=1, source_target_pairs={{0,2},{1,3},{2,0},{3,1},{4,6},{5,7},{6,4},{7,5},{8,10},{9,11},{10,... | collective-permute-start | bytes 393224 | tf_op jit(solution)/shard_map/ppermute | solution.py:306
  27.0 3.8 %collective-permute-start.1 = (bf16[8,128,256]{2,1,0:T(8,128)(2,1)S(1)}, bf16[8,128,256]{2,1,0:T(8,128)(2,1)S(1)}, u32[]{:S(2)}, u32[]{:S(2)}) collective-permute-start(bf16[8,128,256]{2,1,0:T(8,128)(2,1)S(1)} %all-to-all-done.mine_ref), channel_id=1, source_target_pairs={{0,1},{1,0},{2,3},{3,2},{4,5},{5,4},{6,7},{7,6},{8,9},{9,8},{10,11... | collective-permute-start | bytes 1572872 | tf_op jit(solution)/shard_map/ppermute | solution.py:312
  32.2 15.7 %collective-permute-start.3 = (bf16[144,1024]{1,0:T(8,128)(2,1)S(1)}, bf16[144,1024]{1,0:T(8,128)(2,1)S(1)}, u32[]{:S(2)}, u32[]{:S(2)}) collective-permute-start(bf16[144,1024]{1,0:T(8,128)(2,1)S(1)} %get-tuple-element.17), channel_id=1, source_target_pairs={{0,16},{16,32},{32,48},{48,64},{64,80},{80,96},{96,112},{1,17},{17... | collective-permute-start | bytes 884744 | tf_op jit(solution)/shard_map/ppermute | solution.py:326
  40.3 12.1 %all-to-all-start.1 = ((bf16[16,2,16,128]{3,2,1,0:T(8,128)(2,1)}), bf16[16,2,16,128]{3,2,1,0:T(8,128)(2,1)S(1)}, u32[]{:S(2)}, u32[]{:S(2)}) async-start(bf16[16,2,16,128]{3,2,1,0:T(8,128)(2,1)} %get-tuple-element.21), calls=%async_computation.1 | async-start | bytes 262144 | tf_op jit(solution)/shard_map/all_to_all | solution.py:332
  47.9 3.5 %copy-start.1 = (bf16[128,1024]{1,0:T(8,128)(2,1)S(1)}, bf16[128,1024]{1,0:T(8,128)(2,1)}, u32[]{:S(2)}) copy-start(bf16[128,1024]{1,0:T(8,128)(2,1)} %q_ref.3) | copy-start | bytes 786436
  48.1 6.9 %collective-permute-start.5 = (bf16[128,512]{1,0:T(8,128)(2,1)S(1)}, bf16[128,512]{1,0:T(8,128)(2,1)S(1)}, u32[]{:S(2)}, u32[]{:S(2)}) collective-permute-start(bf16[128,512]{1,0:T(8,128)(2,1)S(1)} %mate_join.1), channel_id=1, source_target_pairs={{0,2},{1,3},{2,0},{3,1},{4,6},{5,7},{6,4},{7,5},{8,10},{9,11},{10,... | collective-permute-start | bytes 393224 | tf_op jit(solution)/shard_map/ppermute | solution.py:339

commit v8 on v7

--- a/solution.py
+++ b/solution.py
@@ -307,7 +307,6 @@
     later = lax.ppermute(keep, "pb", [(i + 1, i) for i in range(n_pb - 1)])
     steps = [((z + 1) * n_kv + (i ^ 2), z * n_kv + i) for z in range(n_pb - 1) for i in range(n_kv)]
     later_mate = lax.ppermute(give, ("pb", "kv"), steps)
-    mine, later = lax.optimization_barrier((mine, later))
     later = call(beside_kernel, shape((HD, 2 * lanes), jnp.bfloat16), [VMEM] * 2, "beside", LONG)(later, later_mate)
     other = lax.ppermute(mine, "kv", [(i, i ^ 1) for i in range(n_kv)])
 

time: 55.8 us -> 54.7 us (0.980)
  the two profiles are of different devices: /device:TPU:194 before, /device:TPU:130 now
where the time goes in v8:
time: 54.7 us; the launch traced here: 54.5 us
  starting transfers between devices  32.3 us (59%)
  waiting for transfers between devices  12.4 us (23%)
  Pallas kernels  9.04 us (17%)
  between operations  0.8 us (1%)
    all_to_all x1, waiting for transfers between devices, body(): mine = lax.all_to_all(sent, 'kv', 0, 0, tiled=True, axis_index_groups=ring)  7.98 us
    all_to_all x1, starting transfers between devices, body(): mine = lax.all_to_all(sent, 'kv', 0, 0, tiled=True, axis_index_groups=ring)  7.24 us
    ppermute x1, starting transfers between devices, body(): back = lax.ppermute(part, 'pb', [(i, i + 1) for i in range(n_pb - 1)])  6.1 us
    all_to_all x1, starting transfers between devices, body(): lax.all_to_all(pages, ('head', 'kv'), 0, 0, tiled=True, axis_index_groups...  5.88 us
    ppermute x1, starting transfers between devices, body(): mate_out = lax.ppermute(mate_out, 'kv', to_mate)  3.38 us
    ppermute x1, starting transfers between devices, body(): later_mate = lax.ppermute(give, ('pb', 'kv'), steps)  3 us
    ppermute x1, starting transfers between devices, body(): mate = lax.ppermute(give, 'kv', to_mate)  2.83 us
    ppermute x1, waiting for transfers between devices, body(): mate_out = lax.ppermute(mate_out, 'kv', to_mate)  2.52 us
  transfers between devices with their start and end apart: 8, of which 4 were waited for; matrix products, arithmetic and copies ran while one was open for 0% of the time, Pallas kernels for 12%

profile of v8, /device:TPU:130, one launch (start us, length us, event | category | flops | bytes accessed | tf_op | source)
XLA Modules:
  0.0 54.5 jit_solution(639367594024962958)
XLA Ops:
  0.6 1.8 %spread_keys.1 = bf16[8,128,256]{2,1,0:T(8,128)(2,1)} custom-call(bf16[128,256]{1,0:T(8,128)(2,1)} %keys_ref.1, bf16[128,256]{1,0:T(8,128)(2,1)} %values_ref.1), custom_call_target="tpu_custom_call" | custom-call | flops 1024 | bytes 3145728 | tf_op jit(solution)/shard_map/spread_keys/pallas_call | solution.py:294
  2.4 0.0 copy-start
  2.4 0.0 copy-start.2
  2.4 0.0 copy-start.3
  2.4 7.2 %all-to-all-start = ((bf16[8,128,256]{2,1,0:T(8,128)(2,1)}), bf16[8,128,256]{2,1,0:T(8,128)(2,1)S(1)}, u32[]{:S(2)}, u32[]{:S(2)}) async-start(bf16[8,128,256]{2,1,0:T(8,128)(2,1)} %spread_keys.1), calls=%async_computation | async-start | bytes 1048576 | tf_op jit(solution)/shard_map/all_to_all | solution.py:299
  9.7 0.0 copy-done
  9.7 0.0 copy-done.2
  9.7 0.0 copy-done.3
  9.7 1.5 %turn_queries.1 = (bf16[128,512]{1,0:T(8,128)(2,1)S(1)}, bf16[128,512]{1,0:T(8,128)(2,1)}, s32[8,128]{1,0:T(8,128)S(1)}) custom-call(s32[17]{0:T(128)S(1)} %copy-done.3, s32[1024]{0:T(1024)S(1)} %copy-done.2, bf16[128,1024]{1,0:T(8,128)(2,1)S(1)} %copy-done), custom_call_target="tpu_custom_call" | custom-call | flops 1048576 | bytes 3145728 | tf_op jit(solution)/shard_map/turn_queries/pallas_call | solution.py:303
  11.2 3.0 %collective-permute-start.2 = (bf16[128,512]{1,0:T(8,128)(2,1)}, bf16[128,512]{1,0:T(8,128)(2,1)S(1)}, u32[]{:S(2)}, u32[]{:S(2)}) collective-permute-start(bf16[128,512]{1,0:T(8,128)(2,1)} %get-tuple-element.12), channel_id=1, source_target_pairs={{18,0},{19,1},{16,2},{17,3},{22,4},{23,5},{20,6},{21,7},{26,8},{27... | collective-permute-start | bytes 393224 | tf_op jit(solution)/shard_map/ppermute | solution.py:309
  14.2 1.9 %collective-permute-start.1 = (bf16[128,512]{1,0:T(8,128)(2,1)S(1)}, bf16[128,512]{1,0:T(8,128)(2,1)S(1)}, u32[]{:S(2)}, u32[]{:S(2)}) collective-permute-start(bf16[128,512]{1,0:T(8,128)(2,1)S(1)} %get-tuple-element.11), channel_id=1, source_target_pairs={{16,0},{32,16},{48,32},{64,48},{80,64},{96,80},{112,96},{17,1},{33... | collective-permute-start | bytes 393224 | tf_op jit(solution)/shard_map/ppermute | solution.py:307
  16.2 2.8 %collective-permute-start.4 = (bf16[128,512]{1,0:T(8,128)(2,1)}, bf16[128,512]{1,0:T(8,128)(2,1)}, u32[]{:S(2)}, u32[]{:S(2)}) collective-permute-start(bf16[128,512]{1,0:T(8,128)(2,1)} %get-tuple-element.12), channel_id=1, source_target_pairs={{0,2},{1,3},{2,0},{3,1},{4,6},{5,7},{6,4},{7,5},{8,10},{9,11},{10,... | collective-permute-start | bytes 393224 | tf_op jit(solution)/shard_map/ppermute | solution.py:306
  19.0 8.0 %all-to-all-done.mine_ref = bf16[8,128,256]{2,1,0:T(8,128)(2,1)S(1)} async-done(((bf16[8,128,256]{2,1,0:T(8,128)(2,1)}), bf16[8,128,256]{2,1,0:T(8,128)(2,1)S(1)}, u32[]{:S(2)}, u32[]{:S(2)}) %all-to-all-start) | async-done | bytes 524320 | tf_op jit(solution)/shard_map/all_to_all | solution.py:299
  27.0 1.9 %collective-permute-start = (bf16[8,128,256]{2,1,0:T(8,128)(2,1)S(1)}, bf16[8,128,256]{2,1,0:T(8,128)(2,1)S(1)}, u32[]{:S(2)}, u32[]{:S(2)}) collective-permute-start(bf16[8,128,256]{2,1,0:T(8,128)(2,1)S(1)} %all-to-all-done.mine_ref), channel_id=1, source_target_pairs={{0,1},{1,0},{2,3},{3,2},{4,5},{5,4},{6,7},{7,6},{8,9},{9,8},{10,11... | collective-permute-start | bytes 1572872 | tf_op jit(solution)/shard_map/ppermute | solution.py:311
  28.9 0.4 collective-permute-done.2.right_ref
  29.3 0.0 collective-permute-done.1.left_ref
  29.3 1.5 %collective-permute-done.other_ref = bf16[8,128,256]{2,1,0:T(8,128)(2,1)S(1)} collective-permute-done((bf16[8,128,256]{2,1,0:T(8,128)(2,1)S(1)}, bf16[8,128,256]{2,1,0:T(8,128)(2,1)S(1)}, u32[]{:S(2)}, u32[]{:S(2)}) %collective-permute-start) | collective-permute-done | bytes 524320 | tf_op jit(solution)/shard_map/ppermute | solution.py:311
  30.8 2.2 %later_rows.1 = (bf16[144,1024]{1,0:T(8,128)(2,1)S(1)}, bf16[16,2,16,128]{3,2,1,0:T(8,128)(2,1)}) custom-call(s32[8,128]{1,0:T(8,128)S(1)} %get-tuple-element.10.plan_ref, bf16[128,1024]{1,0:T(8,128)(2,1)S(1)} %beside.1.q_ref, bf16[8,128,256]{2,1,0:T(8,128)(2,1)S(1)} %all-to-all-done.mine_ref, bf16[8,128,256]{2,1,0:T(8,128)(2,1)S(1)} %collective-permute-done.other_ref), custom_call_target="tpu_custom_call" | custom-call | flops 99999997952 | bytes 3145728 | tf_op jit(solution)/shard_map/later_rows/pallas_call | solution.py:319
  33.0 6.1 %collective-permute-start.3 = (bf16[144,1024]{1,0:T(8,128)(2,1)S(1)}, bf16[144,1024]{1,0:T(8,128)(2,1)S(1)}, u32[]{:S(2)}, u32[]{:S(2)}) collective-permute-start(bf16[144,1024]{1,0:T(8,128)(2,1)S(1)} %get-tuple-element.13), channel_id=1, source_target_pairs={{0,16},{16,32},{32,48},{48,64},{64,80},{80,96},{96,112},{1,17},{17... | collective-permute-start | bytes 884744 | tf_op jit(solution)/shard_map/ppermute | solution.py:325
  39.1 5.9 %all-to-all-start.1 = ((bf16[16,2,16,128]{3,2,1,0:T(8,128)(2,1)}), bf16[16,2,16,128]{3,2,1,0:T(8,128)(2,1)S(1)}, u32[]{:S(2)}, u32[]{:S(2)}) async-start(bf16[16,2,16,128]{3,2,1,0:T(8,128)(2,1)} %get-tuple-element.17), calls=%async_computation.1 | async-start | bytes 262144 | tf_op jit(solution)/shard_map/all_to_all | solution.py:331
  45.0 0.0 collective-permute-done.4.q_ref
  45.0 1.7 %mate_row.1 = (f32[128,512]{1,0:T(8,128)S(1)}, f32[1,512]{1,0:T(1,128)S(1)}, f32[1,512]{1,0:T(1,128)S(1)}) custom-call(s32[8,128]{1,0:T(8,128)S(1)} %get-tuple-element.10.plan_ref, bf16[128,512]{1,0:T(8,128)(2,1)} %collective-permute-done.4.q_ref, bf16[8,128,256]{2,1,0:T(8,128)(2,1)S(1)} %all-to-all-done.mine_ref, ...), custom_call_target="tpu_custom_call" | custom-call | flops 99999997952 | bytes 3145728 | tf_op jit(solution)/shard_map/mate_row/pallas_call | solution.py:334
  46.7 0.0 collective-permute-done.3.part_ref
  46.7 0.0 copy-start.1
  46.7 0.1 mate_join.1
  46.8 3.4 %collective-permute-start.5 = (bf16[128,512]{1,0:T(8,128)(2,1)S(1)}, bf16[128,512]{1,0:T(8,128)(2,1)S(1)}, u32[]{:S(2)}, u32[]{:S(2)}) collective-permute-start(bf16[128,512]{1,0:T(8,128)(2,1)S(1)} %mate_join.1), channel_id=1, source_target_pairs={{0,2},{1,3},{2,0},{3,1},{4,6},{5,7},{6,4},{7,5},{8,10},{9,11},{10,... | collective-permute-start | bytes 393224 | tf_op jit(solution)/shard_map/ppermute | solution.py:338
  50.2 0.0 copy-done.1
  50.2 0.9 %own_row.1.own_ref = bf16[128,512]{1,0:T(8,128)(2,1)S(1)} custom-call(s32[8,128]{1,0:T(8,128)S(1)} %get-tuple-element.10.plan_ref, bf16[128,1024]{1,0:T(8,128)(2,1)S(1)} %copy-done.1, bf16[8,128,256]{2,1,0:T(8,128)(2,1)S(1)} %all-to-all-done.mine_ref, bf16[8,128,256]{2,1,0:T(8,128)(2,1)S(1)} %collective-permute-done.other_ref, ...), custom_call_target="tpu_custom_call" | custom-call | flops 1073741824 | bytes 3145728 | tf_op jit(solution)/shard_map/own_row/pallas_call | solution.py:339
  51.2 0.0 all-to-all-done.1.pages_ref
  51.2 2.5 %collective-permute-done.5.mate_ref = bf16[128,512]{1,0:T(8,128)(2,1)S(1)} collective-permute-done((bf16[128,512]{1,0:T(8,128)(2,1)S(1)}, bf16[128,512]{1,0:T(8,128)(2,1)S(1)}, u32[]{:S(2)}, u32[]{:S(2)}) %collective-permute-start.5) | collective-permute-done | bytes 131104 | tf_op jit(solution)/shard_map/ppermute | solution.py:338
  53.7 0.8 %place.1 = (bf16[128,1024]{1,0:T(8,128)(2,1)}, bf16[2,2,16,1024]{3,2,1,0:T(8,128)(2,1)}) custom-call(bf16[128,512]{1,0:T(8,128)(2,1)S(1)} %own_row.1.own_ref, bf16[128,512]{1,0:T(8,128)(2,1)S(1)} %collective-permute-done.5.mate_ref, bf16[16,2,16,128]{3,2,1,0:T(8,128)(2,1)S(1)} %all-to-all-done.1.pages_ref), custom_call_target="tpu_custom_call" | custom-call | flops 1024 | bytes 3145728 | tf_op jit(solution)/shard_map/place/pallas_call | solution.py:343
  (1 shorter events, 0.0 us)
Async XLA Ops:
  2.4 7.3 %copy-start = (bf16[128,1024]{1,0:T(8,128)(2,1)S(1)}, bf16[128,1024]{1,0:T(8,128)(2,1)}, u32[]{:S(2)}) copy-start(bf16[128,1024]{1,0:T(8,128)(2,1)} %q_ref.3) | copy-start | bytes 786436
  2.4 7.3 %copy-start.2 = (s32[1024]{0:T(1024)S(1)}, s32[1024]{0:T(1024)}, u32[]{:S(2)}) copy-start(s32[1024]{0:T(1024)} %table_ref.1) | copy-start | bytes 12292
  2.4 7.3 %copy-start.3 = (s32[17]{0:T(128)S(1)}, s32[17]{0:T(128)}, u32[]{:S(2)}) copy-start(s32[17]{0:T(128)} %lengths_ref.1) | copy-start | bytes 208
  2.4 24.6 %all-to-all-start = ((bf16[8,128,256]{2,1,0:T(8,128)(2,1)}), bf16[8,128,256]{2,1,0:T(8,128)(2,1)S(1)}, u32[]{:S(2)}, u32[]{:S(2)}) async-start(bf16[8,128,256]{2,1,0:T(8,128)(2,1)} %spread_keys.1), calls=%async_computation | async-start | bytes 1048576 | tf_op jit(solution)/shard_map/all_to_all | solution.py:299
  11.2 18.0 %collective-permute-start.2 = (bf16[128,512]{1,0:T(8,128)(2,1)}, bf16[128,512]{1,0:T(8,128)(2,1)S(1)}, u32[]{:S(2)}, u32[]{:S(2)}) collective-permute-start(bf16[128,512]{1,0:T(8,128)(2,1)} %get-tuple-element.12), channel_id=1, source_target_pairs={{18,0},{19,1},{16,2},{17,3},{22,4},{23,5},{20,6},{21,7},{26,8},{27... | collective-permute-start | bytes 393224 | tf_op jit(solution)/shard_map/ppermute | solution.py:309
  14.2 15.0 %collective-permute-start.1 = (bf16[128,512]{1,0:T(8,128)(2,1)S(1)}, bf16[128,512]{1,0:T(8,128)(2,1)S(1)}, u32[]{:S(2)}, u32[]{:S(2)}) collective-permute-start(bf16[128,512]{1,0:T(8,128)(2,1)S(1)} %get-tuple-element.11), channel_id=1, source_target_pairs={{16,0},{32,16},{48,32},{64,48},{80,64},{96,80},{112,96},{17,1},{33... | collective-permute-start | bytes 393224 | tf_op jit(solution)/shard_map/ppermute | solution.py:307
  16.2 28.8 %collective-permute-start.4 = (bf16[128,512]{1,0:T(8,128)(2,1)}, bf16[128,512]{1,0:T(8,128)(2,1)}, u32[]{:S(2)}, u32[]{:S(2)}) collective-permute-start(bf16[128,512]{1,0:T(8,128)(2,1)} %get-tuple-element.12), channel_id=1, source_target_pairs={{0,2},{1,3},{2,0},{3,1},{4,6},{5,7},{6,4},{7,5},{8,10},{9,11},{10,... | collective-permute-start | bytes 393224 | tf_op jit(solution)/shard_map/ppermute | solution.py:306
  27.0 3.8 %collective-permute-start = (bf16[8,128,256]{2,1,0:T(8,128)(2,1)S(1)}, bf16[8,128,256]{2,1,0:T(8,128)(2,1)S(1)}, u32[]{:S(2)}, u32[]{:S(2)}) collective-permute-start(bf16[8,128,256]{2,1,0:T(8,128)(2,1)S(1)} %all-to-all-done.mine_ref), channel_id=1, source_target_pairs={{0,1},{1,0},{2,3},{3,2},{4,5},{5,4},{6,7},{7,6},{8,9},{9,8},{10,11... | collective-permute-start | bytes 1572872 | tf_op jit(solution)/shard_map/ppermute | solution.py:311
  33.0 13.7 %collective-permute-start.3 = (bf16[144,1024]{1,0:T(8,128)(2,1)S(1)}, bf16[144,1024]{1,0:T(8,128)(2,1)S(1)}, u32[]{:S(2)}, u32[]{:S(2)}) collective-permute-start(bf16[144,1024]{1,0:T(8,128)(2,1)S(1)} %get-tuple-element.13), channel_id=1, source_target_pairs={{0,16},{16,32},{32,48},{48,64},{64,80},{80,96},{96,112},{1,17},{17... | collective-permute-start | bytes 884744 | tf_op jit(solution)/shard_map/ppermute | solution.py:325
  39.1 12.1 %all-to-all-start.1 = ((bf16[16,2,16,128]{3,2,1,0:T(8,128)(2,1)}), bf16[16,2,16,128]{3,2,1,0:T(8,128)(2,1)S(1)}, u32[]{:S(2)}, u32[]{:S(2)}) async-start(bf16[16,2,16,128]{3,2,1,0:T(8,128)(2,1)} %get-tuple-element.17), calls=%async_computation.1 | async-start | bytes 262144 | tf_op jit(solution)/shard_map/all_to_all | solution.py:331
  46.7 3.6 %copy-start.1 = (bf16[128,1024]{1,0:T(8,128)(2,1)S(1)}, bf16[128,1024]{1,0:T(8,128)(2,1)}, u32[]{:S(2)}) copy-start(bf16[128,1024]{1,0:T(8,128)(2,1)} %q_ref.3) | copy-start | bytes 786436
  46.8 6.9 %collective-permute-start.5 = (bf16[128,512]{1,0:T(8,128)(2,1)S(1)}, bf16[128,512]{1,0:T(8,128)(2,1)S(1)}, u32[]{:S(2)}, u32[]{:S(2)}) collective-permute-start(bf16[128,512]{1,0:T(8,128)(2,1)S(1)} %mate_join.1), channel_id=1, source_target_pairs={{0,2},{1,3},{2,0},{3,1},{4,6},{5,7},{6,4},{7,5},{8,10},{9,11},{10,... | collective-permute-start | bytes 393224 | tf_op jit(solution)/shard_map/ppermute | solution.py:338
